TPU v7x, 32 devices: a whole 2x2x4 slice. The times are simulated.
32 devices in a mesh: row: 4 (over y, x), col: 8 (over z, core).
Axes of the slice: x: 2, y: 2, z: 4, core: 2. Of those that a mesh axis runs over, the one named last changes fastest.
Arguments:
- factor: float32 [4096, 4096], P('row', 'col'), may hold values from -1 to 2, as said below
- adjoint: float32 [4096, 4096], P('row', 'col'), may hold values from -6 to 6
Outputs:
- panel_adjoint: float32 [4096, 512], P('row')
Inputs may be any that keep to these rules, and one draw needn't show every extreme that they name: In global order, every diagonal block of factor is lower triangular with diagonal entries from 1 to 2.
All inputs are finite; a program needn't handle non-finite values.
Results may differ from a plain program's by a relative error of at most 0.0003.
Values sent between devices are 32-bit elements; how exact they have to be, the bound alone decides.
No kernel may reach another device: no remote copies, remote signals or barrier semaphores. Data moves between devices by JAX's collectives and lax.ppermute only.
A program may use at most 192 MiB of HBM per device.

v0:
```python
import jax
import jax.numpy as jnp
from jax import lax
from jax.sharding import PartitionSpec as P

NB = 256


HIGHEST_PRECISION = lax.Precision.HIGHEST


def from_root(block, axis, holder):
    block = jnp.where(lax.axis_index(axis) == holder, block, jnp.zeros_like(block))
    return lax.psum(block, axis)


def matmul(left_side, right_side):
    return jnp.dot(
        left_side, right_side, precision=HIGHEST_PRECISION, preferred_element_type=jnp.float32
    )


def tmatmul(left_side, right_side):
    return lax.dot_general(
        left_side,
        right_side,
        (((0,), (0,)), ((), ())),
        precision=HIGHEST_PRECISION,
        preferred_element_type=jnp.float32,
    )


def lower_half(matrix):
    dimension = matrix.shape[0]
    positions = jnp.arange(dimension, dtype=jnp.int32)
    weight = jnp.where(
        positions[:, None] > positions[None, :],
        1.0,
        jnp.where(positions[:, None] == positions[None, :], 0.5, 0.0),
    )
    return matrix * weight.astype(matrix.dtype)


def inverse_lower(factor_block):
    dimension = factor_block.shape[0]
    if dimension == 1:
        return 1.0 / factor_block
    half_size = dimension // 2
    upper_inv = inverse_lower(factor_block[:half_size, :half_size])
    lower_inv = inverse_lower(factor_block[half_size:, half_size:])
    corner = -matmul(lower_inv, matmul(factor_block[half_size:, :half_size], upper_inv))
    zero_part = jnp.zeros((half_size, dimension - half_size), factor_block.dtype)
    top_rows = jnp.concatenate([upper_inv, zero_part], 1)
    bottom_rows = jnp.concatenate([corner, lower_inv], 1)
    return jnp.concatenate([top_rows, bottom_rows], 0)


def diagonal_adjoint(factor_block, block_bar, inverse):
    inner_part = lower_half(tmatmul(factor_block, block_bar))
    symmetric = tmatmul(inverse, matmul(inner_part, inverse))
    return lower_half(symmetric + symmetric.T)


def local(factor, adjoint):
    n_rows_grid = lax.axis_size("row")
    n_cols_grid = lax.axis_size("col")
    row_id = lax.axis_index("row")
    col_id = lax.axis_index("col")
    local_rows, local_cols = factor.shape
    stride = n_cols_grid // n_rows_grid
    blocks_across = local_cols // NB
    row_ids = jnp.arange(local_rows, dtype=jnp.int32)
    col_ids = jnp.arange(local_cols, dtype=jnp.int32)
    global_row = (row_ids // NB * n_rows_grid + row_id) * NB + row_ids % NB
    global_col = (col_ids // NB * n_cols_grid + col_id) * NB + col_ids % NB
    trailing = (global_row >= 2 * NB)[:, None]
    keep = (global_row[:, None] >= global_col[None, :]) & (global_col[None, :] >= 2 * NB)
    masked = jnp.where(keep, adjoint, 0.0)
    owned_bar = adjoint[:, :NB]
    owner_terms = [jnp.where(col_id == panel_index, owned_bar, 0.0) for panel_index in range(2)]
    received = []
    for panel_index in range(2):
        received.append(from_root(factor[:, :NB], "col", panel_index))
    first_panel, second_panel = received
    q_first = jnp.where(trailing, first_panel, 0.0)
    q_second = jnp.where(trailing, second_panel, 0.0)
    results = []
    for panel_index, chosen_rows in ((1, q_second), (0, q_first)):
        pick_panel_width = chosen_rows.shape[1]
        pick_blocked = chosen_rows.reshape(blocks_across, stride, NB, pick_panel_width)
        chosen = lax.dynamic_index_in_dim(pick_blocked, col_id // n_rows_grid, 1, False)
        transposed = from_root(
            chosen.reshape(blocks_across * NB, pick_panel_width), "row", col_id % n_rows_grid
        )
        col_part = lax.psum(tmatmul(masked, chosen_rows), "row")
        row_part = matmul(masked, transposed)
        panel_width = row_part.shape[1]
        selector = (
            (jnp.arange(stride, dtype=jnp.int32) == col_id // n_rows_grid)
            & (row_id == col_id % n_rows_grid)
        ).astype(jnp.float32)
        blocked = row_part.reshape(blocks_across, stride, NB, panel_width)
        blocked = blocked + selector[None, :, None, None] * col_part.reshape(
            blocks_across, 1, NB, panel_width
        )
        product = blocked.reshape(local_rows, panel_width)
        results.append(lax.psum(owner_terms[panel_index] - product, "col"))
    y_second, y_first = results
    f_head, s_head, fb_head, sb_head = (
        lax.all_gather(first_panel[:NB], "row", axis=0, tiled=True),
        lax.all_gather(second_panel[:NB], "row", axis=0, tiled=True),
        lax.all_gather(y_first[:NB], "row", axis=0, tiled=True),
        lax.all_gather(y_second[:NB], "row", axis=0, tiled=True),
    )
    l_second = jnp.tril(s_head[NB : 2 * NB])
    inv_second = inverse_lower(l_second)
    g_second = jnp.where(trailing, matmul(y_second, inv_second), 0.0)
    diag_second, cross_term = lax.psum(
        (tmatmul(g_second, q_second), tmatmul(g_second, q_first)), "row"
    )
    k_second = jnp.tril(sb_head[NB : 2 * NB]) - jnp.tril(diag_second)
    e_second = diagonal_adjoint(l_second, k_second, inv_second)
    l_first = jnp.tril(f_head[:NB])
    inv_first = inverse_lower(l_first)
    link_block = f_head[NB : 2 * NB]
    head_rows = fb_head[NB : 2 * NB] - matmul(e_second + e_second.T, link_block) - cross_term
    second_block = ((global_row >= NB) & (global_row < 2 * NB))[:, None]
    first_block = (global_row < NB)[:, None]
    filler = jnp.zeros((local_rows - NB, NB), jnp.float32)
    padded_head = jnp.concatenate([head_rows, filler], 0)
    residual = jnp.where(
        trailing, y_first - matmul(g_second, link_block), jnp.where(second_block, padded_head, 0.0)
    )
    g_first = matmul(residual, inv_first)
    diag_first = lax.psum(tmatmul(g_first, first_panel), "row")
    k_first = jnp.tril(fb_head[:NB]) - jnp.tril(diag_first)
    e_first = diagonal_adjoint(l_first, k_first, inv_first)
    left_half = jnp.where(first_block, jnp.concatenate([e_first, filler], 0), g_first)
    right_half = jnp.where(second_block, jnp.concatenate([e_second, filler], 0), g_second)
    return jnp.concatenate([left_half, right_half], 1)


def solution(mesh):
    placed = (P("row", "col"), P("row", "col"))
    return jax.shard_map(
        local, mesh=mesh, in_specs=placed, out_specs=P("row", None), check_vma=False
    )
```

profile of v0, /device:TPU:0, one launch (start us, length us, event | category | flops | bytes accessed | tf_op | source)
XLA Modules:
  0.0 1045.5 jit_solution(706475589836079452)
XLA Ops:
  6.5 2.7 slice_select_fusion.1
  9.3 68.0 %all-reduce.271.cloned.1.call-done = (f32[1024,256]{1,0:T(8,128)}, f32[1024,256]{1,0:T(8,128)}) async-done(((f32[1024,256]{1,0:T(8,128)}, f32[1024,256]{1,0:T(8,128)}), (f32[1024,256]{1,0:T(8,128)}, f32[1024,256]{1,0:T(8,128)})) %all-reduce.271.cloned.1.call-update) | async-done | bytes 2097168 | tf_op jit(solution)/shard_map/psum | solution.py:14
  77.3 1.8 slice.6684
  79.3 1.7 slice.6169
  86.8 4.5 fusion.4061
  91.3 4.5 fusion.4062
  96.4 9.1 all-gather.9.cloned.1.call-done
  797.9 3.0 fusion.1
  800.9 3.0 fusion.2
  809.0 60.2 %all-reduce.269.cloned.1.call-done = (f32[1024,256]{1,0:T(8,128)}, f32[1024,256]{1,0:T(8,128)}) async-done(((f32[1024,256]{1,0:T(8,128)}, f32[1024,256]{1,0:T(8,128)}), (f32[1024,256]{1,0:T(8,128)}, f32[1024,256]{1,0:T(8,128)})) %all-reduce.269.cloned.1.call-update) | async-done | bytes 2097168 | tf_op jit(solution)/shard_map/psum | solution.py:107
  869.3 2.4 convolution_select_fusion
  871.8 2.5 fusion.4118
  874.3 2.5 fusion.4119
  877.7 1.7 slice.7199
  886.7 35.7 %all-reduce.273.cloned.1.call-done = (f32[256,256]{1,0:T(8,128)}, f32[256,256]{1,0:T(8,128)}) async-done(((f32[256,256]{1,0:T(8,128)}, f32[256,256]{1,0:T(8,128)}), (f32[256,256]{1,0:T(8,128)}, f32[256,256]{1,0:T(8,128)})) %all-reduce.273.cloned.1.call-update) | async-done | bytes 524304 | tf_op jit(solution)/shard_map/psum | solution.py:118
  922.4 28.6 %all-gather.11.cloned.1.call-done = f32[1024,256]{1,0:T(8,128)} async-done(((f32[256,256]{1,0:T(8,128)}), f32[1024,256]{1,0:T(8,128)}) %all-gather.11.cloned.1.call-update) | async-done | bytes 1048592 | tf_op jit(solution)/shard_map/all_gather | solution.py:113
  951.0 1.6 convolution_multiply_fusion.1
  954.0 25.6 %all-gather.7.cloned.1.call-done = f32[1024,256]{1,0:T(8,128)} async-done(((f32[256,256]{1,0:T(8,128)}), f32[1024,256]{1,0:T(8,128)}) %all-gather.7.cloned.1.call-update) | async-done | bytes 1048592 | tf_op jit(solution)/shard_map/all_gather | solution.py:112
  981.3 2.0 fusion
  983.4 2.1 fusion.4072
  987.1 3.0 fusion.4120
  990.4 42.8 %all-reduce.267.cloned.1.call-done = f32[256,256]{1,0:T(8,128)} async-done(((f32[256,256]{1,0:T(8,128)}), f32[256,256]{1,0:T(8,128)}) %all-reduce.267.cloned.1.call-update) | async-done | bytes 262160 | tf_op jit(solution)/shard_map/psum | solution.py:135
  1033.2 1.6 convolution_multiply_fusion
  1037.2 1.6 pad_maximum_fusion
  (1331 shorter events, 217.0 us)
Async XLA Ops:
  6.5 70.8 %all-reduce.271.cloned.1.call-start = ((), (), s32[]{:S(2)}) async-start(), calls=%async_computation.6 | async-start | bytes 4194304 | tf_op jit(solution)/shard_map/psum | solution.py:14
  9.3 96.3 %all-gather.9.cloned.1.call-start = ((), (), s32[]{:S(2)}) async-start(), calls=%async_computation.2 | async-start | bytes 1310720 | tf_op jit(solution)/shard_map/all_gather | solution.py:111
  79.1 328.8 %all-gather.5.cloned.1.call-start = ((), (), s32[]{:S(2)}) async-start(), calls=%async_computation | async-start | bytes 1310720 | tf_op jit(solution)/shard_map/all_gather | solution.py:110
  81.0 715.3 %all-reduce.275.cloned.1.call-start = ((), (), s32[]{:S(2)}) async-start(), calls=%async_computation.8 | async-start | bytes 4194304 | tf_op jit(solution)/shard_map/psum | solution.py:95
  95.8 773.4 %all-reduce.269.cloned.1.call-start = ((), (), s32[]{:S(2)}) async-start(), calls=%async_computation.5 | async-start | bytes 4194304 | tf_op jit(solution)/shard_map/psum | solution.py:107
  155.9 530.6 %copy-start.75 = (f32[2,4]{1,0:T(2,128)}, f32[2,4]{1,0:T(2,128)S(1)}, u32[]{:S(2)}) copy-start(f32[2,4]{1,0:T(2,128)S(1)} %concatenate.5542) | copy-start | bytes 100
  408.8 385.2 %copy-start.5 = (f32[256,256]{1,0:T(8,128)}, f32[256,256]{1,0:T(8,128)S(1)}, u32[]{:S(2)}) copy-start(f32[256,256]{1,0:T(8,128)S(1)} %slice_select_fusion.5) | copy-start | bytes 786436
  415.3 261.1 %copy-start.177 = (f32[2,2]{1,0:T(2,128)S(1)}, f32[2,2]{1,0:T(2,128)}, u32[]{:S(2)}) copy-start(f32[2,2]{1,0:T(2,128)} %fusion.3670) | copy-start | bytes 52
  416.1 260.5 %copy-start.130 = (f32[2,4]{1,0:T(2,128)S(1)}, f32[2,4]{1,0:T(2,128)}, u32[]{:S(2)}) copy-start(f32[2,4]{1,0:T(2,128)} %concatenate.5380) | copy-start | bytes 100
  420.9 258.1 %copy-start.176 = (f32[2,2]{1,0:T(2,128)S(1)}, f32[2,2]{1,0:T(2,128)}, u32[]{:S(2)}) copy-start(f32[2,2]{1,0:T(2,128)} %fusion.3666) | copy-start | bytes 52
  422.2 257.1 %copy-start.149 = (f32[4,4]{1,0:T(4,128)S(1)}, f32[4,4]{1,0:T(4,128)}, u32[]{:S(2)}) copy-start(f32[4,4]{1,0:T(4,128)} %fusion.2196) | copy-start | bytes 196
  426.4 255.4 %copy-start.178 = (f32[2,2]{1,0:T(2,128)S(1)}, f32[2,2]{1,0:T(2,128)}, u32[]{:S(2)}) copy-start(f32[2,2]{1,0:T(2,128)} %fusion.3658) | copy-start | bytes 52
  427.7 254.4 %copy-start.150 = (f32[4,4]{1,0:T(4,128)S(1)}, f32[4,4]{1,0:T(4,128)}, u32[]{:S(2)}) copy-start(f32[4,4]{1,0:T(4,128)} %fusion.2192) | copy-start | bytes 196
  442.0 243.9 %copy-start.151 = (f32[4,4]{1,0:T(4,128)S(1)}, f32[4,4]{1,0:T(4,128)}, u32[]{:S(2)}) copy-start(f32[4,4]{1,0:T(4,128)} %fusion.2184) | copy-start | bytes 196
  445.2 241.2 %copy-start.96 = (f32[16,16]{1,0:T(8,128)S(1)}, f32[16,16]{1,0:T(8,128)}, u32[]{:S(2)}) copy-start(f32[16,16]{1,0:T(8,128)} %fusion.816) | copy-start | bytes 3076
  462.1 230.5 %copy-start.81 = (f32[2,4]{1,0:T(2,128)S(1)}, f32[2,4]{1,0:T(2,128)}, u32[]{:S(2)}) copy-start(f32[2,4]{1,0:T(2,128)} %concatenate.5592) | copy-start | bytes 100
  462.1 230.5 %copy-start.154 = (f32[4,4]{1,0:T(4,128)S(1)}, f32[4,4]{1,0:T(4,128)}, u32[]{:S(2)}) copy-start(f32[4,4]{1,0:T(4,128)} %fusion.2180) | copy-start | bytes 196
  492.5 295.7 %copy-start.77 = (f32[2,4]{1,0:T(2,128)}, f32[2,4]{1,0:T(2,128)S(1)}, u32[]{:S(2)}) copy-start(f32[2,4]{1,0:T(2,128)S(1)} %concatenate.4967) | copy-start | bytes 100
  502.3 286.0 %copy-start.44 = (f32[4,8]{1,0:T(4,128)}, f32[4,8]{1,0:T(4,128)S(1)}, u32[]{:S(2)}) copy-start(f32[4,8]{1,0:T(4,128)S(1)} %concatenate.4963) | copy-start | bytes 388
  521.8 266.5 %copy-start.54 = (f32[8,16]{1,0:T(8,128)}, f32[8,16]{1,0:T(8,128)S(1)}, u32[]{:S(2)}) copy-start(f32[8,16]{1,0:T(8,128)S(1)} %concatenate.4953) | copy-start | bytes 1540
  804.2 118.2 %all-reduce.273.cloned.1.call-start = ((), (), s32[]{:S(2)}) async-start(), calls=%async_computation.7 | async-start | bytes 1048576 | tf_op jit(solution)/shard_map/psum | solution.py:118
  877.0 74.0 %all-gather.11.cloned.1.call-start = ((), (), s32[]{:S(2)}) async-start(), calls=%async_computation.3 | async-start | bytes 1310720 | tf_op jit(solution)/shard_map/all_gather | solution.py:113
  879.5 100.2 %all-gather.7.cloned.1.call-start = ((), (), s32[]{:S(2)}) async-start(), calls=%async_computation.1 | async-start | bytes 1310720 | tf_op jit(solution)/shard_map/all_gather | solution.py:112
  884.8 148.4 %all-reduce.267.cloned.1.call-start = ((), (), s32[]{:S(2)}) async-start(), calls=%async_computation.4 | async-start | bytes 524288 | tf_op jit(solution)/shard_map/psum | solution.py:135
  (185 other events, 9496.8 us)
Sparse Core Ops, SparseCore 0:
  9.8 67.4 all-reduce.270
  79.2 26.2 all-gather.8
  107.4 26.6 all-gather.4
  137.1 70.2 all-reduce.274
  804.3 64.9 all-reduce.268
  877.1 45.1 all-reduce.272
  924.3 26.6 all-gather.10
  953.0 26.6 all-gather.6
  990.2 42.9 all-reduce.266
where the time goes:
time: 1060 us; the launch traced here: 1050 us
  between operations  516 us (49%)
  waiting for transfers between devices  270 us (25%)
  matrix products  172 us (16%)
  local copies, waits for them, and re-layouts  55.7 us (5%)
  other arithmetic  30.1 us (3%)
    dot_general x516, matrix products, matmul(): jnp.dot(left_side, right_side, precision=HIGHEST_PRECISION, preferred_ele...  151 us
    psum x1, waiting for transfers between devices, from_root(): return lax.psum(block, axis)  68 us
    psum x1, waiting for transfers between devices, local(): results.append(lax.psum(owner_terms[panel_index] - product, 'col'))  60.2 us
    psum x1, waiting for transfers between devices, local(): diag_first = lax.psum(tmatmul(g_first, first_panel), 'row')  42.8 us
    psum x1, waiting for transfers between devices, local(): lax.psum((tmatmul(g_second, q_second), tmatmul(g_second, q_first)), 'row')  35.7 us
    all_gather x1, waiting for transfers between devices, local(): lax.all_gather(y_second[:NB], 'row', axis=0, tiled=True)  28.6 us
    all_gather x1, waiting for transfers between devices, local(): lax.all_gather(y_first[:NB], 'row', axis=0, tiled=True)  25.6 us
    slice x30, local copies, waits for them, and re-layouts, inverse_lower(): upper_inv = inverse_lower(factor_block[:half_size, :half_size])  21.9 us
  transfers between devices with their start and end apart: 9, of which 7 were waited for; matrix products, arithmetic and copies ran while one was open for 21% of the time, Pallas kernels for 0%

commit v1 on v0

v1 whole, which is shorter than its diff:
```python
import jax
import jax.numpy as jnp
from jax import lax
from jax.experimental import pallas as pl
from jax.experimental.pallas import tpu as pltpu
from jax.sharding import PartitionSpec as P

NB = 256
HIGH = lax.Precision.HIGH
HIGHEST = lax.Precision.HIGHEST


def matmul(left, right):
    return jnp.dot(left, right, precision=HIGH, preferred_element_type=jnp.float32)


def tmatmul(left, right):
    return lax.dot_general(
        left, right, (((0,), (0,)), ((), ())), precision=HIGH, preferred_element_type=jnp.float32
    )


def dot(left, right):
    return jnp.dot(left, right, precision=HIGHEST, preferred_element_type=jnp.float32)


def tdot(left, right):
    return dot(left.T, right)


def positions():
    rows = lax.broadcasted_iota(jnp.int32, (NB, NB), 0)
    cols = lax.broadcasted_iota(jnp.int32, (NB, NB), 1)
    return rows, cols


def inverse_kernel(block_ref, out_ref):
    rows, cols = positions()
    block = block_ref[...]
    diagonal = rows == cols
    inverse = jnp.where(diagonal, 1.0 / jnp.where(diagonal, block, 1.0), 0.0)
    size = 1
    while size < NB:
        corner = (
            (rows // (2 * size) == cols // (2 * size))
            & (rows // size % 2 == 1)
            & (cols // size % 2 == 0)
        )
        inverse = inverse - dot(inverse, dot(jnp.where(corner, block, 0.0), inverse))
        size *= 2
    out_ref[...] = inverse


def inverse_lower(block):
    return pl.pallas_call(
        inverse_kernel,
        out_shape=jax.ShapeDtypeStruct((NB, NB), jnp.float32),
        name="inverse_lower",
        cost_estimate=pl.CostEstimate(
            flops=16 * 12 * NB**3, bytes_accessed=8 * NB * NB, transcendentals=0
        ),
    )(block)


def head_kernel(l0, l1, c, v0, v1, a00, a10, a11, z00, z10, z11, e0_ref, g0_ref, e1_ref):
    rows, cols = positions()

    def tril(x):
        return jnp.where(rows >= cols, x, 0.0)

    def phi(x):
        return jnp.where(rows > cols, x, jnp.where(rows == cols, 0.5 * x, 0.0))

    def diagonal_adjoint(block, block_bar, inverse_t, inverse):
        inner = phi(tdot(block, block_bar))
        s = dot(inverse_t, dot(inner, inverse))
        return phi(s + s.T)

    link = c[...]
    inv1, inv0 = v1[...], v0[...]
    inv1_t, inv0_t = inv1.T, inv0.T
    cross = dot(inv1_t, z10[...])
    k1 = tril(a11[...] - dot(inv1_t, z11[...]))
    e1 = diagonal_adjoint(tril(l1[...]), k1, inv1_t, inv1)
    rest = a10[...] - dot(e1 + e1.T, link) - cross
    g0_ref[...] = dot(rest, inv0)
    total = dot(inv0_t, z00[...] - tdot(link, cross) + tdot(rest, link))
    k0 = tril(a00[...] - total)
    e0_ref[...] = diagonal_adjoint(tril(l0[...]), k0, inv0_t, inv0)
    e1_ref[...] = e1


def head_blocks(*blocks):
    shape = jax.ShapeDtypeStruct((NB, NB), jnp.float32)
    return pl.pallas_call(
        head_kernel,
        out_shape=(shape, shape, shape),
        name="head_blocks",
        cost_estimate=pl.CostEstimate(
            flops=13 * 12 * NB**3, bytes_accessed=56 * NB * NB, transcendentals=0
        ),
    )(*blocks)


def local(factor, adjoint):
    n_rows = lax.axis_size("row")
    n_cols = lax.axis_size("col")
    n_pairs = n_cols // 2
    row_id = lax.axis_index("row")
    col_id = lax.axis_index("col")
    pair = col_id // 2
    lane = col_id % 2
    x_id = row_id % 2
    near = row_id // 2 == pair % 2
    local_rows, local_cols = factor.shape
    own_rows = local_rows // n_pairs

    def send(value, targets):
        edges = []
        for r in range(n_rows):
            for c in range(n_cols):
                target = targets(r, c // 2, c % 2)
                if target is not None:
                    edges.append((r * n_cols + c, target[0] * n_cols + target[1] * 2 + target[2]))
        return lax.ppermute(value, ("row", "col"), edges)

    def swap(value):
        return send(value, lambda r, p, k: (r, p, 1 - k))

    def rows_of(value, index, size):
        return lax.dynamic_slice_in_dim(value, index * size, size, 0)

    other = swap(adjoint)
    is_first = lane == 0
    whole = jnp.concatenate(
        [jnp.where(is_first, adjoint, other), jnp.where(is_first, other, adjoint)], 1
    )
    row_ids = jnp.arange(local_rows, dtype=jnp.int32)
    global_row = (row_ids // NB * n_rows + row_id) * NB + row_ids % NB
    col_ids = jnp.arange(local_cols, dtype=jnp.int32)
    global_col = (col_ids // NB * n_cols + 2 * pair) * NB + col_ids % NB
    global_col = jnp.concatenate([global_col, global_col + NB])
    trailing = (global_row >= 2 * NB)[:, None]
    masked = jnp.where(trailing & (global_row[:, None] >= global_col[None, :]), whole, 0.0)

    piece_rows = local_rows // 4
    panel = jnp.where(pair == 0, factor[:, :NB], 0.0)
    pieces = []
    for index in (3, 2, 1, 0):
        moving = factor[index * piece_rows : (index + 1) * piece_rows, :NB]
        arrived = panel[index * piece_rows : (index + 1) * piece_rows]
        for hop in range(1, n_pairs):
            moving = send(
                moving, lambda r, p, k, hop=hop: (r, hop, k) if p == hop - 1 else None
            )
            arrived = arrived + moving
        pieces.append(arrived)
    pieces = pieces[::-1]
    head = pieces[0][:NB]
    low = jnp.concatenate(pieces[:2], 0)
    low = jnp.where(trailing[: local_rows // 2], low, 0.0)
    high = jnp.concatenate(pieces[2:], 0)
    chosen_rows = jnp.concatenate([low, high], 0)

    def spread(value):
        def at(d):
            return send(
                value, lambda r, p, k: (r ^ d, p, k) if r // 2 == p % 2 else None
            )

        same = jnp.where(near, value, 0.0) + at(2)
        across = at(1) + at(3)
        return jnp.where(x_id == 0, same, across), jnp.where(x_id == 0, across, same)

    high_0, high_1 = spread(rows_of(high, pair // 2, NB))
    low_0, low_1 = spread(rows_of(low, pair // 2, NB))
    chosen_cols = jnp.concatenate([low_0, high_0, low_1, high_1], 0)

    def from_head(d):
        return send(head, lambda r, p, k: (r ^ d, p, k) if r < 2 else None)

    head_1, head_2, head_3 = from_head(1), from_head(2), from_head(3)

    def by_row(*values):
        result = values[3]
        for index in (2, 1, 0):
            result = jnp.where(row_id == index, values[index], result)
        return result

    top = by_row(head, head_1, head_2, head_3)
    link = by_row(head_1, head, head_3, head_2)
    inverse = inverse_lower(jnp.where(is_first, top, link))

    row_part = matmul(masked, chosen_cols)
    col_part = tmatmul(masked, chosen_rows)

    chosen_other = swap(chosen_rows)
    own_product = tmatmul(row_part, chosen_rows)
    other_product = tmatmul(row_part, chosen_other)
    first_pair = pair == 0
    own_term = jnp.where(is_first, col_part[:NB], col_part[2 * NB : 3 * NB])
    own_sum = jnp.where(first_pair, own_term, 0.0) - own_product - own_product.T
    other_sum = jnp.where(
        is_first,
        jnp.where(first_pair, col_part[2 * NB : 3 * NB], 0.0) - other_product.T,
        -other_product,
    )
    sums = jnp.concatenate([own_sum, other_sum], 0)
    slice_rows = 2 * NB // n_rows
    part = rows_of(sums, row_id, slice_rows)
    for d in range(1, n_rows):
        part = part + send(
            rows_of(sums, row_id ^ d, slice_rows), lambda r, p, k, d=d: (r ^ d, p, k)
        )
    total = part
    for source in range(1, n_pairs):
        total = total + send(
            part, lambda r, p, k, source=source: (r, 0, k) if p == source else None
        )
    gathered = [total] + [
        send(total, lambda r, p, k, d=d: (r ^ d, 0, k) if p == 0 and r ^ d < 2 else None)
        for d in range(1, n_rows)
    ]
    in_first_row = row_id == 0
    sums = jnp.where(
        in_first_row,
        jnp.concatenate(gathered, 0),
        jnp.concatenate([gathered[1], gathered[0], gathered[3], gathered[2]], 0),
    )

    remaining = jnp.where(first_pair, adjoint[:, :NB], 0.0) - row_part
    mine = rows_of(remaining, pair, own_rows)
    for d in range(1, n_pairs):
        mine = mine + send(
            rows_of(remaining, pair ^ d, own_rows), lambda r, p, k, d=d: (r, p ^ d, k)
        )
    half_rows = 2 * NB
    col_same = rows_of(col_part, x_id, half_rows)
    col_across = rows_of(col_part, 1 - x_id, half_rows)
    col_sum = (
        col_same
        + send(col_across, lambda r, p, k: (r ^ 1, p, k) if r // 2 == p % 2 else None)
        + send(col_same, lambda r, p, k: (r ^ 2, p, k) if r // 2 != p % 2 else None)
        + send(col_across, lambda r, p, k: (r ^ 3, p, k) if r // 2 != p % 2 else None)
    )
    for index in range(2):
        mine = mine - send(
            col_sum[index * NB : (index + 1) * NB],
            lambda r, p, k, index=index: (
                (r, p // 2 + index * (n_pairs // 2), k) if r // 2 == p % 2 else None
            ),
        )
    solved = matmul(mine, inverse)
    second = send(solved, lambda r, p, k: (r, p, 0) if k == 1 else None)
    solved = matmul(mine - matmul(second, link), inverse)

    bar = adjoint[:NB, :NB]
    bar_across = send(bar, lambda r, p, k: (r ^ 1, 0, k) if p == 0 and r < 2 else None)
    bar_top = jnp.where(in_first_row, bar, bar_across)
    bar_link = jnp.where(in_first_row, bar_across, bar)
    mine_head = jnp.concatenate([top, link, inverse, bar_top, bar_link], 0)
    their_head = swap(mine_head)
    their_sums = swap(sums)
    firsts = jnp.where(is_first, mine_head, their_head)
    seconds = jnp.where(is_first, their_head, mine_head)
    first_sums = jnp.where(is_first, sums, their_sums)
    second_sums = jnp.where(is_first, their_sums, sums)
    e_first, g_head, e_second = head_blocks(
        firsts[:NB],
        seconds[NB : 2 * NB],
        firsts[NB : 2 * NB],
        firsts[2 * NB : 3 * NB],
        seconds[2 * NB : 3 * NB],
        firsts[3 * NB : 4 * NB],
        firsts[4 * NB :],
        seconds[4 * NB :],
        first_sums[:NB],
        first_sums[NB:] + second_sums[NB:],
        second_sums[:NB],
    )
    leading = jnp.where(
        in_first_row,
        jnp.where(is_first, e_first, 0.0),
        jnp.where(is_first, g_head, e_second),
    )
    solved = jnp.where(first_pair & (row_id < 2), leading, solved)

    column = jnp.zeros((local_rows, NB), jnp.float32)
    column = lax.dynamic_update_slice_in_dim(column, solved, pair * own_rows, 0)
    for d in range(1, n_pairs):
        piece = send(solved, lambda r, p, k, d=d: (r, p ^ d, k))
        column = lax.dynamic_update_slice_in_dim(column, piece, (pair ^ d) * own_rows, 0)
    column_other = swap(column)
    return jnp.concatenate(
        [jnp.where(is_first, column, column_other), jnp.where(is_first, column_other, column)], 1
    )


def solution(mesh):
    placed = (P("row", "col"), P("row", "col"))
    return jax.shard_map(
        local, mesh=mesh, in_specs=placed, out_specs=P("row", None), check_vma=False
    )
```

time: 1060 us -> 251 us (0.24)
  the two profiles are of different devices: /device:TPU:0 before, /device:TPU:11 now
where the time goes in v1:
time: 251 us; the launch traced here: 250 us
  starting transfers between devices  125 us (50%)
  waiting for transfers between devices  67.7 us (27%)
  Pallas kernels  18.6 us (7%)
  other arithmetic  17.6 us (7%)
  matrix products  10.8 us (4%)
  local copies, waits for them, and re-layouts  9.2 us (4%)
    ppermute x48, starting transfers between devices, send(): return lax.ppermute(value, ('row', 'col'), edges)  125 us
    ppermute x48, waiting for transfers between devices, send(): return lax.ppermute(value, ('row', 'col'), edges)  67.7 us
    pallas_call x1, Pallas kernels, inverse_lower(): pl.pallas_call(inverse_kernel, out_shape=jax.ShapeDtypeStruct((NB, NB), j...  10.2 us
    pallas_call x1, Pallas kernels, head_blocks(): pl.pallas_call(head_kernel, out_shape=(shape, shape, shape), name='head_b...  8.4 us
    dot_general x3, matrix products, tmatmul(): lax.dot_general(left, right, (((0,), (0,)), ((), ())), precision=HIGH, pr...  6.73 us
  transfers between devices with their start and end apart: 48, of which 15 were waited for; matrix products, arithmetic and copies ran while one was open for 12% of the time, Pallas kernels for 7%

profile of v1, /device:TPU:11, one launch (start us, length us, event | category | flops | bytes accessed | tf_op | source)
XLA Modules:
  0.0 250.0 jit_solution(8703370897265272331)
XLA Ops:
  7.4 5.5 %collective-permute-start.8 = (f32[1024,512]{1,0:T(8,128)S(1)}, f32[1024,512]{1,0:T(8,128)}, u32[]{:S(2)}, u32[]{:S(2)}) collective-permute-start(f32[1024,512]{1,0:T(8,128)S(1)} %copy-done), channel_id=1, source_target_pairs={{0,1},{1,0},{2,3},{3,2},{4,5},{5,4},{6,7},{7,6},{8,9},{9,8},{10,11... | collective-permute-start | bytes 6291464 | tf_op jit(solution)/shard_map/ppermute | solution.py:125
  12.9 3.1 %collective-permute-start.10 = (f32[256,256]{1,0:T(8,128)S(1)}, f32[256,256]{1,0:T(8,128)S(1)}, u32[]{:S(2)}, u32[]{:S(2)}) collective-permute-start(f32[256,256]{1,0:T(8,128)S(1)} %collective-permute-done.9), channel_id=1, source_target_pairs={{2,4},{3,5},{10,12},{11,13},{18,20},{19,21},{26,28},{27,29}} | collective-permute-start | bytes 786440 | tf_op jit(solution)/shard_map/ppermute | solution.py:125
  18.9 3.6 %collective-permute-done.15 = f32[256,256]{1,0:T(8,128)S(1)} collective-permute-done((f32[256,256]{1,0:T(8,128)}, f32[256,256]{1,0:T(8,128)S(1)}, u32[]{:S(2)}, u32[]{:S(2)}) %collective-permute-start.15) | collective-permute-done | bytes 262176 | tf_op jit(solution)/shard_map/ppermute | solution.py:125
  24.5 3.6 %collective-permute-done = f32[256,256]{1,0:T(8,128)S(1)} collective-permute-done((f32[256,256]{1,0:T(8,128)}, f32[256,256]{1,0:T(8,128)S(1)}, u32[]{:S(2)}, u32[]{:S(2)}) %collective-permute-start) | collective-permute-done | bytes 262176 | tf_op jit(solution)/shard_map/ppermute | solution.py:125
  33.2 4.9 %collective-permute-done.1 = f32[256,256]{1,0:T(8,128)} collective-permute-done((f32[256,256]{1,0:T(8,128)S(1)}, f32[256,256]{1,0:T(8,128)}, u32[]{:S(2)}, u32[]{:S(2)}) %collective-permute-start.1) | collective-permute-done | bytes 262176 | tf_op jit(solution)/shard_map/ppermute | solution.py:125
  58.7 10.2 %inverse_lower.1 = f32[256,256]{1,0:T(8,128)} custom-call(f32[256,256]{1,0:T(8,128)} %broadcast_select_fusion.12.block_ref), custom_call_target="tpu_custom_call" | custom-call | flops 3221225472 | bytes 524288 | tf_op jit(solution)/shard_map/inverse_lower/pallas_call | solution.py:55
  76.4 21.3 %collective-permute-start.24 = (f32[1024,256]{1,0:T(8,128)S(1)}, f32[1024,256]{1,0:T(8,128)S(1)}, u32[]{:S(2)}, u32[]{:S(2)}) collective-permute-start(f32[1024,256]{1,0:T(8,128)S(1)} %copy-done.6), channel_id=1, source_target_pairs={{0,1},{1,0},{2,3},{3,2},{4,5},{5,4},{6,7},{7,6},{8,9},{9,8},{10,11... | collective-permute-start | bytes 3145736 | tf_op jit(solution)/shard_map/ppermute | solution.py:125
  101.6 4.7 %fusion.1 = f32[1024,256]{1,0:T(8,128)} fusion(f32[1024,512]{1,0:T(8,128)S(1)} %get-tuple-element.16, f32[1024,512]{1,0:T(8,128)S(1)} %get-tuple-element.15, s32[1024]{0:T(1024)S(1)} %get-tuple-element.63, s32[1024]{0:T(1024)S(1)} %get-tuple-element.62, pred[1024]{0:T(1024)(128)(4,1)S(1)} %broadcast_compare_fusion, f32[256,256]{1,0:T(8,128)S(1)} %get-tuple-element.47, ...), kind=kOutput, calls=%fused_computation.2 | convolution fusion | flops 1615331328 | bytes 6300672 | tf_op jit(solution)/shard_map/dot_general | solution.py:18
  106.4 3.3 %select_subtract_fusion = (f32[1024,256]{1,0:T(8,128)}, f32[1024,256]{1,0:T(8,128)S(1)}) fusion(f32[1024,512]{1,0:T(8,128)S(1)} %copy-done, pred[]{:T(512)S(6)} %eq.38, f32[256,256]{1,0:T(8,128)S(1)} %get-tuple-element.43, f32[256,256]{1,0:T(8,128)S(1)} %get-tuple-element.41, f32[256,256]{1,0:T(8,128)S(1)} %get-tuple-element.42, ...), kind=kOutput, calls=%fused_computation.22 | convolution fusion | flops 1616117760 | bytes 8397825 | tf_op jit(solution)/shard_map/dot_general | solution.py:14
  112.2 5.6 %collective-permute-start.25 = (f32[128,256]{1,0:T(8,128)S(1)}, f32[128,256]{1,0:T(8,128)S(1)}, u32[]{:S(2)}, u32[]{:S(2)}) collective-permute-start(f32[128,256]{1,0:T(8,128)S(1)} %get-tuple-element.53), channel_id=1, source_target_pairs={{0,8},{1,9},{2,10},{3,11},{4,12},{5,13},{6,14},{7,15},{8,0},{9,1},... | collective-permute-start | bytes 393224 | tf_op jit(solution)/shard_map/ppermute | solution.py:125
  117.8 5.7 %collective-permute-start.26 = (f32[128,256]{1,0:T(8,128)S(1)}, f32[128,256]{1,0:T(8,128)S(1)}, u32[]{:S(2)}, u32[]{:S(2)}) collective-permute-start(f32[128,256]{1,0:T(8,128)S(1)} %get-tuple-element.54), channel_id=1, source_target_pairs={{0,16},{1,17},{2,18},{3,19},{4,20},{5,21},{6,22},{7,23},{8,24},{9,... | collective-permute-start | bytes 393224 | tf_op jit(solution)/shard_map/ppermute | solution.py:125
  123.5 5.7 %collective-permute-start.27 = (f32[128,256]{1,0:T(8,128)S(1)}, f32[128,256]{1,0:T(8,128)}, u32[]{:S(2)}, u32[]{:S(2)}) collective-permute-start(f32[128,256]{1,0:T(8,128)S(1)} %get-tuple-element.55), channel_id=1, source_target_pairs={{0,24},{1,25},{2,26},{3,27},{4,28},{5,29},{6,30},{7,31},{8,16},{9,... | collective-permute-start | bytes 393224 | tf_op jit(solution)/shard_map/ppermute | solution.py:125
  129.3 4.9 %collective-permute-done.27 = f32[128,256]{1,0:T(8,128)} collective-permute-done((f32[128,256]{1,0:T(8,128)S(1)}, f32[128,256]{1,0:T(8,128)}, u32[]{:S(2)}, u32[]{:S(2)}) %collective-permute-start.27) | collective-permute-done | bytes 131104 | tf_op jit(solution)/shard_map/ppermute | solution.py:125
  135.1 2.3 collective-permute-start.28
  139.6 4.6 %collective-permute-start.40 = (f32[512,256]{1,0:T(8,128)S(1)}, f32[512,256]{1,0:T(8,128)S(1)}, u32[]{:S(2)}, u32[]{:S(2)}) collective-permute-start(f32[512,256]{1,0:T(8,128)S(1)} %get-tuple-element.45), channel_id=1, source_target_pairs={{2,26},{3,27},{6,30},{7,31},{10,18},{11,19},{14,22},{15,23},{16,8}... | collective-permute-start | bytes 1572872 | tf_op jit(solution)/shard_map/ppermute | solution.py:125
  149.2 25.6 %collective-permute-start.35 = (f32[256,256]{1,0:T(8,128)S(1)}, f32[256,256]{1,0:T(8,128)S(1)}, u32[]{:S(2)}, u32[]{:S(2)}) collective-permute-start(f32[256,256]{1,0:T(8,128)S(1)} %get-tuple-element.37), channel_id=1, source_target_pairs={{0,2},{1,3},{2,0},{3,1},{4,6},{5,7},{6,4},{7,5},{8,10},{9,11},{10,... | collective-permute-start | bytes 786440 | tf_op jit(solution)/shard_map/ppermute | solution.py:125
  183.4 17.9 %collective-permute-done.37 = f32[256,256]{1,0:T(8,128)S(1)} collective-permute-done((f32[256,256]{1,0:T(8,128)S(1)}, f32[256,256]{1,0:T(8,128)S(1)}, u32[]{:S(2)}, u32[]{:S(2)}) %collective-permute-start.37) | collective-permute-done | bytes 262176 | tf_op jit(solution)/shard_map/ppermute | solution.py:125
  201.3 2.9 %collective-permute-done.41 = f32[256,256]{1,0:T(8,128)S(1)} collective-permute-done((f32[256,256]{1,0:T(8,128)S(1)}, f32[256,256]{1,0:T(8,128)S(1)}, u32[]{:S(2)}, u32[]{:S(2)}) %collective-permute-start.41) | collective-permute-done | bytes 262176 | tf_op jit(solution)/shard_map/ppermute | solution.py:125
  204.6 3.6 %collective-permute-start.43 = (f32[256,256]{1,0:T(8,128)S(1)}, f32[256,256]{1,0:T(8,128)S(1)}, u32[]{:S(2)}, u32[]{:S(2)}) collective-permute-start(f32[256,256]{1,0:T(8,128)S(1)} %fusion.70), channel_id=1, source_target_pairs={{1,0},{3,2},{5,4},{7,6},{9,8},{11,10},{13,12},{15,14},{17,16},{19,... | collective-permute-start | bytes 786440 | tf_op jit(solution)/shard_map/ppermute | solution.py:125
  209.2 8.4 %head_blocks.1 = (f32[256,256]{1,0:T(8,128)}, f32[256,256]{1,0:T(8,128)}, f32[256,256]{1,0:T(8,128)}) custom-call(f32[256,256]{1,0:T(8,128)} %get-tuple-element.64.l0, f32[256,256]{1,0:T(8,128)} %get-tuple-element.27.l1, f32[256,256]{1,0:T(8,128)} %get-tuple-element.65.c, f32[256,256]{1,0:T(8,128)} %get-tuple-element.66.v0, ...), custom_call_target="tpu_custom_call" | custom-call | flops 2617245696 | bytes 3670016 | tf_op jit(solution)/shard_map/head_blocks/pallas_call | solution.py:95
  221.7 7.4 %collective-permute-done.44 = f32[256,256]{1,0:T(8,128)S(1)} collective-permute-done((f32[256,256]{1,0:T(8,128)S(1)}, f32[256,256]{1,0:T(8,128)S(1)}, u32[]{:S(2)}, u32[]{:S(2)}) %collective-permute-start.44) | collective-permute-done | bytes 262176 | tf_op jit(solution)/shard_map/ppermute | solution.py:125
  229.1 3.7 %collective-permute-done.45 = f32[256,256]{1,0:T(8,128)S(1)} collective-permute-done((f32[256,256]{1,0:T(8,128)S(1)}, f32[256,256]{1,0:T(8,128)S(1)}, u32[]{:S(2)}, u32[]{:S(2)}) %collective-permute-start.45) | collective-permute-done | bytes 262176 | tf_op jit(solution)/shard_map/ppermute | solution.py:125
  232.8 12.5 %collective-permute-done.46 = f32[256,256]{1,0:T(8,128)S(1)} collective-permute-done((f32[256,256]{1,0:T(8,128)S(1)}, f32[256,256]{1,0:T(8,128)S(1)}, u32[]{:S(2)}, u32[]{:S(2)}) %collective-permute-start.46) | collective-permute-done | bytes 262176 | tf_op jit(solution)/shard_map/ppermute | solution.py:125
  246.0 2.3 collective-permute-done.47
  (151 shorter events, 75.9 us)
Async XLA Ops:
  4.8 17.7 %collective-permute-start.15 = (f32[256,256]{1,0:T(8,128)}, f32[256,256]{1,0:T(8,128)S(1)}, u32[]{:S(2)}, u32[]{:S(2)}) collective-permute-start(f32[256,256]{1,0:T(8,128)} %get-tuple-element.23), channel_id=1, source_target_pairs={{0,2},{1,3},{8,10},{9,11},{16,18},{17,19},{24,26},{25,27}} | collective-permute-start | bytes 786440 | tf_op jit(solution)/shard_map/ppermute | solution.py:125
  6.1 22.0 %collective-permute-start = (f32[256,256]{1,0:T(8,128)}, f32[256,256]{1,0:T(8,128)S(1)}, u32[]{:S(2)}, u32[]{:S(2)}) collective-permute-start(f32[256,256]{1,0:T(8,128)} %get-tuple-element.21), channel_id=1, source_target_pairs={{0,2},{1,3},{8,10},{9,11},{16,18},{17,19},{24,26},{25,27}} | collective-permute-start | bytes 786440 | tf_op jit(solution)/shard_map/ppermute | solution.py:125
  7.4 92.0 %collective-permute-start.8 = (f32[1024,512]{1,0:T(8,128)S(1)}, f32[1024,512]{1,0:T(8,128)}, u32[]{:S(2)}, u32[]{:S(2)}) collective-permute-start(f32[1024,512]{1,0:T(8,128)S(1)} %copy-done), channel_id=1, source_target_pairs={{0,1},{1,0},{2,3},{3,2},{4,5},{5,4},{6,7},{7,6},{8,9},{9,8},{10,11... | collective-permute-start | bytes 6291464 | tf_op jit(solution)/shard_map/ppermute | solution.py:125
  12.9 18.0 %collective-permute-start.10 = (f32[256,256]{1,0:T(8,128)S(1)}, f32[256,256]{1,0:T(8,128)S(1)}, u32[]{:S(2)}, u32[]{:S(2)}) collective-permute-start(f32[256,256]{1,0:T(8,128)S(1)} %collective-permute-done.9), channel_id=1, source_target_pairs={{2,4},{3,5},{10,12},{11,13},{18,20},{19,21},{26,28},{27,29}} | collective-permute-start | bytes 786440 | tf_op jit(solution)/shard_map/ppermute | solution.py:125
  40.2 30.5 %collective-permute-start.6 = (f32[256,256]{1,0:T(8,128)}, f32[256,256]{1,0:T(8,128)}, u32[]{:S(2)}, u32[]{:S(2)}) collective-permute-start(f32[256,256]{1,0:T(8,128)} %slice.89), channel_id=1, source_target_pairs={{0,8},{1,9},{8,0},{9,1}} | collective-permute-start | bytes 786440 | tf_op jit(solution)/shard_map/ppermute | solution.py:125
  51.7 21.9 %collective-permute-start.18 = (f32[256,256]{1,0:T(8,128)}, f32[256,256]{1,0:T(8,128)}, u32[]{:S(2)}, u32[]{:S(2)}) collective-permute-start(f32[256,256]{1,0:T(8,128)} %constant_dynamic-slice_fusion.5), channel_id=1, source_target_pairs={{0,16},{1,17},{4,20},{5,21},{8,24},{9,25},{12,28},{13,29},{18,2},{... | collective-permute-start | bytes 786440 | tf_op jit(solution)/shard_map/ppermute | solution.py:125
  53.0 21.3 %collective-permute-start.19 = (f32[256,256]{1,0:T(8,128)}, f32[256,256]{1,0:T(8,128)}, u32[]{:S(2)}, u32[]{:S(2)}) collective-permute-start(f32[256,256]{1,0:T(8,128)} %constant_dynamic-slice_fusion.5), channel_id=1, source_target_pairs={{0,8},{1,9},{4,12},{5,13},{8,0},{9,1},{12,4},{13,5},{18,26},{19,27... | collective-permute-start | bytes 786440 | tf_op jit(solution)/shard_map/ppermute | solution.py:125
  55.4 20.9 %collective-permute-start.20 = (f32[256,256]{1,0:T(8,128)}, f32[256,256]{1,0:T(8,128)}, u32[]{:S(2)}, u32[]{:S(2)}) collective-permute-start(f32[256,256]{1,0:T(8,128)} %constant_dynamic-slice_fusion.5), channel_id=1, source_target_pairs={{0,24},{1,25},{4,28},{5,29},{8,16},{9,17},{12,20},{13,21},{18,10},... | collective-permute-start | bytes 786440 | tf_op jit(solution)/shard_map/ppermute | solution.py:125
  70.6 28.2 %collective-permute-start.21 = (f32[256,256]{1,0:T(8,128)}, f32[256,256]{1,0:T(8,128)S(1)}, u32[]{:S(2)}, u32[]{:S(2)}) collective-permute-start(f32[256,256]{1,0:T(8,128)} %fusion.17), channel_id=1, source_target_pairs={{0,16},{1,17},{4,20},{5,21},{8,24},{9,25},{12,28},{13,29},{18,2},{... | collective-permute-start | bytes 786440 | tf_op jit(solution)/shard_map/ppermute | solution.py:125
  73.6 25.7 %collective-permute-start.22 = (f32[256,256]{1,0:T(8,128)}, f32[256,256]{1,0:T(8,128)S(1)}, u32[]{:S(2)}, u32[]{:S(2)}) collective-permute-start(f32[256,256]{1,0:T(8,128)} %fusion.17), channel_id=1, source_target_pairs={{0,8},{1,9},{4,12},{5,13},{8,0},{9,1},{12,4},{13,5},{18,26},{19,27... | collective-permute-start | bytes 786440 | tf_op jit(solution)/shard_map/ppermute | solution.py:125
  74.3 25.0 %collective-permute-start.23 = (f32[256,256]{1,0:T(8,128)}, f32[256,256]{1,0:T(8,128)S(1)}, u32[]{:S(2)}, u32[]{:S(2)}) collective-permute-start(f32[256,256]{1,0:T(8,128)} %fusion.17), channel_id=1, source_target_pairs={{0,24},{1,25},{4,28},{5,29},{8,16},{9,17},{12,20},{13,21},{18,10},... | collective-permute-start | bytes 786440 | tf_op jit(solution)/shard_map/ppermute | solution.py:125
  76.4 33.3 %collective-permute-start.24 = (f32[1024,256]{1,0:T(8,128)S(1)}, f32[1024,256]{1,0:T(8,128)S(1)}, u32[]{:S(2)}, u32[]{:S(2)}) collective-permute-start(f32[1024,256]{1,0:T(8,128)S(1)} %copy-done.6), channel_id=1, source_target_pairs={{0,1},{1,0},{2,3},{3,2},{4,5},{5,4},{6,7},{7,6},{8,9},{9,8},{10,11... | collective-permute-start | bytes 3145736 | tf_op jit(solution)/shard_map/ppermute | solution.py:125
  98.9 47.5 %collective-permute-start.7 = (f32[1280,256]{1,0:T(8,128)}, f32[1280,256]{1,0:T(8,128)}, u32[]{:S(2)}, u32[]{:S(2)}) collective-permute-start(f32[1280,256]{1,0:T(8,128)} %select_dynamic-update-slice_fusion), channel_id=1, source_target_pairs={{0,1},{1,0},{2,3},{3,2},{4,5},{5,4},{6,7},{7,6},{8,9},{9,8},{10,11... | collective-permute-start | bytes 3932168 | tf_op jit(solution)/shard_map/ppermute | solution.py:125
  112.2 17.0 %collective-permute-start.25 = (f32[128,256]{1,0:T(8,128)S(1)}, f32[128,256]{1,0:T(8,128)S(1)}, u32[]{:S(2)}, u32[]{:S(2)}) collective-permute-start(f32[128,256]{1,0:T(8,128)S(1)} %get-tuple-element.53), channel_id=1, source_target_pairs={{0,8},{1,9},{2,10},{3,11},{4,12},{5,13},{6,14},{7,15},{8,0},{9,1},... | collective-permute-start | bytes 393224 | tf_op jit(solution)/shard_map/ppermute | solution.py:125
  138.9 36.1 %collective-permute-start.38 = (f32[512,256]{1,0:T(8,128)S(1)}, f32[512,256]{1,0:T(8,128)S(1)}, u32[]{:S(2)}, u32[]{:S(2)}) collective-permute-start(f32[512,256]{1,0:T(8,128)S(1)} %get-tuple-element.45), channel_id=1, source_target_pairs={{0,8},{1,9},{4,12},{5,13},{8,0},{9,1},{12,4},{13,5},{18,26},{19,27... | collective-permute-start | bytes 1572872 | tf_op jit(solution)/shard_map/ppermute | solution.py:125
  139.6 38.9 %collective-permute-start.40 = (f32[512,256]{1,0:T(8,128)S(1)}, f32[512,256]{1,0:T(8,128)S(1)}, u32[]{:S(2)}, u32[]{:S(2)}) collective-permute-start(f32[512,256]{1,0:T(8,128)S(1)} %get-tuple-element.45), channel_id=1, source_target_pairs={{2,26},{3,27},{6,30},{7,31},{10,18},{11,19},{14,22},{15,23},{16,8}... | collective-permute-start | bytes 1572872 | tf_op jit(solution)/shard_map/ppermute | solution.py:125
  144.2 32.0 %collective-permute-start.39 = (f32[512,256]{1,0:T(8,128)S(1)}, f32[512,256]{1,0:T(8,128)S(1)}, u32[]{:S(2)}, u32[]{:S(2)}) collective-permute-start(f32[512,256]{1,0:T(8,128)S(1)} %get-tuple-element.44), channel_id=1, source_target_pairs={{2,18},{3,19},{6,22},{7,23},{10,26},{11,27},{14,30},{15,31},{16,0}... | collective-permute-start | bytes 1572872 | tf_op jit(solution)/shard_map/ppermute | solution.py:125
  147.0 27.8 %collective-permute-start.33 = (f32[128,256]{1,0:T(8,128)S(1)}, f32[128,256]{1,0:T(8,128)S(1)}, u32[]{:S(2)}, u32[]{:S(2)}) collective-permute-start(f32[128,256]{1,0:T(8,128)S(1)} %add_add_fusion.1), channel_id=1, source_target_pairs={{16,8},{17,9},{24,0},{25,1}} | collective-permute-start | bytes 393224 | tf_op jit(solution)/shard_map/ppermute | solution.py:125
  149.2 31.9 %collective-permute-start.35 = (f32[256,256]{1,0:T(8,128)S(1)}, f32[256,256]{1,0:T(8,128)S(1)}, u32[]{:S(2)}, u32[]{:S(2)}) collective-permute-start(f32[256,256]{1,0:T(8,128)S(1)} %get-tuple-element.37), channel_id=1, source_target_pairs={{0,2},{1,3},{2,0},{3,1},{4,6},{5,7},{6,4},{7,5},{8,10},{9,11},{10,... | collective-permute-start | bytes 786440 | tf_op jit(solution)/shard_map/ppermute | solution.py:125
  174.9 26.3 %collective-permute-start.37 = (f32[256,256]{1,0:T(8,128)S(1)}, f32[256,256]{1,0:T(8,128)S(1)}, u32[]{:S(2)}, u32[]{:S(2)}) collective-permute-start(f32[256,256]{1,0:T(8,128)S(1)} %get-tuple-element.38), channel_id=1, source_target_pairs={{0,6},{1,7},{2,4},{3,5},{4,2},{5,3},{6,0},{7,1},{8,14},{9,15},{10,... | collective-permute-start | bytes 786440 | tf_op jit(solution)/shard_map/ppermute | solution.py:125
  176.2 32.0 %collective-permute-start.34 = (f32[512,256]{1,0:T(8,128)S(1)}, f32[512,256]{1,0:T(8,128)S(1)}, u32[]{:S(2)}, u32[]{:S(2)}) collective-permute-start(f32[512,256]{1,0:T(8,128)S(1)} %maximum_select_fusion.4), channel_id=1, source_target_pairs={{0,1},{1,0},{2,3},{3,2},{4,5},{5,4},{6,7},{7,6},{8,9},{9,8},{10,11... | collective-permute-start | bytes 1572872 | tf_op jit(solution)/shard_map/ppermute | solution.py:125
  178.7 25.4 %collective-permute-start.41 = (f32[256,256]{1,0:T(8,128)S(1)}, f32[256,256]{1,0:T(8,128)S(1)}, u32[]{:S(2)}, u32[]{:S(2)}) collective-permute-start(f32[256,256]{1,0:T(8,128)S(1)} %get-tuple-element.56), channel_id=1, source_target_pairs={{0,0},{1,1},{4,2},{5,3},{8,8},{9,9},{12,10},{13,11},{18,16},{19,17... | collective-permute-start | bytes 786440 | tf_op jit(solution)/shard_map/ppermute | solution.py:125
  181.1 23.0 %collective-permute-start.42 = (f32[256,256]{1,0:T(8,128)S(1)}, f32[256,256]{1,0:T(8,128)S(1)}, u32[]{:S(2)}, u32[]{:S(2)}) collective-permute-start(f32[256,256]{1,0:T(8,128)S(1)} %get-tuple-element.57), channel_id=1, source_target_pairs={{0,4},{1,5},{4,6},{5,7},{8,12},{9,13},{12,14},{13,15},{18,20},{19,... | collective-permute-start | bytes 786440 | tf_op jit(solution)/shard_map/ppermute | solution.py:125
  220.5 24.8 %collective-permute-start.46 = (f32[256,256]{1,0:T(8,128)S(1)}, f32[256,256]{1,0:T(8,128)S(1)}, u32[]{:S(2)}, u32[]{:S(2)}) collective-permute-start(f32[256,256]{1,0:T(8,128)S(1)} %get-tuple-element.61), channel_id=1, source_target_pairs={{0,6},{1,7},{2,4},{3,5},{4,2},{5,3},{6,0},{7,1},{8,14},{9,15},{10,... | collective-permute-start | bytes 786440 | tf_op jit(solution)/shard_map/ppermute | solution.py:125
  (37 other events, 352.1 us)

commit v2 on v0

v2 whole, which is shorter than its diff:
```python
import functools

import jax
import jax.numpy as jnp
from jax import lax
from jax.experimental import pallas as pl
from jax.experimental.pallas import tpu as pltpu
from jax.sharding import PartitionSpec as P

NB = 256
ROW, PAIR, LANE = 0, 1, 2
SQUARE = jax.ShapeDtypeStruct((NB, NB), jnp.float32)


def dot(left, right):
    return jnp.dot(
        left, right, precision=lax.Precision.HIGHEST, preferred_element_type=jnp.float32
    )


def split(value):
    high = value.astype(jnp.bfloat16)
    return high, (value - high.astype(jnp.float32)).astype(jnp.bfloat16)


def dot3(left, right):
    once = functools.partial(jnp.dot, preferred_element_type=jnp.float32)
    return once(left[0], right[0]) + (once(left[0], right[1]) + once(left[1], right[0]))


def quick(left, right):
    return dot3(split(left), split(right))


def positions():
    rows = lax.broadcasted_iota(jnp.int32, (NB, NB), 0)
    cols = lax.broadcasted_iota(jnp.int32, (NB, NB), 1)
    return rows, cols


def call(kernel, name, out_shape, ids, *arrays, scratch=()):
    sizes = [x.size * x.dtype.itemsize for x in (*arrays, *jax.tree.leaves(out_shape))]
    return pl.pallas_call(
        kernel,
        out_shape=out_shape,
        in_specs=[pl.BlockSpec(memory_space=pltpu.SMEM)]
        + [pl.BlockSpec(memory_space=pltpu.VMEM)] * len(arrays),
        scratch_shapes=list(scratch),
        name=name,
        cost_estimate=pl.CostEstimate(flops=1, bytes_accessed=1, transcendentals=0),
        compiler_params=pltpu.CompilerParams(vmem_limit_bytes=min(60, 16 + sum(sizes) // 2**19) * 2**20),
    )(ids, *arrays)


def inverse_kernel(ids, block_ref, out_ref):
    @pl.when((ids[PAIR] == 0) & (ids[ROW] < 2))
    def _():
        half = NB // 2
        rows = lax.broadcasted_iota(jnp.int32, (half, half), 0)
        cols = lax.broadcasted_iota(jnp.int32, (half, half), 1)
        blocks = [block_ref[:half, :half], block_ref[half:, half:]]
        diagonal = rows == cols
        inverses = [
            jnp.where(diagonal, 1.0 / jnp.where(diagonal, x, 1.0), 0.0) for x in blocks
        ]
        size = 1
        while size < half:
            corner = (
                (rows // (2 * size) == cols // (2 * size))
                & (rows // size % 2 == 1)
                & (cols // size % 2 == 0)
            )
            inner = [dot(jnp.where(corner, x, 0.0), y) for x, y in zip(blocks, inverses)]
            inverses = [y - dot(y, x) for x, y in zip(inner, inverses)]
            size *= 2
        out_ref[:half, :half] = inverses[0]
        out_ref[:half, half:] = jnp.zeros((half, half), jnp.float32)
        out_ref[half:, half:] = inverses[1]
        out_ref[half:, :half] = -dot(inverses[1], dot(block_ref[half:, :half], inverses[0]))

    @pl.when((ids[PAIR] != 0) | (ids[ROW] >= 2))
    def _():
        out_ref[...] = jnp.zeros_like(out_ref)


def mask_kernel(n_rows, n_cols, ids, own, other, low_1, low_2, high_1, high_2):
    rows, cols = positions()
    below = rows - cols
    first = ids[LANE] == 0
    blocks = own.shape[0] // NB

    def masked(index, half, core):
        at = pl.ds(pl.multiple_of(index * NB, NB), NB)
        columns = slice(half * NB, (half + 1) * NB)
        mine = first if core == 0 else jnp.logical_not(first)
        value = jnp.where(mine, own[at, columns], other[at, columns])
        row_block = index * n_rows + ids[ROW]
        col_block = 2 * ids[PAIR] + half * n_cols + core
        least = jnp.where(row_block > col_block, -NB, jnp.where(row_block == col_block, 0, NB))
        least = jnp.where(row_block >= 2, least, NB)
        return split(jnp.where(below >= least, value, 0.0))

    @pl.loop(0, blocks)
    def _(index):
        for core in range(2):
            columns = slice(core * NB, (core + 1) * NB)
            at = pl.ds(pl.multiple_of(index * NB, NB), NB)
            low_1[at, columns], low_2[at, columns] = masked(index, 0, core)

    @pl.loop(0, blocks // 2)
    def _(index):
        for core in range(2):
            columns = slice(core * NB, (core + 1) * NB)
            at = pl.ds(pl.multiple_of(index * NB, NB), NB)
            high_1[at, columns], high_2[at, columns] = masked(index + blocks // 2, 1, core)


def column_kernel(n_rows, ids, low_1, low_2, high_1, high_2, *refs):
    refs, turned, low_ref, targets, sums = refs[:-7], refs[-7], refs[-6], refs[-5:-1], refs[-1]
    blocks = low_1.shape[0] // NB
    per_piece = blocks // 4
    low = jnp.zeros((NB, 2 * NB), jnp.float32)
    high = jnp.zeros((NB, 2 * NB), jnp.float32)
    for index, piece in enumerate(refs):
        for inner in range(per_piece):
            block = index * per_piece + inner
            at = slice(inner * NB, (inner + 1) * NB)
            value = piece[at, :]
            if block == 0:
                value = jnp.where(ids[ROW] >= 2, value, 0.0)
            value = value.T
            turned[:, block * NB : (block + 1) * NB] = value
            value = split(value)
            at = slice(block * NB, (block + 1) * NB)
            low += dot3(value, (low_1[at, :], low_2[at, :]))
            if block >= blocks // 2:
                block -= blocks // 2
                at = slice(block * NB, (block + 1) * NB)
                high += dot3(value, (high_1[at, :], high_2[at, :]))
    low_ref[...] = low
    sums[0], sums[1], sums[2], sums[3] = low[:, :NB], low[:, NB:], high[:, :NB], high[:, NB:]
    for d in range(n_rows):
        target = ids[ROW] ^ d
        targets[d][...] = sums[jnp.where(target // 2 == ids[PAIR] % 2, 0, 2) + target % 2]


def row_kernel(n_pairs, n_rows, ids, low_1, low_2, high_1, high_2, *refs):
    held, (turned, turned_other, adjoint, low), columns = refs[:4], refs[4:8], refs[8:12]
    shares, slices = refs[12 : 12 + n_pairs], refs[12 + n_pairs : 12 + n_pairs + n_rows]
    remaining, sums = refs[-2:]
    pair, row = ids[PAIR], ids[ROW]
    x_is_0 = row % 2 == 0
    near = row // 2 == pair % 2
    first = ids[LANE] == 0

    def panel(same, across):
        return split(
            jnp.concatenate(
                [jnp.where(x_is_0, same, across), jnp.where(x_is_0, across, same)], 0
            )
        )

    v0, v1, v2, v3 = [ref[...] for ref in held]
    panel_low = panel(jnp.where(near, v0, v2), jnp.where(near, v1, v3))
    panel_high = panel(jnp.where(near, v2, v0), jnp.where(near, v3, v1))
    own = jnp.zeros((NB, NB), jnp.float32)
    other = jnp.zeros((NB, NB), jnp.float32)
    for block in range(n_pairs):
        at = slice(block * NB, (block + 1) * NB)
        product = dot3((low_1[at, :], low_2[at, :]), panel_low)
        if block >= n_pairs // 2:
            upper = slice((block - n_pairs // 2) * NB, (block - n_pairs // 2 + 1) * NB)
            product += dot3((high_1[upper, :], high_2[upper, :]), panel_high)
        remaining[block] = jnp.where(pair == 0, adjoint[at, :NB], 0.0) - product
        product = split(product)
        own += dot3(split(turned[:, at]), product)
        other += dot3(split(turned_other[:, at]), product)
    for d in range(n_pairs):
        shares[d][...] = remaining[pair ^ d]
    first_pair = pair == 0
    own_term = jnp.where(first, low[:, :NB], low[:, NB:])
    own_term = jnp.where(first_pair, own_term, 0.0)
    cross_term = jnp.where(first_pair, low[:, NB:], 0.0)
    own_sum = (own_term - own).T - own
    other_sum = jnp.where(first, cross_term.T - other, -other.T)
    height = 2 * NB // n_rows
    for index in range(n_rows // 2):
        at = slice(index * height, (index + 1) * height)
        sums[index] = own_sum[at]
        sums[index + n_rows // 2] = other_sum[at]
    for d in range(n_rows):
        slices[d][:NB, :] = columns[d][...]
        slices[d][NB:, :] = sums[row ^ d]


def by_row(row, values):
    result = values[3]
    for index in (2, 1, 0):
        result = jnp.where(row == index, values[index], result)
    return result


def carried_blocks(ids, refs):
    values = [ref[...] for ref in refs]
    top = by_row(ids[ROW], values)
    link = by_row(ids[ROW], [values[1], values[0], values[3], values[2]])
    return jnp.where(ids[LANE] == 0, top, link), link


def solve_kernel(n_pairs, ids, *refs):
    shares, owned, carried = refs[:n_pairs], refs[n_pairs], refs[n_pairs + 1 : -2]
    total_ref, solved = refs[-2:]
    total = shares[0][...]
    for ref in shares[1:]:
        total = total + ref[...]
    total = total - owned[...].T
    inverse, _ = carried_blocks(ids, carried)
    total_ref[...] = total
    solved[:NB, :] = quick(total, inverse)
    solved[NB:, :] = inverse


def end_kernel(ids, total, solved, second, c0, c1, c2, c3, blocks, across, blocks_other, across_other, sums_ref, sums_other, out_ref):
    row, first = ids[ROW], ids[LANE] == 0
    leading = (ids[PAIR] == 0) & (row < 2)

    @pl.when(jnp.logical_not(leading))
    def _():
        inverse, link = carried_blocks(ids, (c0, c1, c2, c3))
        whole = quick(total[...] - quick(second[:NB, :], link), inverse)
        out_ref[...] = jnp.where(first, whole, solved[:NB, :])

    @pl.when(leading)
    def _():
        rows, cols = positions()
        in_first_row = row == 0

        def tril(x):
            return jnp.where(rows >= cols, x, 0.0)

        def phi(x):
            return jnp.where(rows > cols, x, jnp.where(rows == cols, 0.5 * x, 0.0))

        def diagonal_adjoint(block, block_bar, inverse_t, inverse):
            inner = phi(quick(block.T, block_bar))
            s = quick(inverse_t, quick(inner, inverse))
            return phi(s + s.T)

        def by_lane(own, other):
            return jnp.where(first, own, other), jnp.where(first, other, own)

        def held(own, other):
            firsts, seconds = by_lane(own[...], other[...])
            return [x[i * NB : (i + 1) * NB] for x in (firsts, seconds) for i in range(2)]

        mine, theirs = held(blocks, blocks_other), held(across, across_other)
        l0, a00, _, _ = [jnp.where(in_first_row, a, b) for a, b in zip(mine, theirs)]
        link, a10, l1, a11 = [jnp.where(in_first_row, b, a) for a, b in zip(mine, theirs)]
        inv0, inv1 = by_lane(solved[NB:, :], second[NB:, :])

        def ordered(ref):
            value = ref[...]
            height = value.shape[0] // 4
            parts = [value[i * height : (i + 1) * height] for i in range(4)]
            swapped = jnp.concatenate([parts[1], parts[0], parts[3], parts[2]], 0)
            return jnp.where(in_first_row, value, swapped)

        sums_0, sums_1 = by_lane(ordered(sums_ref), ordered(sums_other))
        z00, z11, z10 = sums_0[:NB], sums_1[:NB], sums_0[NB:] + sums_1[NB:]
        inv1_t, inv0_t = inv1.T, inv0.T
        cross = quick(inv1_t, z10)
        k1 = tril(a11 - quick(inv1_t, z11))
        e1 = diagonal_adjoint(tril(l1), k1, inv1_t, inv1)
        rest = a10 - quick(e1 + e1.T, link) - cross
        g0 = quick(rest, inv0)
        k0 = tril(a00 - quick(inv0_t, z00 - quick(link.T, cross) + quick(rest.T, link)))
        e0 = diagonal_adjoint(tril(l0), k0, inv0_t, inv0)
        out_ref[...] = jnp.where(
            in_first_row, jnp.where(first, e0, 0.0), jnp.where(first, g0, e1)
        )


def place_kernel(n_pairs, ids, *refs):
    own, other, out_ref = refs[:n_pairs], refs[n_pairs:-1], refs[-1]
    first = ids[LANE] == 0
    for d in range(n_pairs):
        at = pl.ds(pl.multiple_of((ids[PAIR] ^ d) * NB, NB), NB)
        mine, theirs = own[d][...], other[d][...]
        out_ref[at, :NB] = jnp.where(first, mine, theirs)
        out_ref[at, NB:] = jnp.where(first, theirs, mine)


def after(value, *earlier):
    return lax.optimization_barrier((value, *earlier))[0]


def together(*values):
    return lax.optimization_barrier(values)


def local(factor, adjoint):
    n_rows = lax.axis_size("row")
    n_cols = lax.axis_size("col")
    n_pairs = n_cols // 2
    row_id = lax.axis_index("row")
    col_id = lax.axis_index("col")
    pair = col_id // 2
    lane = col_id % 2
    ids = jnp.stack([row_id, pair, lane])
    near = row_id // 2 == pair % 2
    first_pair = pair == 0
    local_rows = factor.shape[0]
    piece_rows = local_rows // 4

    def send(value, targets):
        edges = []
        for r in range(n_rows):
            for c in range(n_cols):
                target = targets(r, c // 2, c % 2)
                if target is not None:
                    edges.append((r * n_cols + c, target[0] * n_cols + target[1] * 2 + target[2]))
        return lax.ppermute(value, ("row", "col"), edges)

    def swap(value):
        return send(value, lambda r, p, k: (r, p, 1 - k))

    def swap_rows(value, d):
        return send(value, lambda r, p, k: (r ^ d, p, k))

    def swap_pairs(value, d):
        return send(value, lambda r, p, k: (r, p ^ d, k))

    panel = together(
        *[factor[i * piece_rows : (i + 1) * piece_rows, :NB] for i in range(4)], factor[:NB, :NB]
    )
    corner = panel[-1]

    def hop(value, number):
        return send(value, lambda r, p, k: (r, number, k) if p == number - 1 else None)

    def travel(value, hops):
        arrived = [value]
        for number in hops:
            arrived.append(hop(arrived[-1], number))
        return arrived

    def here(arrived):
        value = arrived[0]
        for p in range(1, len(arrived)):
            value = jnp.where(pair == p, arrived[p], value)
        return value

    middle = n_pairs // 2
    row_ids = jnp.arange(piece_rows, dtype=jnp.int32)
    trailing = ((row_ids >= NB) | (row_id >= 2))[:, None]

    def chosen(nearer, farther):
        start = pair // 2 % (piece_rows // NB) * NB
        value = here(nearer[:middle] + farther[middle:])
        return lax.dynamic_slice_in_dim(value, start, NB, 0)

    own_inverse = call(inverse_kernel, "inverse", SQUARE, ids, corner)
    carried = jnp.where((row_id == 1) & (lane == 0), corner, own_inverse)
    leading_piece = jnp.where(
        row_id < 2, jnp.concatenate([carried, panel[0][NB:]], 0), panel[0]
    )
    blocks = jnp.concatenate([corner, adjoint[:NB, :NB]], 0)
    across = send(blocks, lambda r, p, k: (r ^ 1, p, k) if p == 0 and r < 2 else None)
    every, nearest = range(1, n_pairs), range(1, middle)
    arrived_3, arrived_1, arrived_2 = [travel(panel[i], every) for i in (3, 1, 2)]
    arrived_0 = travel(leading_piece, nearest)
    high = swap_rows(chosen(arrived_2, arrived_3), 2)
    high, across, blocks, *rest = together(high, across, blocks, *arrived_3, *arrived_1, *arrived_2, *arrived_0)
    arrived_3, rest = rest[:n_pairs], rest[n_pairs:]
    arrived_1, rest = rest[:n_pairs], rest[n_pairs:]
    arrived_2, arrived_0 = rest[:n_pairs], rest[n_pairs:]

    masked_0 = [jnp.where(trailing, x, 0.0) for x in arrived_0]
    low = chosen(masked_0, arrived_1)
    held = jnp.where(near, low, high)
    held = [held] + [swap_rows(held, d) for d in range(1, n_rows)]
    carried = [x[:NB] for x in arrived_0]
    carried = carried + travel(carried[-1], range(middle, n_pairs))[1:]
    columns = jax.ShapeDtypeStruct((local_rows, 2 * NB), jnp.bfloat16)
    half_columns = jax.ShapeDtypeStruct((local_rows // 2, 2 * NB), jnp.bfloat16)
    masked = call(
        functools.partial(mask_kernel, n_rows, n_cols),
        "masked",
        (columns, columns, half_columns, half_columns),
        ids,
        adjoint,
        swap(after(adjoint, high)),
    )
    pieces = here(masked_0), here(arrived_1), here(arrived_2), here(arrived_3)
    rest = together(*held, *masked, *pieces, *carried)
    held, masked, pieces, carried = rest[:4], rest[4:8], rest[8:12], here(rest[12:])

    turned, low, *block_sums = call(
        functools.partial(column_kernel, n_rows),
        "columns",
        (
            jax.ShapeDtypeStruct((NB, local_rows), jnp.float32),
            jax.ShapeDtypeStruct((NB, 2 * NB), jnp.float32),
        )
        + (SQUARE,) * n_rows,
        ids,
        *masked,
        *pieces,
        scratch=(pltpu.VMEM((4, NB, NB), jnp.float32),),
    )

    height = 2 * NB // n_rows
    rows = call(
        functools.partial(row_kernel, n_pairs, n_rows),
        "rows",
        (SQUARE,) * n_pairs
        + (jax.ShapeDtypeStruct((NB + height, NB), jnp.float32),) * n_rows,
        ids,
        *masked,
        *held,
        turned,
        swap(turned),
        adjoint,
        low,
        *block_sums,
        scratch=(
            pltpu.VMEM((n_pairs, NB, NB), jnp.float32),
            pltpu.VMEM((n_rows, height, NB), jnp.float32),
        ),
    )
    carried = [carried] + [swap_rows(carried, d) for d in range(1, n_rows)]
    rest = together(*carried, *rows)
    carried, rows = rest[:n_rows], rest[n_rows:]
    shares, slices = rows[:n_pairs], rows[n_pairs:]

    farther_shares = [swap_pairs(shares[d], d) for d in range(2, n_pairs)]
    slices = [slices[0]] + [swap_rows(slices[d], d) for d in range(1, n_rows)]
    next_share, *rest = together(shares[1], *farther_shares, *slices)
    farther_shares, slices = rest[: n_pairs - 2], rest[n_pairs - 2 :]
    slices = sum(slices[1:], slices[0])

    def owner(r, p, k):
        half = 0 if r // 2 == p % 2 else 1
        return p % 2 * 2 + r % 2, p // 2 + half * (n_pairs // 2), k

    owned = send(slices[:NB], owner)
    total = slices[NB:]
    totals = [total] + [swap_pairs(total, d) for d in range(1, n_pairs)]
    next_share = swap_pairs(next_share, 1)
    owned, next_share, *totals = together(owned, next_share, *totals)
    shares = [shares[0], next_share, *farther_shares]

    mine, solved = call(
        functools.partial(solve_kernel, n_pairs),
        "solve",
        (SQUARE, jax.ShapeDtypeStruct((2 * NB, NB), jnp.float32)),
        ids,
        *shares,
        owned,
        *carried,
    )
    total = sum(totals[1:], totals[0])
    sums = [total] + [swap_rows(total, d) for d in range(1, n_rows)]
    second = swap(solved)
    blocks_other = swap(after(blocks, solved))
    second, blocks_other, *sums = together(second, blocks_other, *sums)
    across_other = swap(after(across, second))
    sums = jnp.concatenate(sums, 0)
    result = call(
        end_kernel,
        "end",
        SQUARE,
        ids,
        mine,
        solved,
        second,
        *carried,
        blocks,
        across,
        blocks_other,
        across_other,
        sums,
        swap(sums),
    )
    results = [result] + [swap_pairs(result, d) for d in range(1, n_pairs)]
    return call(
        functools.partial(place_kernel, n_pairs),
        "place",
        jax.ShapeDtypeStruct((local_rows, 2 * NB), jnp.float32),
        ids,
        *results,
        *[swap(x) for x in results],
    )


def solution(mesh):
    placed = (P("row", "col"), P("row", "col"))
    return jax.shard_map(
        local, mesh=mesh, in_specs=placed, out_specs=P("row", None), check_vma=False
    )
```

time: 1060 us -> 179 us (0.17); the launches traced: 1050 us -> 178 us
  between operations: 516 us -> 0.4 us
  waiting for transfers between devices: 270 us -> 88.6 us
  matrix products: 172 us -> 0 us
  starting transfers between devices: 1.44 us -> 60.4 us
  local copies, waits for them, and re-layouts: 55.7 us -> 3.63 us
  other arithmetic: 30.1 us -> 2.89 us
  Pallas kernels: 0 us -> 22.1 us
    psum x5 -> x0, waiting for transfers between devices: 207 us -> none  [the longest x1 68 us: from_root(): return lax.psum(block, axis)]
    dot_general x525 -> x0, matrix products: 172 us -> none  [the longest x516 151 us: matmul(): jnp.dot(left_side, right_side, precision=HIGHEST_PRECISION, preferred_ele...]
    ppermute x0 -> x46, waiting for transfers between devices: none -> 88.6 us  [send(): return lax.ppermute(value, ('row', 'col'), edges)]
    all_gather x4 -> x0, waiting for transfers between devices: 63.4 us -> none  [the longest x1 28.6 us: local(): lax.all_gather(y_second[:NB], 'row', axis=0, tiled=True)]
    ppermute x0 -> x46, starting transfers between devices: none -> 60.4 us  [send(): return lax.ppermute(value, ('row', 'col'), edges)]
    slice x48 -> x4, local copies, waits for them, and re-layouts: 37.6 us -> 2.17 us  [the longest x1 2.12 us: local(): factor[i * piece_rows:(i + 1) * piece_rows, :NB]]
    pallas_call x0 -> x7, Pallas kernels: none -> 22.1 us  [call(): pl.pallas_call(kernel, out_shape=out_shape, in_specs=[pl.BlockSpec(memory...]
    concatenate x207 -> x1, other arithmetic: 19.7 us -> 0.04 us  [local(): blocks = jnp.concatenate([corner, adjoint[:NB, :NB]], 0)]
  transfers between devices with their start and end apart: 9 -> 46, of which waited for: 7 -> 22; matrix products, arithmetic and copies ran while one was open for 21% -> 2% of each run, Pallas kernels for 0% -> 7%
where the time goes in v2:
time: 179 us; the launch traced here: 178 us
  waiting for transfers between devices  88.6 us (49%)
  starting transfers between devices  60.4 us (34%)
  Pallas kernels  22.1 us (12%)
  local copies, waits for them, and re-layouts  3.63 us (2%)
  other arithmetic  2.89 us (2%)
    ppermute x46, waiting for transfers between devices, send(): return lax.ppermute(value, ('row', 'col'), edges)  88.6 us
    ppermute x46, starting transfers between devices, send(): return lax.ppermute(value, ('row', 'col'), edges)  60.4 us
    pallas_call x7, Pallas kernels, call(): pl.pallas_call(kernel, out_shape=out_shape, in_specs=[pl.BlockSpec(memory...  22.1 us
  transfers between devices with their start and end apart: 46, of which 22 were waited for; matrix products, arithmetic and copies ran while one was open for 2% of the time, Pallas kernels for 7%

profile of v2, /device:TPU:0, one launch (start us, length us, event | category | flops | bytes accessed | tf_op | source)
XLA Modules:
  0.0 178.1 jit_solution(3424843966119902455)
XLA Ops:
  2.1 5.6 %collective-permute-start = (f32[256,256]{1,0:T(8,128)S(1)}, f32[256,256]{1,0:T(8,128)}, u32[]{:S(2)}, u32[]{:S(2)}) collective-permute-start(f32[256,256]{1,0:T(8,128)S(1)} %get-tuple-element.121), channel_id=1, source_target_pairs={{0,2},{1,3},{8,10},{9,11},{16,18},{17,19},{24,26},{25,27}} | collective-permute-start | bytes 786440 | tf_op jit(solution)/shard_map/ppermute | solution.py:322
  15.2 4.3 %collective-permute-done.6 = f32[256,256]{1,0:T(8,128)} collective-permute-done((f32[256,256]{1,0:T(8,128)}, f32[256,256]{1,0:T(8,128)}, u32[]{:S(2)}, u32[]{:S(2)}) %collective-permute-start.6) | collective-permute-done | bytes 262176 | tf_op jit(solution)/shard_map/ppermute | solution.py:322
  20.8 3.0 %collective-permute-done.3 = f32[256,256]{1,0:T(8,128)} collective-permute-done((f32[256,256]{1,0:T(8,128)S(1)}, f32[256,256]{1,0:T(8,128)}, u32[]{:S(2)}, u32[]{:S(2)}) %collective-permute-start.3) | collective-permute-done | bytes 262176 | tf_op jit(solution)/shard_map/ppermute | solution.py:322
  26.6 3.4 %collective-permute-start.5 = (f32[512,256]{1,0:T(8,128)S(1)}, f32[512,256]{1,0:T(8,128)}, u32[]{:S(2)}, u32[]{:S(2)}) collective-permute-start(f32[512,256]{1,0:T(8,128)S(1)} %pad_maximum_fusion.blocks), channel_id=1, source_target_pairs={{0,8},{1,9},{8,0},{9,1}} | collective-permute-start | bytes 1572872 | tf_op jit(solution)/shard_map/ppermute | solution.py:322
  30.0 4.6 %inverse.1 = f32[256,256]{1,0:T(8,128)S(1)} custom-call(s32[3]{0:T(128)S(1)} %pad_add_fusion.ids, f32[256,256]{1,0:T(8,128)S(1)} %get-tuple-element.101.block_ref), custom_call_target="tpu_custom_call" | custom-call | flops 1 | bytes 1 | tf_op jit(solution)/shard_map/inverse/pallas_call | solution.py:43
  42.1 3.4 %collective-permute-done.4 = f32[256,256]{1,0:T(8,128)S(1)} collective-permute-done((f32[256,256]{1,0:T(8,128)S(1)}, f32[256,256]{1,0:T(8,128)S(1)}, u32[]{:S(2)}, u32[]{:S(2)}) %collective-permute-start.4) | collective-permute-done | bytes 262176 | tf_op jit(solution)/shard_map/ppermute | solution.py:322
  52.8 2.5 %masked.1 = (bf16[1024,512]{1,0:T(8,128)(2,1)S(1)}, bf16[1024,512]{1,0:T(8,128)(2,1)S(1)}, bf16[512,512]{1,0:T(8,128)(2,1)S(1)}, bf16[512,512]{1,0:T(8,128)(2,1)S(1)}) custom-call(s32[3]{0:T(128)S(1)} %pad_add_fusion.ids, f32[1024,512]{1,0:T(8,128)S(1)} %copy-done, f32[1024,512]{1,0:T(8,128)} %collective-permute-done.15.other), custom_call_target="tpu_custom_call" | custom-call | flops 1 | bytes 1 | tf_op jit(solution)/shard_map/masked/pallas_call | solution.py:43
  55.4 3.1 %collective-permute-done.14.refs_3_ = f32[256,256]{1,0:T(8,128)S(1)} collective-permute-done((f32[256,256]{1,0:T(8,128)S(1)}, f32[256,256]{1,0:T(8,128)S(1)}, u32[]{:S(2)}, u32[]{:S(2)}) %collective-permute-start.14) | collective-permute-done | bytes 262176 | tf_op jit(solution)/shard_map/ppermute | solution.py:322
  58.5 4.4 %collective-permute-done.13.refs_2_ = f32[256,256]{1,0:T(8,128)S(1)} collective-permute-done((f32[256,256]{1,0:T(8,128)S(1)}, f32[256,256]{1,0:T(8,128)S(1)}, u32[]{:S(2)}, u32[]{:S(2)}) %collective-permute-start.13) | collective-permute-done | bytes 262176 | tf_op jit(solution)/shard_map/ppermute | solution.py:322
  68.7 5.0 %rows.1 = (f32[256,256]{1,0:T(8,128)S(1)}, f32[256,256]{1,0:T(8,128)S(1)}, f32[256,256]{1,0:T(8,128)S(1)}, f32[256,256]{1,0:T(8,128)S(1)}, f32[384,256]{1,0:T(8,...) custom-call(s32[3]{0:T(128)S(1)} %pad_add_fusion.ids, ...), custom_call_target="tpu_custom_call" | custom-call | flops 1 | bytes 1 | tf_op jit(solution)/shard_map/rows/pallas_call | solution.py:43
  75.3 5.2 %collective-permute-done.19.refs_7_.c2 = f32[256,256]{1,0:T(8,128)S(1)} collective-permute-done((f32[256,256]{1,0:T(8,128)S(1)}, f32[256,256]{1,0:T(8,128)S(1)}, u32[]{:S(2)}, u32[]{:S(2)}) %collective-permute-start.19) | collective-permute-done | bytes 262176 | tf_op jit(solution)/shard_map/ppermute | solution.py:322
  84.0 3.2 %collective-permute-start.23 = (f32[256,256]{1,0:T(8,128)S(1)}, f32[256,256]{1,0:T(8,128)S(1)}, u32[]{:S(2)}, u32[]{:S(2)}) collective-permute-start(f32[256,256]{1,0:T(8,128)S(1)} %get-tuple-element.155), channel_id=1, source_target_pairs={{0,6},{1,7},{2,4},{3,5},{4,2},{5,3},{6,0},{7,1},{8,14},{9,15},{10,... | collective-permute-start | bytes 786440 | tf_op jit(solution)/shard_map/ppermute | solution.py:322
  87.2 16.8 %collective-permute-done.22.refs_2_ = f32[256,256]{1,0:T(8,128)S(1)} collective-permute-done((f32[256,256]{1,0:T(8,128)S(1)}, f32[256,256]{1,0:T(8,128)S(1)}, u32[]{:S(2)}, u32[]{:S(2)}) %collective-permute-start.22) | collective-permute-done | bytes 262176 | tf_op jit(solution)/shard_map/ppermute | solution.py:322
  104.8 8.1 %collective-permute-start.28 = (f32[256,256]{1,0:T(8,128)S(1)}, f32[256,256]{1,0:T(8,128)S(1)}, u32[]{:S(2)}, u32[]{:S(2)}) collective-permute-start(f32[256,256]{1,0:T(8,128)S(1)} %get-tuple-element.164), channel_id=1, source_target_pairs={{0,2},{1,3},{2,0},{3,1},{4,6},{5,7},{6,4},{7,5},{8,10},{9,11},{10,... | collective-permute-start | bytes 786440 | tf_op jit(solution)/shard_map/ppermute | solution.py:322
  114.8 2.5 %collective-permute-start.29 = (f32[128,256]{1,0:T(8,128)S(1)}, f32[128,256]{1,0:T(8,128)S(1)}, u32[]{:S(2)}, u32[]{:S(2)}) collective-permute-start(f32[128,256]{1,0:T(8,128)S(1)} %slice.30), channel_id=1, source_target_pairs={{0,2},{1,3},{2,0},{3,1},{4,6},{5,7},{6,4},{7,5},{8,10},{9,11},{10,... | collective-permute-start | bytes 393224 | tf_op jit(solution)/shard_map/ppermute | solution.py:322
  117.3 7.5 %collective-permute-done.31 = f32[128,256]{1,0:T(8,128)S(1)} collective-permute-done((f32[128,256]{1,0:T(8,128)S(1)}, f32[128,256]{1,0:T(8,128)S(1)}, u32[]{:S(2)}, u32[]{:S(2)}) %collective-permute-start.31) | collective-permute-done | bytes 131104 | tf_op jit(solution)/shard_map/ppermute | solution.py:322
  124.8 5.4 %collective-permute-done.30 = f32[128,256]{1,0:T(8,128)S(1)} collective-permute-done((f32[128,256]{1,0:T(8,128)S(1)}, f32[128,256]{1,0:T(8,128)S(1)}, u32[]{:S(2)}, u32[]{:S(2)}) %collective-permute-start.30) | collective-permute-done | bytes 131104 | tf_op jit(solution)/shard_map/ppermute | solution.py:322
  131.8 3.3 %collective-permute-start.36 = (f32[128,256]{1,0:T(8,128)S(1)}, f32[128,256]{1,0:T(8,128)S(1)}, u32[]{:S(2)}, u32[]{:S(2)}) collective-permute-start(f32[128,256]{1,0:T(8,128)S(1)} %add_add_fusion.1), channel_id=1, source_target_pairs={{0,24},{1,25},{2,26},{3,27},{4,28},{5,29},{6,30},{7,31},{8,16},{9,... | collective-permute-start | bytes 393224 | tf_op jit(solution)/shard_map/ppermute | solution.py:322
  136.2 2.8 %collective-permute-done.36 = f32[128,256]{1,0:T(8,128)S(1)} collective-permute-done((f32[128,256]{1,0:T(8,128)S(1)}, f32[128,256]{1,0:T(8,128)S(1)}, u32[]{:S(2)}, u32[]{:S(2)}) %collective-permute-start.36) | collective-permute-done | bytes 131104 | tf_op jit(solution)/shard_map/ppermute | solution.py:322
  139.0 2.6 %collective-permute-done.35 = f32[128,256]{1,0:T(8,128)S(1)} collective-permute-done((f32[128,256]{1,0:T(8,128)S(1)}, f32[128,256]{1,0:T(8,128)S(1)}, u32[]{:S(2)}, u32[]{:S(2)}) %collective-permute-start.35) | collective-permute-done | bytes 131104 | tf_op jit(solution)/shard_map/ppermute | solution.py:322
  145.5 5.0 %end.1.refs_0_ = f32[256,256]{1,0:T(8,128)S(1)} custom-call(s32[3]{0:T(128)S(1)} %pad_add_fusion.ids, f32[256,256]{1,0:T(8,128)S(1)} %get-tuple-element.173.total, f32[512,256]{1,0:T(8,128)S(1)} %get-tuple-element.174.solved, f32[512,256]{1,0:T(8,128)S(1)} %collective-permute-done.32.second, f32[256,256]{1,0:T(8,128)S(1)} %select_select_fusion.refs_5_.c0, ...), custom_call_target="tpu_custom_call" | custom-call | flops 1 | bytes 1 | tf_op jit(solution)/shard_map/end/pallas_call | solution.py:43
  151.0 4.0 %collective-permute-start.39 = (f32[256,256]{1,0:T(8,128)S(1)}, f32[256,256]{1,0:T(8,128)S(1)}, u32[]{:S(2)}, u32[]{:S(2)}) collective-permute-start(f32[256,256]{1,0:T(8,128)S(1)} %end.1.refs_0_), channel_id=1, source_target_pairs={{0,2},{1,3},{2,0},{3,1},{4,6},{5,7},{6,4},{7,5},{8,10},{9,11},{10,... | collective-permute-start | bytes 786440 | tf_op jit(solution)/shard_map/ppermute | solution.py:322
  155.0 6.7 %collective-permute-done.41.refs_3_ = f32[256,256]{1,0:T(8,128)S(1)} collective-permute-done((f32[256,256]{1,0:T(8,128)S(1)}, f32[256,256]{1,0:T(8,128)S(1)}, u32[]{:S(2)}, u32[]{:S(2)}) %collective-permute-start.41) | collective-permute-done | bytes 262176 | tf_op jit(solution)/shard_map/ppermute | solution.py:322
  161.7 12.5 %collective-permute-done.40.refs_2_ = f32[256,256]{1,0:T(8,128)S(1)} collective-permute-done((f32[256,256]{1,0:T(8,128)S(1)}, f32[256,256]{1,0:T(8,128)S(1)}, u32[]{:S(2)}, u32[]{:S(2)}) %collective-permute-start.40) | collective-permute-done | bytes 262176 | tf_op jit(solution)/shard_map/ppermute | solution.py:322
  (111 shorter events, 52.8 us)
Async XLA Ops:
  7.8 11.7 %collective-permute-start.6 = (f32[256,256]{1,0:T(8,128)}, f32[256,256]{1,0:T(8,128)}, u32[]{:S(2)}, u32[]{:S(2)}) collective-permute-start(f32[256,256]{1,0:T(8,128)} %get-tuple-element.113), channel_id=1, source_target_pairs={{0,2},{1,3},{8,10},{9,11},{16,18},{17,19},{24,26},{25,27}} | collective-permute-start | bytes 786440 | tf_op jit(solution)/shard_map/ppermute | solution.py:322
  9.8 14.1 %collective-permute-start.3 = (f32[256,256]{1,0:T(8,128)S(1)}, f32[256,256]{1,0:T(8,128)}, u32[]{:S(2)}, u32[]{:S(2)}) collective-permute-start(f32[256,256]{1,0:T(8,128)S(1)} %get-tuple-element.117), channel_id=1, source_target_pairs={{0,2},{1,3},{8,10},{9,11},{16,18},{17,19},{24,26},{25,27}} | collective-permute-start | bytes 786440 | tf_op jit(solution)/shard_map/ppermute | solution.py:322
  19.5 16.7 %collective-permute-start.7 = (f32[256,256]{1,0:T(8,128)}, f32[256,256]{1,0:T(8,128)}, u32[]{:S(2)}, u32[]{:S(2)}) collective-permute-start(f32[256,256]{1,0:T(8,128)} %collective-permute-done.6), channel_id=1, source_target_pairs={{2,4},{3,5},{10,12},{11,13},{18,20},{19,21},{26,28},{27,29}} | collective-permute-start | bytes 786440 | tf_op jit(solution)/shard_map/ppermute | solution.py:322
  23.8 13.0 %collective-permute-start.9 = (f32[256,256]{1,0:T(8,128)}, f32[256,256]{1,0:T(8,128)}, u32[]{:S(2)}, u32[]{:S(2)}) collective-permute-start(f32[256,256]{1,0:T(8,128)} %collective-permute-done.3), channel_id=1, source_target_pairs={{2,4},{3,5},{10,12},{11,13},{18,20},{19,21},{26,28},{27,29}} | collective-permute-start | bytes 786440 | tf_op jit(solution)/shard_map/ppermute | solution.py:322
  25.2 12.3 %collective-permute-start.2 = (f32[256,256]{1,0:T(8,128)}, f32[256,256]{1,0:T(8,128)}, u32[]{:S(2)}, u32[]{:S(2)}) collective-permute-start(f32[256,256]{1,0:T(8,128)} %collective-permute-done.1), channel_id=1, source_target_pairs={{4,6},{5,7},{12,14},{13,15},{20,22},{21,23},{28,30},{29,31}} | collective-permute-start | bytes 786440 | tf_op jit(solution)/shard_map/ppermute | solution.py:322
  26.6 14.8 %collective-permute-start.5 = (f32[512,256]{1,0:T(8,128)S(1)}, f32[512,256]{1,0:T(8,128)}, u32[]{:S(2)}, u32[]{:S(2)}) collective-permute-start(f32[512,256]{1,0:T(8,128)S(1)} %pad_maximum_fusion.blocks), channel_id=1, source_target_pairs={{0,8},{1,9},{8,0},{9,1}} | collective-permute-start | bytes 1572872 | tf_op jit(solution)/shard_map/ppermute | solution.py:322
  48.8 14.1 %collective-permute-start.13 = (f32[256,256]{1,0:T(8,128)S(1)}, f32[256,256]{1,0:T(8,128)S(1)}, u32[]{:S(2)}, u32[]{:S(2)}) collective-permute-start(f32[256,256]{1,0:T(8,128)S(1)} %get-tuple-element.130.refs_0_), channel_id=1, source_target_pairs={{0,16},{1,17},{2,18},{3,19},{4,20},{5,21},{6,22},{7,23},{8,24},{9,... | collective-permute-start | bytes 786440 | tf_op jit(solution)/shard_map/ppermute | solution.py:322
  50.4 12.5 %collective-permute-start.12 = (f32[256,256]{1,0:T(8,128)S(1)}, f32[256,256]{1,0:T(8,128)S(1)}, u32[]{:S(2)}, u32[]{:S(2)}) collective-permute-start(f32[256,256]{1,0:T(8,128)S(1)} %get-tuple-element.130.refs_0_), channel_id=1, source_target_pairs={{0,8},{1,9},{2,10},{3,11},{4,12},{5,13},{6,14},{7,15},{8,0},{9,1},... | collective-permute-start | bytes 786440 | tf_op jit(solution)/shard_map/ppermute | solution.py:322
  66.6 13.9 %collective-permute-start.19 = (f32[256,256]{1,0:T(8,128)S(1)}, f32[256,256]{1,0:T(8,128)S(1)}, u32[]{:S(2)}, u32[]{:S(2)}) collective-permute-start(f32[256,256]{1,0:T(8,128)S(1)} %select_select_fusion.refs_5_.c0), channel_id=1, source_target_pairs={{0,16},{1,17},{2,18},{3,19},{4,20},{5,21},{6,22},{7,23},{8,24},{9,... | collective-permute-start | bytes 786440 | tf_op jit(solution)/shard_map/ppermute | solution.py:322
  68.0 12.4 %collective-permute-start.18 = (f32[256,256]{1,0:T(8,128)S(1)}, f32[256,256]{1,0:T(8,128)S(1)}, u32[]{:S(2)}, u32[]{:S(2)}) collective-permute-start(f32[256,256]{1,0:T(8,128)S(1)} %select_select_fusion.refs_5_.c0), channel_id=1, source_target_pairs={{0,8},{1,9},{2,10},{3,11},{4,12},{5,13},{6,14},{7,15},{8,0},{9,1},... | collective-permute-start | bytes 786440 | tf_op jit(solution)/shard_map/ppermute | solution.py:322
  80.4 23.5 %collective-permute-start.24 = (f32[384,256]{1,0:T(8,128)S(1)}, f32[384,256]{1,0:T(8,128)S(1)}, u32[]{:S(2)}, u32[]{:S(2)}) collective-permute-start(f32[384,256]{1,0:T(8,128)S(1)} %get-tuple-element.157), channel_id=1, source_target_pairs={{0,8},{1,9},{2,10},{3,11},{4,12},{5,13},{6,14},{7,15},{8,0},{9,1},... | collective-permute-start | bytes 1179656 | tf_op jit(solution)/shard_map/ppermute | solution.py:322
  81.8 22.2 %collective-permute-start.25 = (f32[384,256]{1,0:T(8,128)S(1)}, f32[384,256]{1,0:T(8,128)S(1)}, u32[]{:S(2)}, u32[]{:S(2)}) collective-permute-start(f32[384,256]{1,0:T(8,128)S(1)} %get-tuple-element.158), channel_id=1, source_target_pairs={{0,16},{1,17},{2,18},{3,19},{4,20},{5,21},{6,22},{7,23},{8,24},{9,... | collective-permute-start | bytes 1179656 | tf_op jit(solution)/shard_map/ppermute | solution.py:322
  82.4 21.6 %collective-permute-start.26 = (f32[384,256]{1,0:T(8,128)S(1)}, f32[384,256]{1,0:T(8,128)S(1)}, u32[]{:S(2)}, u32[]{:S(2)}) collective-permute-start(f32[384,256]{1,0:T(8,128)S(1)} %get-tuple-element.159), channel_id=1, source_target_pairs={{0,24},{1,25},{2,26},{3,27},{4,28},{5,29},{6,30},{7,31},{8,16},{9,... | collective-permute-start | bytes 1179656 | tf_op jit(solution)/shard_map/ppermute | solution.py:322
  83.9 20.0 %collective-permute-start.22 = (f32[256,256]{1,0:T(8,128)S(1)}, f32[256,256]{1,0:T(8,128)S(1)}, u32[]{:S(2)}, u32[]{:S(2)}) collective-permute-start(f32[256,256]{1,0:T(8,128)S(1)} %get-tuple-element.154), channel_id=1, source_target_pairs={{0,4},{1,5},{2,6},{3,7},{4,0},{5,1},{6,2},{7,3},{8,12},{9,13},{10,... | collective-permute-start | bytes 786440 | tf_op jit(solution)/shard_map/ppermute | solution.py:322
  84.0 20.0 %collective-permute-start.23 = (f32[256,256]{1,0:T(8,128)S(1)}, f32[256,256]{1,0:T(8,128)S(1)}, u32[]{:S(2)}, u32[]{:S(2)}) collective-permute-start(f32[256,256]{1,0:T(8,128)S(1)} %get-tuple-element.155), channel_id=1, source_target_pairs={{0,6},{1,7},{2,4},{3,5},{4,2},{5,3},{6,0},{7,1},{8,14},{9,15},{10,... | collective-permute-start | bytes 786440 | tf_op jit(solution)/shard_map/ppermute | solution.py:322
  104.1 26.1 %collective-permute-start.27 = (f32[256,256]{1,0:T(8,128)S(1)}, f32[256,256]{1,0:T(8,128)S(1)}, u32[]{:S(2)}, u32[]{:S(2)}) collective-permute-start(f32[256,256]{1,0:T(8,128)S(1)} %slice.29), channel_id=1, source_target_pairs={{0,0},{1,1},{2,20},{3,21},{4,2},{5,3},{6,22},{7,23},{8,8},{9,9},{1... | collective-permute-start | bytes 786440 | tf_op jit(solution)/shard_map/ppermute | solution.py:322
  104.8 25.4 %collective-permute-start.28 = (f32[256,256]{1,0:T(8,128)S(1)}, f32[256,256]{1,0:T(8,128)S(1)}, u32[]{:S(2)}, u32[]{:S(2)}) collective-permute-start(f32[256,256]{1,0:T(8,128)S(1)} %get-tuple-element.164), channel_id=1, source_target_pairs={{0,2},{1,3},{2,0},{3,1},{4,6},{5,7},{6,4},{7,5},{8,10},{9,11},{10,... | collective-permute-start | bytes 786440 | tf_op jit(solution)/shard_map/ppermute | solution.py:322
  112.9 11.9 %collective-permute-start.31 = (f32[128,256]{1,0:T(8,128)S(1)}, f32[128,256]{1,0:T(8,128)S(1)}, u32[]{:S(2)}, u32[]{:S(2)}) collective-permute-start(f32[128,256]{1,0:T(8,128)S(1)} %slice.30), channel_id=1, source_target_pairs={{0,6},{1,7},{2,4},{3,5},{4,2},{5,3},{6,0},{7,1},{8,14},{9,15},{10,... | collective-permute-start | bytes 393224 | tf_op jit(solution)/shard_map/ppermute | solution.py:322
  114.8 15.4 %collective-permute-start.30 = (f32[128,256]{1,0:T(8,128)S(1)}, f32[128,256]{1,0:T(8,128)S(1)}, u32[]{:S(2)}, u32[]{:S(2)}) collective-permute-start(f32[128,256]{1,0:T(8,128)S(1)} %slice.30), channel_id=1, source_target_pairs={{0,4},{1,5},{2,6},{3,7},{4,0},{5,1},{6,2},{7,3},{8,12},{9,13},{10,... | collective-permute-start | bytes 393224 | tf_op jit(solution)/shard_map/ppermute | solution.py:322
  114.8 15.4 %collective-permute-start.29 = (f32[128,256]{1,0:T(8,128)S(1)}, f32[128,256]{1,0:T(8,128)S(1)}, u32[]{:S(2)}, u32[]{:S(2)}) collective-permute-start(f32[128,256]{1,0:T(8,128)S(1)} %slice.30), channel_id=1, source_target_pairs={{0,2},{1,3},{2,0},{3,1},{4,6},{5,7},{6,4},{7,5},{8,10},{9,11},{10,... | collective-permute-start | bytes 393224 | tf_op jit(solution)/shard_map/ppermute | solution.py:322
  150.6 23.5 %collective-permute-start.40 = (f32[256,256]{1,0:T(8,128)S(1)}, f32[256,256]{1,0:T(8,128)S(1)}, u32[]{:S(2)}, u32[]{:S(2)}) collective-permute-start(f32[256,256]{1,0:T(8,128)S(1)} %end.1.refs_0_), channel_id=1, source_target_pairs={{0,4},{1,5},{2,6},{3,7},{4,0},{5,1},{6,2},{7,3},{8,12},{9,13},{10,... | collective-permute-start | bytes 786440 | tf_op jit(solution)/shard_map/ppermute | solution.py:322
  151.0 23.2 %collective-permute-start.39 = (f32[256,256]{1,0:T(8,128)S(1)}, f32[256,256]{1,0:T(8,128)S(1)}, u32[]{:S(2)}, u32[]{:S(2)}) collective-permute-start(f32[256,256]{1,0:T(8,128)S(1)} %end.1.refs_0_), channel_id=1, source_target_pairs={{0,2},{1,3},{2,0},{3,1},{4,6},{5,7},{6,4},{7,5},{8,10},{9,11},{10,... | collective-permute-start | bytes 786440 | tf_op jit(solution)/shard_map/ppermute | solution.py:322
  155.0 19.7 %collective-permute-start.42 = (f32[256,256]{1,0:T(8,128)S(1)}, f32[256,256]{1,0:T(8,128)S(1)}, u32[]{:S(2)}, u32[]{:S(2)}) collective-permute-start(f32[256,256]{1,0:T(8,128)S(1)} %end.1.refs_0_), channel_id=1, source_target_pairs={{0,1},{1,0},{2,3},{3,2},{4,5},{5,4},{6,7},{7,6},{8,9},{9,8},{10,11... | collective-permute-start | bytes 786440 | tf_op jit(solution)/shard_map/ppermute | solution.py:322
  161.7 13.0 %collective-permute-start.45 = (f32[256,256]{1,0:T(8,128)S(1)}, f32[256,256]{1,0:T(8,128)S(1)}, u32[]{:S(2)}, u32[]{:S(2)}) collective-permute-start(f32[256,256]{1,0:T(8,128)S(1)} %collective-permute-done.41.refs_3_), channel_id=1, source_target_pairs={{0,1},{1,0},{2,3},{3,2},{4,5},{5,4},{6,7},{7,6},{8,9},{9,8},{10,11... | collective-permute-start | bytes 786440 | tf_op jit(solution)/shard_map/ppermute | solution.py:322
  (31 other events, 252.4 us)

commit v3 on v2

--- a/solution.py
+++ b/solution.py
@@ -144,14 +144,11 @@
         targets[d][...] = sums[jnp.where(target // 2 == ids[PAIR] % 2, 0, 2) + target % 2]
 
 
-def row_kernel(n_pairs, n_rows, ids, low_1, low_2, high_1, high_2, *refs):
-    held, (turned, turned_other, adjoint, low), columns = refs[:4], refs[4:8], refs[8:12]
-    shares, slices = refs[12 : 12 + n_pairs], refs[12 + n_pairs : 12 + n_pairs + n_rows]
-    remaining, sums = refs[-2:]
+def row_kernel(n_pairs, ids, low_1, low_2, high_1, high_2, v0, v1, v2, v3, adjoint, *refs):
+    shares, product_ref, remaining = refs[:n_pairs], refs[-2], refs[-1]
     pair, row = ids[PAIR], ids[ROW]
     x_is_0 = row % 2 == 0
     near = row // 2 == pair % 2
-    first = ids[LANE] == 0
 
     def panel(same, across):
         return split(
@@ -160,11 +157,9 @@
             )
         )
 
-    v0, v1, v2, v3 = [ref[...] for ref in held]
+    v0, v1, v2, v3 = [ref[...] for ref in (v0, v1, v2, v3)]
     panel_low = panel(jnp.where(near, v0, v2), jnp.where(near, v1, v3))
     panel_high = panel(jnp.where(near, v2, v0), jnp.where(near, v3, v1))
-    own = jnp.zeros((NB, NB), jnp.float32)
-    other = jnp.zeros((NB, NB), jnp.float32)
     for block in range(n_pairs):
         at = slice(block * NB, (block + 1) * NB)
         product = dot3((low_1[at, :], low_2[at, :]), panel_low)
@@ -172,12 +167,21 @@
             upper = slice((block - n_pairs // 2) * NB, (block - n_pairs // 2 + 1) * NB)
             product += dot3((high_1[upper, :], high_2[upper, :]), panel_high)
         remaining[block] = jnp.where(pair == 0, adjoint[at, :NB], 0.0) - product
-        product = split(product)
+        product_ref[at, :] = product
+    for d in range(n_pairs):
+        shares[d][...] = remaining[pair ^ d]
+
+
+def sum_kernel(n_rows, ids, turned, turned_other, product_ref, low, *refs):
+    slices, sums = refs[:-1], refs[-1]
+    first, first_pair = ids[LANE] == 0, ids[PAIR] == 0
+    own = jnp.zeros((NB, NB), jnp.float32)
+    other = jnp.zeros((NB, NB), jnp.float32)
+    for block in range(turned.shape[1] // NB):
+        at = slice(block * NB, (block + 1) * NB)
+        product = split(product_ref[at, :])
         own += dot3(split(turned[:, at]), product)
         other += dot3(split(turned_other[:, at]), product)
-    for d in range(n_pairs):
-        shares[d][...] = remaining[pair ^ d]
-    first_pair = pair == 0
     own_term = jnp.where(first, low[:, :NB], low[:, NB:])
     own_term = jnp.where(first_pair, own_term, 0.0)
     cross_term = jnp.where(first_pair, low[:, NB:], 0.0)
@@ -189,22 +193,14 @@
         sums[index] = own_sum[at]
         sums[index + n_rows // 2] = other_sum[at]
     for d in range(n_rows):
-        slices[d][:NB, :] = columns[d][...]
-        slices[d][NB:, :] = sums[row ^ d]
-
-
-def by_row(row, values):
-    result = values[3]
-    for index in (2, 1, 0):
-        result = jnp.where(row == index, values[index], result)
-    return result
+        slices[d][...] = sums[ids[ROW] ^ d]
 
 
 def carried_blocks(ids, refs):
-    values = [ref[...] for ref in refs]
-    top = by_row(ids[ROW], values)
-    link = by_row(ids[ROW], [values[1], values[0], values[3], values[2]])
-    return jnp.where(ids[LANE] == 0, top, link), link
+    same, other = [ref[...] for ref in refs]
+    even = ids[ROW] % 2 == 0
+    link = jnp.where(even, other, same)
+    return jnp.where(ids[LANE] == 0, jnp.where(even, same, other), link), link
 
 
 def solve_kernel(n_pairs, ids, *refs):
@@ -216,21 +212,14 @@
     total = total - owned[...].T
     inverse, _ = carried_blocks(ids, carried)
     total_ref[...] = total
-    solved[:NB, :] = quick(total, inverse)
-    solved[NB:, :] = inverse
-
-
-def end_kernel(ids, total, solved, second, c0, c1, c2, c3, blocks, across, blocks_other, across_other, sums_ref, sums_other, out_ref):
+    solved[...] = quick(total, inverse)
+
+
+def lead_kernel(ids, c0, c1, c0_other, c1_other, blocks, across, blocks_other, across_other, sums_ref, sums_other, out_ref):
     row, first = ids[ROW], ids[LANE] == 0
-    leading = (ids[PAIR] == 0) & (row < 2)
-
-    @pl.when(jnp.logical_not(leading))
-    def _():
-        inverse, link = carried_blocks(ids, (c0, c1, c2, c3))
-        whole = quick(total[...] - quick(second[:NB, :], link), inverse)
-        out_ref[...] = jnp.where(first, whole, solved[:NB, :])
-
-    @pl.when(leading)
+    own, other = (c0, c1), (c0_other, c1_other)
+
+    @pl.when((ids[PAIR] == 0) & (row < 2))
     def _():
         rows, cols = positions()
         in_first_row = row == 0
@@ -256,7 +245,8 @@
         mine, theirs = held(blocks, blocks_other), held(across, across_other)
         l0, a00, _, _ = [jnp.where(in_first_row, a, b) for a, b in zip(mine, theirs)]
         link, a10, l1, a11 = [jnp.where(in_first_row, b, a) for a, b in zip(mine, theirs)]
-        inv0, inv1 = by_lane(solved[NB:, :], second[NB:, :])
+        inv0, _ = by_lane(*[jnp.where(in_first_row, x[...], y[...]) for x, y in (own, other)])
+        _, inv1 = by_lane(*[jnp.where(in_first_row, y[...], x[...]) for x, y in (own, other)])
 
         def ordered(ref):
             value = ref[...]
@@ -280,6 +270,13 @@
         )
 
 
+def end_kernel(ids, total, solved, second, c0, c1, lead, out_ref):
+    inverse, link = carried_blocks(ids, (c0, c1))
+    whole = quick(total[...] - quick(second[...], link), inverse)
+    whole = jnp.where(ids[LANE] == 0, whole, solved[...])
+    out_ref[...] = jnp.where((ids[PAIR] == 0) & (ids[ROW] < 2), lead[...], whole)
+
+
 def place_kernel(n_pairs, ids, *refs):
     own, other, out_ref = refs[:n_pairs], refs[n_pairs:-1], refs[-1]
     first = ids[LANE] == 0
@@ -369,18 +366,22 @@
     every, nearest = range(1, n_pairs), range(1, middle)
     arrived_3, arrived_1, arrived_2 = [travel(panel[i], every) for i in (3, 1, 2)]
     arrived_0 = travel(leading_piece, nearest)
+    carried = [x[:NB] for x in arrived_0]
+    carried = carried + travel(carried[-1], range(middle, n_pairs - 1))[1:]
     high = swap_rows(chosen(arrived_2, arrived_3), 2)
-    high, across, blocks, *rest = together(high, across, blocks, *arrived_3, *arrived_1, *arrived_2, *arrived_0)
+    high, across, blocks, *rest = together(
+        high, across, blocks, *arrived_3, *arrived_1, *arrived_2, *arrived_0, *carried
+    )
     arrived_3, rest = rest[:n_pairs], rest[n_pairs:]
     arrived_1, rest = rest[:n_pairs], rest[n_pairs:]
-    arrived_2, arrived_0 = rest[:n_pairs], rest[n_pairs:]
+    arrived_2, rest = rest[:n_pairs], rest[n_pairs:]
+    arrived_0, carried = rest[:middle], rest[middle:]
 
     masked_0 = [jnp.where(trailing, x, 0.0) for x in arrived_0]
     low = chosen(masked_0, arrived_1)
     held = jnp.where(near, low, high)
     held = [held] + [swap_rows(held, d) for d in range(1, n_rows)]
-    carried = [x[:NB] for x in arrived_0]
-    carried = carried + travel(carried[-1], range(middle, n_pairs))[1:]
+    carried.append(hop(carried[-1], n_pairs - 1))
     columns = jax.ShapeDtypeStruct((local_rows, 2 * NB), jnp.bfloat16)
     half_columns = jax.ShapeDtypeStruct((local_rows // 2, 2 * NB), jnp.bfloat16)
     masked = call(
@@ -392,9 +393,6 @@
         swap(after(adjoint, high)),
     )
     pieces = here(masked_0), here(arrived_1), here(arrived_2), here(arrived_3)
-    rest = together(*held, *masked, *pieces, *carried)
-    held, masked, pieces, carried = rest[:4], rest[4:8], rest[8:12], here(rest[12:])
-
     turned, low, *block_sums = call(
         functools.partial(column_kernel, n_rows),
         "columns",
@@ -409,87 +407,136 @@
         scratch=(pltpu.VMEM((4, NB, NB), jnp.float32),),
     )
 
+    rest = together(*held, turned, low, *block_sums, *carried)
+    held, (turned, low), rest = rest[:n_rows], rest[n_rows : n_rows + 2], rest[n_rows + 2 :]
+    block_sums, carried = rest[:n_rows], here(rest[n_rows:])
+    turned_other, blocks_other, across_other = swap(turned), swap(blocks), swap(across)
+
     height = 2 * NB // n_rows
-    rows = call(
-        functools.partial(row_kernel, n_pairs, n_rows),
+    *shares, product = call(
+        functools.partial(row_kernel, n_pairs),
         "rows",
-        (SQUARE,) * n_pairs
-        + (jax.ShapeDtypeStruct((NB + height, NB), jnp.float32),) * n_rows,
+        (SQUARE,) * n_pairs + (jax.ShapeDtypeStruct((local_rows, NB), jnp.float32),),
         ids,
         *masked,
         *held,
+        adjoint,
+        scratch=(pltpu.VMEM((n_pairs, NB, NB), jnp.float32),),
+    )
+    slices = call(
+        functools.partial(sum_kernel, n_rows),
+        "sums",
+        (jax.ShapeDtypeStruct((height, NB), jnp.float32),) * n_rows,
+        ids,
         turned,
-        swap(turned),
-        adjoint,
+        turned_other,
+        product,
         low,
-        *block_sums,
-        scratch=(
-            pltpu.VMEM((n_pairs, NB, NB), jnp.float32),
-            pltpu.VMEM((n_rows, height, NB), jnp.float32),
-        ),
-    )
-    carried = [carried] + [swap_rows(carried, d) for d in range(1, n_rows)]
-    rest = together(*carried, *rows)
-    carried, rows = rest[:n_rows], rest[n_rows:]
-    shares, slices = rows[:n_pairs], rows[n_pairs:]
-
-    farther_shares = [swap_pairs(shares[d], d) for d in range(2, n_pairs)]
+        scratch=(pltpu.VMEM((n_rows, height, NB), jnp.float32),),
+    )
+    rest = together(blocks_other, across_other, carried, *slices, *shares, *block_sums)
+    (blocks_other, across_other, carried), rest = rest[:3], rest[3:]
+    slices, shares, block_sums = (
+        rest[:n_rows],
+        rest[n_rows : n_rows + n_pairs],
+        rest[n_rows + n_pairs :],
+    )
+
+    def folded(values, bit):
+        kept = {d: value for d, value in values.items() if not d & bit}
+        moved = {d: swap_pairs(value, bit) for d, value in values.items() if d & bit}
+        return kept, moved
+
+    def added(kept, moved, bit):
+        return {d: value + moved[d ^ bit] for d, value in kept.items()}
+
+    nearest_share, shares = shares[1], {d: x for d, x in enumerate(shares) if d != 1}
+    kept, moved = folded(shares, 1)
     slices = [slices[0]] + [swap_rows(slices[d], d) for d in range(1, n_rows)]
-    next_share, *rest = together(shares[1], *farther_shares, *slices)
-    farther_shares, slices = rest[: n_pairs - 2], rest[n_pairs - 2 :]
-    slices = sum(slices[1:], slices[0])
+    carried = jnp.where(row_id < 2, carried, swap_rows(carried, 2))
+    rest = together(
+        carried, nearest_share, *block_sums, *slices, *kept.values(), *moved.values()
+    )
+    (carried, nearest_share), rest = rest[:2], rest[2:]
+    block_sums, rest = rest[:n_rows], rest[n_rows:]
+    total, rest = sum(rest[1:n_rows], rest[0]), rest[n_rows:]
+    kept, moved = dict(zip(kept, rest)), dict(zip(moved, rest[len(kept) :]))
+    own_share = kept.pop(0)
+    shares = added(kept, moved, 1)
+    bit = 2
+    while bit < n_pairs // 2:
+        shares[0] = jnp.zeros_like(own_share)
+        shares = added(*folded(shares, bit), bit)
+        own_share = own_share + shares.pop(0)
+        bit *= 2
+    moved = swap_pairs(shares[bit], bit)
+    total_other = swap_pairs(total, 1)
+    block_sums = [block_sums[0]] + [swap_rows(block_sums[d], d) for d in range(1, n_rows)]
+    rest = together(own_share, moved, nearest_share, carried, total, total_other, *block_sums)
+    own_share, moved, nearest_share, carried, total, total_other = rest[:6]
+    total, owned = total + total_other, sum(rest[7:], rest[6])
 
     def owner(r, p, k):
         half = 0 if r // 2 == p % 2 else 1
         return p % 2 * 2 + r % 2, p // 2 + half * (n_pairs // 2), k
 
-    owned = send(slices[:NB], owner)
-    total = slices[NB:]
-    totals = [total] + [swap_pairs(total, d) for d in range(1, n_pairs)]
-    next_share = swap_pairs(next_share, 1)
-    owned, next_share, *totals = together(owned, next_share, *totals)
-    shares = [shares[0], next_share, *farther_shares]
+    owned = send(owned, owner)
+    bit = 2
+    while bit < n_pairs:
+        total = total + swap_pairs(total, bit)
+        bit *= 2
+    carried = [carried, swap_rows(carried, 1)]
+    nearest_share = swap_pairs(nearest_share, 1)
+    owned, total, nearest_share, *carried = together(owned, total, nearest_share, *carried)
+    shares = own_share, moved, nearest_share
 
     mine, solved = call(
-        functools.partial(solve_kernel, n_pairs),
-        "solve",
-        (SQUARE, jax.ShapeDtypeStruct((2 * NB, NB), jnp.float32)),
-        ids,
-        *shares,
-        owned,
-        *carried,
-    )
-    total = sum(totals[1:], totals[0])
+        functools.partial(solve_kernel, 3), "solve", (SQUARE, SQUARE), ids, *shares, owned, *carried
+    )
     sums = [total] + [swap_rows(total, d) for d in range(1, n_rows)]
-    second = swap(solved)
-    blocks_other = swap(after(blocks, solved))
-    second, blocks_other, *sums = together(second, blocks_other, *sums)
-    across_other = swap(after(across, second))
-    sums = jnp.concatenate(sums, 0)
-    result = call(
-        end_kernel,
-        "end",
+    second, *rest = together(swap(solved), *[swap(x) for x in carried], *sums)
+    carried_other, sums = rest[:2], jnp.concatenate(rest[2:], 0)
+    sums_other = swap(sums)
+    lead = call(
+        lead_kernel,
+        "lead",
         SQUARE,
         ids,
-        mine,
-        solved,
-        second,
         *carried,
+        *carried_other,
         blocks,
         across,
         blocks_other,
         across_other,
         sums,
-        swap(sums),
-    )
-    results = [result] + [swap_pairs(result, d) for d in range(1, n_pairs)]
+        sums_other,
+    )
+    result = call(end_kernel, "end", SQUARE, ids, mine, solved, second, *carried, lead)
+    results, others, bit = {0: result}, {}, n_pairs // 2
+    while bit:
+        for d, value in list(results.items()):
+            results[d ^ bit] = swap_pairs(value, bit)
+        if bit == 2:
+            results[1] = swap_pairs(result, 1)
+            others[0] = swap(result)
+            names = sorted(results)
+            rest = together(others[0], *[results[d] for d in names])
+            others[0], results = rest[0], dict(zip(names, rest[1:]))
+            for d in names:
+                if d ^ 1 not in results:
+                    results[d ^ 1] = swap_pairs(results[d], 1)
+            break
+        bit //= 2
+    for d in range(n_pairs):
+        if d not in others:
+            others[d] = swap(results[d])
     return call(
         functools.partial(place_kernel, n_pairs),
         "place",
         jax.ShapeDtypeStruct((local_rows, 2 * NB), jnp.float32),
         ids,
-        *results,
-        *[swap(x) for x in results],
+        *[results[d] for d in range(n_pairs)],
+        *[others[d] for d in range(n_pairs)],
     )
 
 

time: 179 us -> 157 us (0.88)
  waiting for transfers between devices: 88.6 us -> 73.1 us
  starting transfers between devices: 60.4 us -> 54.9 us
    ppermute x46 -> x49, waiting for transfers between devices: 88.6 us -> 73.1 us  [send(): return lax.ppermute(value, ('row', 'col'), edges)]
    ppermute x46 -> x49, starting transfers between devices: 60.4 us -> 54.9 us  [send(): return lax.ppermute(value, ('row', 'col'), edges)]
    pallas_call x7 -> x9, Pallas kernels: 22.1 us -> 21.6 us  [call(): pl.pallas_call(kernel, out_shape=out_shape, in_specs=[pl.BlockSpec(memory...]
  transfers between devices with their start and end apart: 46 -> 49, of which waited for: 22 -> 16; matrix products, arithmetic and copies ran while one was open for 2% -> 2% of each run, Pallas kernels for 7% -> 9%
where the time goes in v3:
time: 157 us
  waiting for transfers between devices  73.1 us (47%)
  starting transfers between devices  54.9 us (35%)
  Pallas kernels  21.6 us (14%)
  other arithmetic  3.92 us (2%)
  local copies, waits for them, and re-layouts  3 us (2%)
    ppermute x49, waiting for transfers between devices, send(): return lax.ppermute(value, ('row', 'col'), edges)  73.1 us
    ppermute x49, starting transfers between devices, send(): return lax.ppermute(value, ('row', 'col'), edges)  54.9 us
    pallas_call x9, Pallas kernels, call(): pl.pallas_call(kernel, out_shape=out_shape, in_specs=[pl.BlockSpec(memory...  21.6 us
  transfers between devices with their start and end apart: 49, of which 16 were waited for; matrix products, arithmetic and copies ran while one was open for 2% of the time, Pallas kernels for 9%

profile of v3, /device:TPU:0, one launch (start us, length us, event | category | flops | bytes accessed | tf_op | source)
XLA Modules:
  0.0 157.0 jit_solution(15192175245572390686)
XLA Ops:
  1.5 5.6 %collective-permute-start = (f32[256,256]{1,0:T(8,128)S(1)}, f32[256,256]{1,0:T(8,128)}, u32[]{:S(2)}, u32[]{:S(2)}) collective-permute-start(f32[256,256]{1,0:T(8,128)S(1)} %get-tuple-element.146), channel_id=1, source_target_pairs={{0,2},{1,3},{8,10},{9,11},{16,18},{17,19},{24,26},{25,27}} | collective-permute-start | bytes 786440 | tf_op jit(solution)/shard_map/ppermute | solution.py:319
  7.1 2.0 %collective-permute-start.3 = (f32[256,256]{1,0:T(8,128)S(1)}, f32[256,256]{1,0:T(8,128)}, u32[]{:S(2)}, u32[]{:S(2)}) collective-permute-start(f32[256,256]{1,0:T(8,128)S(1)} %get-tuple-element.142), channel_id=1, source_target_pairs={{0,2},{1,3},{8,10},{9,11},{16,18},{17,19},{24,26},{25,27}} | collective-permute-start | bytes 786440 | tf_op jit(solution)/shard_map/ppermute | solution.py:319
  9.1 2.0 %collective-permute-start.6 = (f32[256,256]{1,0:T(8,128)S(1)}, f32[256,256]{1,0:T(8,128)}, u32[]{:S(2)}, u32[]{:S(2)}) collective-permute-start(f32[256,256]{1,0:T(8,128)S(1)} %get-tuple-element.138), channel_id=1, source_target_pairs={{0,2},{1,3},{8,10},{9,11},{16,18},{17,19},{24,26},{25,27}} | collective-permute-start | bytes 786440 | tf_op jit(solution)/shard_map/ppermute | solution.py:319
  14.5 4.6 %inverse.1 = f32[256,256]{1,0:T(8,128)S(1)} custom-call(s32[3]{0:T(128)S(1)} %pad_add_fusion.ids, f32[256,256]{1,0:T(8,128)S(1)} %get-tuple-element.124.block_ref), custom_call_target="tpu_custom_call" | custom-call | flops 1 | bytes 1 | tf_op jit(solution)/shard_map/inverse/pallas_call | solution.py:43
  27.1 3.4 %collective-permute-start.5 = (f32[512,256]{1,0:T(8,128)S(1)}, f32[512,256]{1,0:T(8,128)S(1)}, u32[]{:S(2)}, u32[]{:S(2)}) collective-permute-start(f32[512,256]{1,0:T(8,128)S(1)} %pad_maximum_fusion.blocks), channel_id=1, source_target_pairs={{0,8},{1,9},{8,0},{9,1}} | collective-permute-start | bytes 1572872 | tf_op jit(solution)/shard_map/ppermute | solution.py:319
  32.9 7.8 %collective-permute-done.5.across = f32[512,256]{1,0:T(8,128)S(1)} collective-permute-done((f32[512,256]{1,0:T(8,128)S(1)}, f32[512,256]{1,0:T(8,128)S(1)}, u32[]{:S(2)}, u32[]{:S(2)}) %collective-permute-start.5) | collective-permute-done | bytes 524320 | tf_op jit(solution)/shard_map/ppermute | solution.py:319
  48.2 2.5 %masked.1 = (bf16[1024,512]{1,0:T(8,128)(2,1)S(1)}, bf16[1024,512]{1,0:T(8,128)(2,1)S(1)}, bf16[512,512]{1,0:T(8,128)(2,1)S(1)}, bf16[512,512]{1,0:T(8,128)(2,1)S(1)}) custom-call(s32[3]{0:T(128)S(1)} %pad_add_fusion.ids, f32[1024,512]{1,0:T(8,128)S(1)} %copy-done, f32[1024,512]{1,0:T(8,128)} %collective-permute-done.18.other), custom_call_target="tpu_custom_call" | custom-call | flops 1 | bytes 1 | tf_op jit(solution)/shard_map/masked/pallas_call | solution.py:43
  50.7 2.1 %columns.1 = (f32[256,1024]{1,0:T(8,128)S(1)}, f32[256,512]{1,0:T(8,128)S(1)}, f32[256,256]{1,0:T(8,128)S(1)}, f32[256,256]{1,0:T(8,128)S(1)}, f32[256,256]{1,0:T(8,128)S(1)}, /*index=5*/f32[256,256]{1,0:T(8,128)S(1)}) custom-call(s32[3]{0:T(128)S(1)} %pad_add_fusion.ids, bf16[1024,512]{1,0:T(8,128)(2,1)S(1)} %get-tuple-element.133.low_1, ...), custom_call_target="tpu_custom_call" | custom-call | flops 1 | bytes 1 | tf_op jit(solution)/shard_map/columns/pallas_call | solution.py:43
  52.9 6.4 %collective-permute-done.16.v2 = f32[256,256]{1,0:T(8,128)S(1)} collective-permute-done((f32[256,256]{1,0:T(8,128)S(1)}, f32[256,256]{1,0:T(8,128)S(1)}, u32[]{:S(2)}, u32[]{:S(2)}) %collective-permute-start.16) | collective-permute-done | bytes 262176 | tf_op jit(solution)/shard_map/ppermute | solution.py:319
  59.9 2.1 %rows.1 = (f32[256,256]{1,0:T(8,128)S(1)}, f32[256,256]{1,0:T(8,128)S(1)}, f32[256,256]{1,0:T(8,128)S(1)}, f32[256,256]{1,0:T(8,128)S(1)}, f32[1024,256]{1,0:T(8,128)S(1)}) custom-call(s32[3]{0:T(128)S(1)} %pad_add_fusion.ids, bf16[1024,512]{1,0:T(8,128)(2,1)S(1)} %get-tuple-element.133.low_1, bf16[1024,512]{1,0:T(8,128)(2,1)S(1)} %get-tuple-element.134.low_2, ...), custom_call_target="tpu_custom_call" | custom-call | flops 1 | bytes 1 | tf_op jit(solution)/shard_map/rows/pallas_call | solution.py:43
  65.1 2.2 %collective-permute-start.25 = (f32[256,256]{1,0:T(8,128)S(1)}, f32[256,256]{1,0:T(8,128)S(1)}, u32[]{:S(2)}, u32[]{:S(2)}) collective-permute-start(f32[256,256]{1,0:T(8,128)S(1)} %get-tuple-element.191), channel_id=1, source_target_pairs={{0,2},{1,3},{2,0},{3,1},{4,6},{5,7},{6,4},{7,5},{8,10},{9,11},{10,... | collective-permute-start | bytes 786440 | tf_op jit(solution)/shard_map/ppermute | solution.py:319
  70.8 6.0 %collective-permute-done.21 = f32[256,256]{1,0:T(8,128)S(1)} collective-permute-done((f32[256,256]{1,0:T(8,128)S(1)}, f32[256,256]{1,0:T(8,128)S(1)}, u32[]{:S(2)}, u32[]{:S(2)}) %collective-permute-start.21) | collective-permute-done | bytes 262176 | tf_op jit(solution)/shard_map/ppermute | solution.py:319
  76.9 2.3 %collective-permute-done.23 = f32[128,256]{1,0:T(8,128)S(1)} collective-permute-done((f32[128,256]{1,0:T(8,128)S(1)}, f32[128,256]{1,0:T(8,128)S(1)}, u32[]{:S(2)}, u32[]{:S(2)}) %collective-permute-start.23) | collective-permute-done | bytes 131104 | tf_op jit(solution)/shard_map/ppermute | solution.py:319
  84.5 9.7 %collective-permute-done.27 = f32[128,256]{1,0:T(8,128)S(1)} collective-permute-done((f32[128,256]{1,0:T(8,128)S(1)}, f32[128,256]{1,0:T(8,128)S(1)}, u32[]{:S(2)}, u32[]{:S(2)}) %collective-permute-start.27) | collective-permute-done | bytes 131104 | tf_op jit(solution)/shard_map/ppermute | solution.py:319
  96.0 3.0 %collective-permute-start.33 = (f32[256,256]{1,0:T(8,128)S(1)}, f32[256,256]{1,0:T(8,128)S(1)}, u32[]{:S(2)}, u32[]{:S(2)}) collective-permute-start(f32[256,256]{1,0:T(8,128)S(1)} %get-tuple-element.213), channel_id=1, source_target_pairs={{0,2},{1,3},{2,0},{3,1},{4,6},{5,7},{6,4},{7,5},{8,10},{9,11},{10,... | collective-permute-start | bytes 786440 | tf_op jit(solution)/shard_map/ppermute | solution.py:319
  101.7 6.8 %collective-permute-done.32 = f32[128,256]{1,0:T(8,128)S(1)} collective-permute-done((f32[128,256]{1,0:T(8,128)S(1)}, f32[128,256]{1,0:T(8,128)S(1)}, u32[]{:S(2)}, u32[]{:S(2)}) %collective-permute-start.32) | collective-permute-done | bytes 131104 | tf_op jit(solution)/shard_map/ppermute | solution.py:319
  110.9 4.7 %collective-permute-start.39 = (f32[128,256]{1,0:T(8,128)S(1)}, f32[128,256]{1,0:T(8,128)S(1)}, u32[]{:S(2)}, u32[]{:S(2)}) collective-permute-start(f32[128,256]{1,0:T(8,128)S(1)} %add.51), channel_id=1, source_target_pairs={{0,16},{1,17},{2,18},{3,19},{4,20},{5,21},{6,22},{7,23},{8,24},{9,... | collective-permute-start | bytes 393224 | tf_op jit(solution)/shard_map/ppermute | solution.py:319
  115.6 2.9 %collective-permute-start.40 = (f32[128,256]{1,0:T(8,128)S(1)}, f32[128,256]{1,0:T(8,128)S(1)}, u32[]{:S(2)}, u32[]{:S(2)}) collective-permute-start(f32[128,256]{1,0:T(8,128)S(1)} %add.51), channel_id=1, source_target_pairs={{0,24},{1,25},{2,26},{3,27},{4,28},{5,29},{6,30},{7,31},{8,16},{9,... | collective-permute-start | bytes 393224 | tf_op jit(solution)/shard_map/ppermute | solution.py:319
  118.5 4.0 %collective-permute-done.39 = f32[128,256]{1,0:T(8,128)S(1)} collective-permute-done((f32[128,256]{1,0:T(8,128)S(1)}, f32[128,256]{1,0:T(8,128)S(1)}, u32[]{:S(2)}, u32[]{:S(2)}) %collective-permute-start.39) | collective-permute-done | bytes 131104 | tf_op jit(solution)/shard_map/ppermute | solution.py:319
  124.6 4.5 %lead.1 = f32[256,256]{1,0:T(8,128)S(1)} custom-call(s32[3]{0:T(128)S(1)} %pad_add_fusion.ids, f32[256,256]{1,0:T(8,128)S(1)} %broadcast_select_fusion.refs_4_.c0, f32[256,256]{1,0:T(8,128)S(1)} %collective-permute-done.34.refs_5_.c1, f32[256,256]{1,0:T(8,128)S(1)} %collective-permute-done.36.c0_other, f32[256,256]{1,0:T(8,128)S(1)} %collective-permute-done.37.c1_other, ...), custom_call_target="tpu_custom_call" | custom-call | flops 1 | bytes 1 | tf_op jit(solution)/shard_map/lead/pallas_call | solution.py:43
  131.9 9.8 %collective-permute-done.43.refs_1_ = f32[256,256]{1,0:T(8,128)S(1)} collective-permute-done((f32[256,256]{1,0:T(8,128)S(1)}, f32[256,256]{1,0:T(8,128)S(1)}, u32[]{:S(2)}, u32[]{:S(2)}) %collective-permute-start.43) | collective-permute-done | bytes 262176 | tf_op jit(solution)/shard_map/ppermute | solution.py:319
  141.7 3.9 %collective-permute-done.44.refs_2_ = f32[256,256]{1,0:T(8,128)S(1)} collective-permute-done((f32[256,256]{1,0:T(8,128)S(1)}, f32[256,256]{1,0:T(8,128)S(1)}, u32[]{:S(2)}, u32[]{:S(2)}) %collective-permute-start.44) | collective-permute-done | bytes 262176 | tf_op jit(solution)/shard_map/ppermute | solution.py:319
  146.2 7.3 %collective-permute-done.45.refs_3_ = f32[256,256]{1,0:T(8,128)S(1)} collective-permute-done((f32[256,256]{1,0:T(8,128)S(1)}, f32[256,256]{1,0:T(8,128)S(1)}, u32[]{:S(2)}, u32[]{:S(2)}) %collective-permute-start.45) | collective-permute-done | bytes 262176 | tf_op jit(solution)/shard_map/ppermute | solution.py:319
  155.0 2.0 %place.1 = f32[1024,512]{1,0:T(8,128)} custom-call(s32[3]{0:T(128)S(1)} %pad_add_fusion.ids, f32[256,256]{1,0:T(8,128)S(1)} %end.1.refs_0_, f32[256,256]{1,0:T(8,128)S(1)} %collective-permute-done.43.refs_1_, f32[256,256]{1,0:T(8,128)S(1)} %collective-permute-done.44.refs_2_, f32[256,256]{1,0:T(8,128)S(1)} %collective-permute-done.45.refs_3_, ...), custom_call_target="tpu_custom_call" | custom-call | flops 1 | bytes 1 | tf_op jit(solution)/shard_map/place/pallas_call | solution.py:43
  (123 shorter events, 48.7 us)
Async XLA Ops:
  1.5 11.6 %collective-permute-start = (f32[256,256]{1,0:T(8,128)S(1)}, f32[256,256]{1,0:T(8,128)}, u32[]{:S(2)}, u32[]{:S(2)}) collective-permute-start(f32[256,256]{1,0:T(8,128)S(1)} %get-tuple-element.146), channel_id=1, source_target_pairs={{0,2},{1,3},{8,10},{9,11},{16,18},{17,19},{24,26},{25,27}} | collective-permute-start | bytes 786440 | tf_op jit(solution)/shard_map/ppermute | solution.py:319
  7.1 14.8 %collective-permute-start.3 = (f32[256,256]{1,0:T(8,128)S(1)}, f32[256,256]{1,0:T(8,128)}, u32[]{:S(2)}, u32[]{:S(2)}) collective-permute-start(f32[256,256]{1,0:T(8,128)S(1)} %get-tuple-element.142), channel_id=1, source_target_pairs={{0,2},{1,3},{8,10},{9,11},{16,18},{17,19},{24,26},{25,27}} | collective-permute-start | bytes 786440 | tf_op jit(solution)/shard_map/ppermute | solution.py:319
  9.1 15.2 %collective-permute-start.6 = (f32[256,256]{1,0:T(8,128)S(1)}, f32[256,256]{1,0:T(8,128)}, u32[]{:S(2)}, u32[]{:S(2)}) collective-permute-start(f32[256,256]{1,0:T(8,128)S(1)} %get-tuple-element.138), channel_id=1, source_target_pairs={{0,2},{1,3},{8,10},{9,11},{16,18},{17,19},{24,26},{25,27}} | collective-permute-start | bytes 786440 | tf_op jit(solution)/shard_map/ppermute | solution.py:319
  13.1 12.6 %collective-permute-start.1 = (f32[256,256]{1,0:T(8,128)}, f32[256,256]{1,0:T(8,128)}, u32[]{:S(2)}, u32[]{:S(2)}) collective-permute-start(f32[256,256]{1,0:T(8,128)} %collective-permute-done), channel_id=1, source_target_pairs={{2,4},{3,5},{10,12},{11,13},{18,20},{19,21},{26,28},{27,29}} | collective-permute-start | bytes 786440 | tf_op jit(solution)/shard_map/ppermute | solution.py:319
  19.9 10.7 %collective-permute-start.11 = (f32[256,256]{1,0:T(8,128)}, f32[256,256]{1,0:T(8,128)}, u32[]{:S(2)}, u32[]{:S(2)}) collective-permute-start(f32[256,256]{1,0:T(8,128)} %select_select_fusion.6), channel_id=1, source_target_pairs={{0,2},{1,3},{8,10},{9,11},{16,18},{17,19},{24,26},{25,27}} | collective-permute-start | bytes 786440 | tf_op jit(solution)/shard_map/ppermute | solution.py:319
  27.1 13.5 %collective-permute-start.5 = (f32[512,256]{1,0:T(8,128)S(1)}, f32[512,256]{1,0:T(8,128)S(1)}, u32[]{:S(2)}, u32[]{:S(2)}) collective-permute-start(f32[512,256]{1,0:T(8,128)S(1)} %pad_maximum_fusion.blocks), channel_id=1, source_target_pairs={{0,8},{1,9},{8,0},{9,1}} | collective-permute-start | bytes 1572872 | tf_op jit(solution)/shard_map/ppermute | solution.py:319
  45.2 14.0 %collective-permute-start.16 = (f32[256,256]{1,0:T(8,128)S(1)}, f32[256,256]{1,0:T(8,128)S(1)}, u32[]{:S(2)}, u32[]{:S(2)}) collective-permute-start(f32[256,256]{1,0:T(8,128)S(1)} %get-tuple-element.161.v0), channel_id=1, source_target_pairs={{0,16},{1,17},{2,18},{3,19},{4,20},{5,21},{6,22},{7,23},{8,24},{9,... | collective-permute-start | bytes 786440 | tf_op jit(solution)/shard_map/ppermute | solution.py:319
  45.3 14.0 %collective-permute-start.17 = (f32[256,256]{1,0:T(8,128)S(1)}, f32[256,256]{1,0:T(8,128)S(1)}, u32[]{:S(2)}, u32[]{:S(2)}) collective-permute-start(f32[256,256]{1,0:T(8,128)S(1)} %get-tuple-element.161.v0), channel_id=1, source_target_pairs={{0,24},{1,25},{2,26},{3,27},{4,28},{5,29},{6,30},{7,31},{8,16},{9,... | collective-permute-start | bytes 786440 | tf_op jit(solution)/shard_map/ppermute | solution.py:319
  47.2 12.1 %collective-permute-start.19 = (f32[256,256]{1,0:T(8,128)S(1)}, f32[256,256]{1,0:T(8,128)S(1)}, u32[]{:S(2)}, u32[]{:S(2)}) collective-permute-start(f32[256,256]{1,0:T(8,128)S(1)} %copy-done.7), channel_id=1, source_target_pairs={{4,6},{5,7},{12,14},{13,15},{20,22},{21,23},{28,30},{29,31}} | collective-permute-start | bytes 786440 | tf_op jit(solution)/shard_map/ppermute | solution.py:319
  64.9 12.0 %collective-permute-start.21 = (f32[256,256]{1,0:T(8,128)S(1)}, f32[256,256]{1,0:T(8,128)S(1)}, u32[]{:S(2)}, u32[]{:S(2)}) collective-permute-start(f32[256,256]{1,0:T(8,128)S(1)} %select_select_fusion), channel_id=1, source_target_pairs={{0,16},{1,17},{2,18},{3,19},{4,20},{5,21},{6,22},{7,23},{8,24},{9,... | collective-permute-start | bytes 786440 | tf_op jit(solution)/shard_map/ppermute | solution.py:319
  65.1 14.1 %collective-permute-start.25 = (f32[256,256]{1,0:T(8,128)S(1)}, f32[256,256]{1,0:T(8,128)S(1)}, u32[]{:S(2)}, u32[]{:S(2)}) collective-permute-start(f32[256,256]{1,0:T(8,128)S(1)} %get-tuple-element.191), channel_id=1, source_target_pairs={{0,2},{1,3},{2,0},{3,1},{4,6},{5,7},{6,4},{7,5},{8,10},{9,11},{10,... | collective-permute-start | bytes 786440 | tf_op jit(solution)/shard_map/ppermute | solution.py:319
  67.9 11.3 %collective-permute-start.23 = (f32[128,256]{1,0:T(8,128)S(1)}, f32[128,256]{1,0:T(8,128)S(1)}, u32[]{:S(2)}, u32[]{:S(2)}) collective-permute-start(f32[128,256]{1,0:T(8,128)S(1)} %get-tuple-element.187), channel_id=1, source_target_pairs={{0,16},{1,17},{2,18},{3,19},{4,20},{5,21},{6,22},{7,23},{8,24},{9,... | collective-permute-start | bytes 393224 | tf_op jit(solution)/shard_map/ppermute | solution.py:319
  79.2 15.0 %collective-permute-start.26 = (f32[256,256]{1,0:T(8,128)S(1)}, f32[256,256]{1,0:T(8,128)S(1)}, u32[]{:S(2)}, u32[]{:S(2)}) collective-permute-start(f32[256,256]{1,0:T(8,128)S(1)} %add.43), channel_id=1, source_target_pairs={{0,4},{1,5},{2,6},{3,7},{4,0},{5,1},{6,2},{7,3},{8,12},{9,13},{10,... | collective-permute-start | bytes 786440 | tf_op jit(solution)/shard_map/ppermute | solution.py:319
  80.9 13.3 %collective-permute-start.28 = (f32[256,256]{1,0:T(8,128)S(1)}, f32[256,256]{1,0:T(8,128)S(1)}, u32[]{:S(2)}, u32[]{:S(2)}) collective-permute-start(f32[256,256]{1,0:T(8,128)S(1)} %get-tuple-element.202), channel_id=1, source_target_pairs={{0,8},{1,9},{2,10},{3,11},{4,12},{5,13},{6,14},{7,15},{8,0},{9,1},... | collective-permute-start | bytes 786440 | tf_op jit(solution)/shard_map/ppermute | solution.py:319
  82.2 12.0 %collective-permute-start.29 = (f32[256,256]{1,0:T(8,128)S(1)}, f32[256,256]{1,0:T(8,128)S(1)}, u32[]{:S(2)}, u32[]{:S(2)}) collective-permute-start(f32[256,256]{1,0:T(8,128)S(1)} %get-tuple-element.203), channel_id=1, source_target_pairs={{0,16},{1,17},{2,18},{3,19},{4,20},{5,21},{6,22},{7,23},{8,24},{9,... | collective-permute-start | bytes 786440 | tf_op jit(solution)/shard_map/ppermute | solution.py:319
  83.1 12.2 %collective-permute-start.30 = (f32[256,256]{1,0:T(8,128)S(1)}, f32[256,256]{1,0:T(8,128)S(1)}, u32[]{:S(2)}, u32[]{:S(2)}) collective-permute-start(f32[256,256]{1,0:T(8,128)S(1)} %get-tuple-element.204), channel_id=1, source_target_pairs={{0,24},{1,25},{2,26},{3,27},{4,28},{5,29},{6,30},{7,31},{8,16},{9,... | collective-permute-start | bytes 786440 | tf_op jit(solution)/shard_map/ppermute | solution.py:319
  95.3 13.3 %collective-permute-start.31 = (f32[256,256]{1,0:T(8,128)S(1)}, f32[256,256]{1,0:T(8,128)S(1)}, u32[]{:S(2)}, u32[]{:S(2)}) collective-permute-start(f32[256,256]{1,0:T(8,128)S(1)} %add_add_fusion), channel_id=1, source_target_pairs={{0,0},{1,1},{2,20},{3,21},{4,2},{5,3},{6,22},{7,23},{8,8},{9,9},{1... | collective-permute-start | bytes 786440 | tf_op jit(solution)/shard_map/ppermute | solution.py:319
  96.0 12.6 %collective-permute-start.33 = (f32[256,256]{1,0:T(8,128)S(1)}, f32[256,256]{1,0:T(8,128)S(1)}, u32[]{:S(2)}, u32[]{:S(2)}) collective-permute-start(f32[256,256]{1,0:T(8,128)S(1)} %get-tuple-element.213), channel_id=1, source_target_pairs={{0,2},{1,3},{2,0},{3,1},{4,6},{5,7},{6,4},{7,5},{8,10},{9,11},{10,... | collective-permute-start | bytes 786440 | tf_op jit(solution)/shard_map/ppermute | solution.py:319
  110.3 12.3 %collective-permute-start.35 = (f32[256,256]{1,0:T(8,128)S(1)}, f32[256,256]{1,0:T(8,128)S(1)}, u32[]{:S(2)}, u32[]{:S(2)}) collective-permute-start(f32[256,256]{1,0:T(8,128)S(1)} %get-tuple-element.220.solved), channel_id=1, source_target_pairs={{0,1},{1,0},{2,3},{3,2},{4,5},{5,4},{6,7},{7,6},{8,9},{9,8},{10,11... | collective-permute-start | bytes 786440 | tf_op jit(solution)/shard_map/ppermute | solution.py:319
  110.4 12.2 %collective-permute-start.36 = (f32[256,256]{1,0:T(8,128)S(1)}, f32[256,256]{1,0:T(8,128)S(1)}, u32[]{:S(2)}, u32[]{:S(2)}) collective-permute-start(f32[256,256]{1,0:T(8,128)S(1)} %broadcast_select_fusion.refs_4_.c0), channel_id=1, source_target_pairs={{0,1},{1,0},{2,3},{3,2},{4,5},{5,4},{6,7},{7,6},{8,9},{9,8},{10,11... | collective-permute-start | bytes 786440 | tf_op jit(solution)/shard_map/ppermute | solution.py:319
  110.9 11.7 %collective-permute-start.37 = (f32[256,256]{1,0:T(8,128)S(1)}, f32[256,256]{1,0:T(8,128)S(1)}, u32[]{:S(2)}, u32[]{:S(2)}) collective-permute-start(f32[256,256]{1,0:T(8,128)S(1)} %collective-permute-done.34.refs_5_.c1), channel_id=1, source_target_pairs={{0,1},{1,0},{2,3},{3,2},{4,5},{5,4},{6,7},{7,6},{8,9},{9,8},{10,11... | collective-permute-start | bytes 786440 | tf_op jit(solution)/shard_map/ppermute | solution.py:319
  110.9 11.6 %collective-permute-start.39 = (f32[128,256]{1,0:T(8,128)S(1)}, f32[128,256]{1,0:T(8,128)S(1)}, u32[]{:S(2)}, u32[]{:S(2)}) collective-permute-start(f32[128,256]{1,0:T(8,128)S(1)} %add.51), channel_id=1, source_target_pairs={{0,16},{1,17},{2,18},{3,19},{4,20},{5,21},{6,22},{7,23},{8,24},{9,... | collective-permute-start | bytes 393224 | tf_op jit(solution)/shard_map/ppermute | solution.py:319
  130.5 11.2 %collective-permute-start.43 = (f32[256,256]{1,0:T(8,128)S(1)}, f32[256,256]{1,0:T(8,128)S(1)}, u32[]{:S(2)}, u32[]{:S(2)}) collective-permute-start(f32[256,256]{1,0:T(8,128)S(1)} %end.1.refs_0_), channel_id=1, source_target_pairs={{0,2},{1,3},{2,0},{3,1},{4,6},{5,7},{6,4},{7,5},{8,10},{9,11},{10,... | collective-permute-start | bytes 786440 | tf_op jit(solution)/shard_map/ppermute | solution.py:319
  130.5 15.1 %collective-permute-start.44 = (f32[256,256]{1,0:T(8,128)S(1)}, f32[256,256]{1,0:T(8,128)S(1)}, u32[]{:S(2)}, u32[]{:S(2)}) collective-permute-start(f32[256,256]{1,0:T(8,128)S(1)} %end.1.refs_0_), channel_id=1, source_target_pairs={{0,4},{1,5},{2,6},{3,7},{4,0},{5,1},{6,2},{7,3},{8,12},{9,13},{10,... | collective-permute-start | bytes 786440 | tf_op jit(solution)/shard_map/ppermute | solution.py:319
  (35 other events, 278.3 us)

commit v4 on v3

--- a/solution.py
+++ b/solution.py
@@ -215,11 +215,18 @@
     solved[...] = quick(total, inverse)
 
 
-def lead_kernel(ids, c0, c1, c0_other, c1_other, blocks, across, blocks_other, across_other, sums_ref, sums_other, out_ref):
+def end_kernel(ids, total, solved, second, c0, c1, c0_other, c1_other, blocks, across, blocks_other, across_other, sums_ref, sums_other, out_ref):
     row, first = ids[ROW], ids[LANE] == 0
     own, other = (c0, c1), (c0_other, c1_other)
-
-    @pl.when((ids[PAIR] == 0) & (row < 2))
+    leading = (ids[PAIR] == 0) & (row < 2)
+
+    @pl.when(jnp.logical_not(leading))
+    def _():
+        inverse, link = carried_blocks(ids, own)
+        whole = quick(total[...] - quick(second[...], link), inverse)
+        out_ref[...] = jnp.where(first, whole, solved[...])
+
+    @pl.when(leading)
     def _():
         rows, cols = positions()
         in_first_row = row == 0
@@ -268,13 +275,6 @@
         out_ref[...] = jnp.where(
             in_first_row, jnp.where(first, e0, 0.0), jnp.where(first, g0, e1)
         )
-
-
-def end_kernel(ids, total, solved, second, c0, c1, lead, out_ref):
-    inverse, link = carried_blocks(ids, (c0, c1))
-    whole = quick(total[...] - quick(second[...], link), inverse)
-    whole = jnp.where(ids[LANE] == 0, whole, solved[...])
-    out_ref[...] = jnp.where((ids[PAIR] == 0) & (ids[ROW] < 2), lead[...], whole)
 
 
 def place_kernel(n_pairs, ids, *refs):
@@ -470,7 +470,11 @@
         own_share = own_share + shares.pop(0)
         bit *= 2
     moved = swap_pairs(shares[bit], bit)
-    total_other = swap_pairs(total, 1)
+    bit = 1
+    while bit < n_pairs // 2:
+        total = total + swap_pairs(total, bit)
+        bit *= 2
+    total_other = swap_pairs(total, bit)
     block_sums = [block_sums[0]] + [swap_rows(block_sums[d], d) for d in range(1, n_rows)]
     rest = together(own_share, moved, nearest_share, carried, total, total_other, *block_sums)
     own_share, moved, nearest_share, carried, total, total_other = rest[:6]
@@ -481,27 +485,26 @@
         return p % 2 * 2 + r % 2, p // 2 + half * (n_pairs // 2), k
 
     owned = send(owned, owner)
-    bit = 2
-    while bit < n_pairs:
-        total = total + swap_pairs(total, bit)
-        bit *= 2
     carried = [carried, swap_rows(carried, 1)]
     nearest_share = swap_pairs(nearest_share, 1)
-    owned, total, nearest_share, *carried = together(owned, total, nearest_share, *carried)
+    sums = [total] + [swap_rows(total, d) for d in range(1, n_rows)]
+    owned, nearest_share, *rest = together(owned, nearest_share, *carried, *sums)
+    carried, sums = rest[:2], jnp.concatenate(rest[2:], 0)
     shares = own_share, moved, nearest_share
 
     mine, solved = call(
         functools.partial(solve_kernel, 3), "solve", (SQUARE, SQUARE), ids, *shares, owned, *carried
     )
-    sums = [total] + [swap_rows(total, d) for d in range(1, n_rows)]
-    second, *rest = together(swap(solved), *[swap(x) for x in carried], *sums)
-    carried_other, sums = rest[:2], jnp.concatenate(rest[2:], 0)
-    sums_other = swap(sums)
-    lead = call(
-        lead_kernel,
-        "lead",
+    second, sums_other = swap(solved), swap(sums)
+    carried_other = [swap(x) for x in carried]
+    result = call(
+        end_kernel,
+        "end",
         SQUARE,
         ids,
+        mine,
+        solved,
+        second,
         *carried,
         *carried_other,
         blocks,
@@ -511,7 +514,6 @@
         sums,
         sums_other,
     )
-    result = call(end_kernel, "end", SQUARE, ids, mine, solved, second, *carried, lead)
     results, others, bit = {0: result}, {}, n_pairs // 2
     while bit:
         for d, value in list(results.items()):

time: 157 us -> 150 us (0.955)
  starting transfers between devices: 54.9 us -> 51.4 us
  waiting for transfers between devices: 73.1 us -> 70 us
    ppermute x49, starting transfers between devices: 54.9 us -> 51.4 us  [send(): return lax.ppermute(value, ('row', 'col'), edges)]
    ppermute x49, waiting for transfers between devices: 73.1 us -> 70 us  [send(): return lax.ppermute(value, ('row', 'col'), edges)]
    pallas_call x9 -> x8, Pallas kernels: 21.6 us -> 20.4 us  [call(): pl.pallas_call(kernel, out_shape=out_shape, in_specs=[pl.BlockSpec(memory...]
  transfers between devices with their start and end apart: 49 -> 49, of which waited for: 16 -> 17; matrix products, arithmetic and copies ran while one was open for 2% -> 3% of each run, Pallas kernels for 9% -> 9%
where the time goes in v4:
time: 150 us; the launch traced here: 149 us
  waiting for transfers between devices  70 us (47%)
  starting transfers between devices  51.4 us (34%)
  Pallas kernels  20.4 us (14%)
  other arithmetic  3.92 us (3%)
  local copies, waits for them, and re-layouts  3 us (2%)
    ppermute x49, waiting for transfers between devices, send(): return lax.ppermute(value, ('row', 'col'), edges)  70 us
    ppermute x49, starting transfers between devices, send(): return lax.ppermute(value, ('row', 'col'), edges)  51.4 us
    pallas_call x8, Pallas kernels, call(): pl.pallas_call(kernel, out_shape=out_shape, in_specs=[pl.BlockSpec(memory...  20.4 us
  transfers between devices with their start and end apart: 49, of which 17 were waited for; matrix products, arithmetic and copies ran while one was open for 3% of the time, Pallas kernels for 9%

profile of v4, /device:TPU:0, one launch (start us, length us, event | category | flops | bytes accessed | tf_op | source)
XLA Modules:
  0.0 149.2 jit_solution(3612307284046218023)
XLA Ops:
  1.5 5.6 %collective-permute-start = (f32[256,256]{1,0:T(8,128)S(1)}, f32[256,256]{1,0:T(8,128)}, u32[]{:S(2)}, u32[]{:S(2)}) collective-permute-start(f32[256,256]{1,0:T(8,128)S(1)} %get-tuple-element.142), channel_id=1, source_target_pairs={{0,2},{1,3},{8,10},{9,11},{16,18},{17,19},{24,26},{25,27}} | collective-permute-start | bytes 786440 | tf_op jit(solution)/shard_map/ppermute | solution.py:319
  7.1 2.0 %collective-permute-start.3 = (f32[256,256]{1,0:T(8,128)S(1)}, f32[256,256]{1,0:T(8,128)}, u32[]{:S(2)}, u32[]{:S(2)}) collective-permute-start(f32[256,256]{1,0:T(8,128)S(1)} %get-tuple-element.138), channel_id=1, source_target_pairs={{0,2},{1,3},{8,10},{9,11},{16,18},{17,19},{24,26},{25,27}} | collective-permute-start | bytes 786440 | tf_op jit(solution)/shard_map/ppermute | solution.py:319
  9.1 2.0 %collective-permute-start.6 = (f32[256,256]{1,0:T(8,128)S(1)}, f32[256,256]{1,0:T(8,128)}, u32[]{:S(2)}, u32[]{:S(2)}) collective-permute-start(f32[256,256]{1,0:T(8,128)S(1)} %get-tuple-element.134), channel_id=1, source_target_pairs={{0,2},{1,3},{8,10},{9,11},{16,18},{17,19},{24,26},{25,27}} | collective-permute-start | bytes 786440 | tf_op jit(solution)/shard_map/ppermute | solution.py:319
  14.5 4.6 %inverse.1 = f32[256,256]{1,0:T(8,128)S(1)} custom-call(s32[3]{0:T(128)S(1)} %pad_add_fusion.ids, f32[256,256]{1,0:T(8,128)S(1)} %get-tuple-element.120.block_ref), custom_call_target="tpu_custom_call" | custom-call | flops 1 | bytes 1 | tf_op jit(solution)/shard_map/inverse/pallas_call | solution.py:43
  19.9 2.0 %collective-permute-start.11 = (f32[256,256]{1,0:T(8,128)}, f32[256,256]{1,0:T(8,128)}, u32[]{:S(2)}, u32[]{:S(2)}) collective-permute-start(f32[256,256]{1,0:T(8,128)} %select_select_fusion.6), channel_id=1, source_target_pairs={{0,2},{1,3},{8,10},{9,11},{16,18},{17,19},{24,26},{25,27}} | collective-permute-start | bytes 786440 | tf_op jit(solution)/shard_map/ppermute | solution.py:319
  27.1 3.4 %collective-permute-start.5 = (f32[512,256]{1,0:T(8,128)S(1)}, f32[512,256]{1,0:T(8,128)S(1)}, u32[]{:S(2)}, u32[]{:S(2)}) collective-permute-start(f32[512,256]{1,0:T(8,128)S(1)} %pad_maximum_fusion.blocks), channel_id=1, source_target_pairs={{0,8},{1,9},{8,0},{9,1}} | collective-permute-start | bytes 1572872 | tf_op jit(solution)/shard_map/ppermute | solution.py:319
  32.9 7.8 %collective-permute-done.5.across = f32[512,256]{1,0:T(8,128)S(1)} collective-permute-done((f32[512,256]{1,0:T(8,128)S(1)}, f32[512,256]{1,0:T(8,128)S(1)}, u32[]{:S(2)}, u32[]{:S(2)}) %collective-permute-start.5) | collective-permute-done | bytes 524320 | tf_op jit(solution)/shard_map/ppermute | solution.py:319
  45.3 2.0 %collective-permute-start.17 = (f32[256,256]{1,0:T(8,128)S(1)}, f32[256,256]{1,0:T(8,128)S(1)}, u32[]{:S(2)}, u32[]{:S(2)}) collective-permute-start(f32[256,256]{1,0:T(8,128)S(1)} %get-tuple-element.157.v0), channel_id=1, source_target_pairs={{0,24},{1,25},{2,26},{3,27},{4,28},{5,29},{6,30},{7,31},{8,16},{9,... | collective-permute-start | bytes 786440 | tf_op jit(solution)/shard_map/ppermute | solution.py:319
  48.2 2.5 %masked.1 = (bf16[1024,512]{1,0:T(8,128)(2,1)S(1)}, bf16[1024,512]{1,0:T(8,128)(2,1)S(1)}, bf16[512,512]{1,0:T(8,128)(2,1)S(1)}, bf16[512,512]{1,0:T(8,128)(2,1)S(1)}) custom-call(s32[3]{0:T(128)S(1)} %pad_add_fusion.ids, f32[1024,512]{1,0:T(8,128)S(1)} %copy-done, f32[1024,512]{1,0:T(8,128)} %collective-permute-done.18.other), custom_call_target="tpu_custom_call" | custom-call | flops 1 | bytes 1 | tf_op jit(solution)/shard_map/masked/pallas_call | solution.py:43
  50.7 2.1 %columns.1 = (f32[256,1024]{1,0:T(8,128)S(1)}, f32[256,512]{1,0:T(8,128)S(1)}, f32[256,256]{1,0:T(8,128)S(1)}, f32[256,256]{1,0:T(8,128)S(1)}, f32[256,256]{1,0:T(8,128)S(1)}, /*index=5*/f32[256,256]{1,0:T(8,128)S(1)}) custom-call(s32[3]{0:T(128)S(1)} %pad_add_fusion.ids, bf16[1024,512]{1,0:T(8,128)(2,1)S(1)} %get-tuple-element.129.low_1, ...), custom_call_target="tpu_custom_call" | custom-call | flops 1 | bytes 1 | tf_op jit(solution)/shard_map/columns/pallas_call | solution.py:43
  52.9 6.4 %collective-permute-done.16.v2 = f32[256,256]{1,0:T(8,128)S(1)} collective-permute-done((f32[256,256]{1,0:T(8,128)S(1)}, f32[256,256]{1,0:T(8,128)S(1)}, u32[]{:S(2)}, u32[]{:S(2)}) %collective-permute-start.16) | collective-permute-done | bytes 262176 | tf_op jit(solution)/shard_map/ppermute | solution.py:319
  59.9 2.1 %rows.1 = (f32[256,256]{1,0:T(8,128)S(1)}, f32[256,256]{1,0:T(8,128)S(1)}, f32[256,256]{1,0:T(8,128)S(1)}, f32[256,256]{1,0:T(8,128)S(1)}, f32[1024,256]{1,0:T(8,128)S(1)}) custom-call(s32[3]{0:T(128)S(1)} %pad_add_fusion.ids, bf16[1024,512]{1,0:T(8,128)(2,1)S(1)} %get-tuple-element.129.low_1, bf16[1024,512]{1,0:T(8,128)(2,1)S(1)} %get-tuple-element.130.low_2, ...), custom_call_target="tpu_custom_call" | custom-call | flops 1 | bytes 1 | tf_op jit(solution)/shard_map/rows/pallas_call | solution.py:43
  65.1 2.2 %collective-permute-start.25 = (f32[256,256]{1,0:T(8,128)S(1)}, f32[256,256]{1,0:T(8,128)S(1)}, u32[]{:S(2)}, u32[]{:S(2)}) collective-permute-start(f32[256,256]{1,0:T(8,128)S(1)} %get-tuple-element.187), channel_id=1, source_target_pairs={{0,2},{1,3},{2,0},{3,1},{4,6},{5,7},{6,4},{7,5},{8,10},{9,11},{10,... | collective-permute-start | bytes 786440 | tf_op jit(solution)/shard_map/ppermute | solution.py:319
  70.8 6.0 %collective-permute-done.21 = f32[256,256]{1,0:T(8,128)S(1)} collective-permute-done((f32[256,256]{1,0:T(8,128)S(1)}, f32[256,256]{1,0:T(8,128)S(1)}, u32[]{:S(2)}, u32[]{:S(2)}) %collective-permute-start.21) | collective-permute-done | bytes 262176 | tf_op jit(solution)/shard_map/ppermute | solution.py:319
  76.9 2.3 %collective-permute-done.23 = f32[128,256]{1,0:T(8,128)S(1)} collective-permute-done((f32[128,256]{1,0:T(8,128)S(1)}, f32[128,256]{1,0:T(8,128)S(1)}, u32[]{:S(2)}, u32[]{:S(2)}) %collective-permute-start.23) | collective-permute-done | bytes 131104 | tf_op jit(solution)/shard_map/ppermute | solution.py:319
  87.4 12.7 %collective-permute-done.28 = f32[128,256]{1,0:T(8,128)S(1)} collective-permute-done((f32[128,256]{1,0:T(8,128)S(1)}, f32[128,256]{1,0:T(8,128)S(1)}, u32[]{:S(2)}, u32[]{:S(2)}) %collective-permute-start.28) | collective-permute-done | bytes 131104 | tf_op jit(solution)/shard_map/ppermute | solution.py:319
  105.3 2.5 %collective-permute-start.36 = (f32[128,256]{1,0:T(8,128)S(1)}, f32[128,256]{1,0:T(8,128)S(1)}, u32[]{:S(2)}, u32[]{:S(2)}) collective-permute-start(f32[128,256]{1,0:T(8,128)S(1)} %add.51), channel_id=1, source_target_pairs={{0,16},{1,17},{2,18},{3,19},{4,20},{5,21},{6,22},{7,23},{8,24},{9,... | collective-permute-start | bytes 393224 | tf_op jit(solution)/shard_map/ppermute | solution.py:319
  107.8 4.1 %collective-permute-done.36 = f32[128,256]{1,0:T(8,128)S(1)} collective-permute-done((f32[128,256]{1,0:T(8,128)S(1)}, f32[128,256]{1,0:T(8,128)S(1)}, u32[]{:S(2)}, u32[]{:S(2)}) %collective-permute-start.36) | collective-permute-done | bytes 131104 | tf_op jit(solution)/shard_map/ppermute | solution.py:319
  111.9 2.8 %collective-permute-done.37 = f32[128,256]{1,0:T(8,128)S(1)} collective-permute-done((f32[128,256]{1,0:T(8,128)S(1)}, f32[128,256]{1,0:T(8,128)S(1)}, u32[]{:S(2)}, u32[]{:S(2)}) %collective-permute-start.37) | collective-permute-done | bytes 131104 | tf_op jit(solution)/shard_map/ppermute | solution.py:319
  118.2 4.5 %end.1.refs_0_ = f32[256,256]{1,0:T(8,128)S(1)} custom-call(s32[3]{0:T(128)S(1)} %pad_add_fusion.ids, f32[256,256]{1,0:T(8,128)S(1)} %get-tuple-element.215.total, f32[256,256]{1,0:T(8,128)S(1)} %get-tuple-element.216.solved, f32[256,256]{1,0:T(8,128)S(1)} %collective-permute-done.38.second, f32[256,256]{1,0:T(8,128)S(1)} %broadcast_select_fusion.refs_4_.c0, ...), custom_call_target="tpu_custom_call" | custom-call | flops 1 | bytes 1 | tf_op jit(solution)/shard_map/end/pallas_call | solution.py:43
  125.1 10.8 %collective-permute-done.43.refs_1_ = f32[256,256]{1,0:T(8,128)S(1)} collective-permute-done((f32[256,256]{1,0:T(8,128)S(1)}, f32[256,256]{1,0:T(8,128)S(1)}, u32[]{:S(2)}, u32[]{:S(2)}) %collective-permute-start.43) | collective-permute-done | bytes 262176 | tf_op jit(solution)/shard_map/ppermute | solution.py:319
  135.9 2.2 %collective-permute-done.44.refs_2_ = f32[256,256]{1,0:T(8,128)S(1)} collective-permute-done((f32[256,256]{1,0:T(8,128)S(1)}, f32[256,256]{1,0:T(8,128)S(1)}, u32[]{:S(2)}, u32[]{:S(2)}) %collective-permute-start.44) | collective-permute-done | bytes 262176 | tf_op jit(solution)/shard_map/ppermute | solution.py:319
  138.6 7.0 %collective-permute-done.45.refs_3_ = f32[256,256]{1,0:T(8,128)S(1)} collective-permute-done((f32[256,256]{1,0:T(8,128)S(1)}, f32[256,256]{1,0:T(8,128)S(1)}, u32[]{:S(2)}, u32[]{:S(2)}) %collective-permute-start.45) | collective-permute-done | bytes 262176 | tf_op jit(solution)/shard_map/ppermute | solution.py:319
  147.2 2.0 %place.1 = f32[1024,512]{1,0:T(8,128)} custom-call(s32[3]{0:T(128)S(1)} %pad_add_fusion.ids, f32[256,256]{1,0:T(8,128)S(1)} %end.1.refs_0_, f32[256,256]{1,0:T(8,128)S(1)} %collective-permute-done.43.refs_1_, f32[256,256]{1,0:T(8,128)S(1)} %collective-permute-done.44.refs_2_, f32[256,256]{1,0:T(8,128)S(1)} %collective-permute-done.45.refs_3_, ...), custom_call_target="tpu_custom_call" | custom-call | flops 1 | bytes 1 | tf_op jit(solution)/shard_map/place/pallas_call | solution.py:43
  (122 shorter events, 47.0 us)
Async XLA Ops:
  1.5 11.6 %collective-permute-start = (f32[256,256]{1,0:T(8,128)S(1)}, f32[256,256]{1,0:T(8,128)}, u32[]{:S(2)}, u32[]{:S(2)}) collective-permute-start(f32[256,256]{1,0:T(8,128)S(1)} %get-tuple-element.142), channel_id=1, source_target_pairs={{0,2},{1,3},{8,10},{9,11},{16,18},{17,19},{24,26},{25,27}} | collective-permute-start | bytes 786440 | tf_op jit(solution)/shard_map/ppermute | solution.py:319
  7.1 14.8 %collective-permute-start.3 = (f32[256,256]{1,0:T(8,128)S(1)}, f32[256,256]{1,0:T(8,128)}, u32[]{:S(2)}, u32[]{:S(2)}) collective-permute-start(f32[256,256]{1,0:T(8,128)S(1)} %get-tuple-element.138), channel_id=1, source_target_pairs={{0,2},{1,3},{8,10},{9,11},{16,18},{17,19},{24,26},{25,27}} | collective-permute-start | bytes 786440 | tf_op jit(solution)/shard_map/ppermute | solution.py:319
  9.1 15.2 %collective-permute-start.6 = (f32[256,256]{1,0:T(8,128)S(1)}, f32[256,256]{1,0:T(8,128)}, u32[]{:S(2)}, u32[]{:S(2)}) collective-permute-start(f32[256,256]{1,0:T(8,128)S(1)} %get-tuple-element.134), channel_id=1, source_target_pairs={{0,2},{1,3},{8,10},{9,11},{16,18},{17,19},{24,26},{25,27}} | collective-permute-start | bytes 786440 | tf_op jit(solution)/shard_map/ppermute | solution.py:319
  13.1 12.6 %collective-permute-start.1 = (f32[256,256]{1,0:T(8,128)}, f32[256,256]{1,0:T(8,128)}, u32[]{:S(2)}, u32[]{:S(2)}) collective-permute-start(f32[256,256]{1,0:T(8,128)} %collective-permute-done), channel_id=1, source_target_pairs={{2,4},{3,5},{10,12},{11,13},{18,20},{19,21},{26,28},{27,29}} | collective-permute-start | bytes 786440 | tf_op jit(solution)/shard_map/ppermute | solution.py:319
  19.9 10.7 %collective-permute-start.11 = (f32[256,256]{1,0:T(8,128)}, f32[256,256]{1,0:T(8,128)}, u32[]{:S(2)}, u32[]{:S(2)}) collective-permute-start(f32[256,256]{1,0:T(8,128)} %select_select_fusion.6), channel_id=1, source_target_pairs={{0,2},{1,3},{8,10},{9,11},{16,18},{17,19},{24,26},{25,27}} | collective-permute-start | bytes 786440 | tf_op jit(solution)/shard_map/ppermute | solution.py:319
  27.1 13.5 %collective-permute-start.5 = (f32[512,256]{1,0:T(8,128)S(1)}, f32[512,256]{1,0:T(8,128)S(1)}, u32[]{:S(2)}, u32[]{:S(2)}) collective-permute-start(f32[512,256]{1,0:T(8,128)S(1)} %pad_maximum_fusion.blocks), channel_id=1, source_target_pairs={{0,8},{1,9},{8,0},{9,1}} | collective-permute-start | bytes 1572872 | tf_op jit(solution)/shard_map/ppermute | solution.py:319
  45.2 14.0 %collective-permute-start.16 = (f32[256,256]{1,0:T(8,128)S(1)}, f32[256,256]{1,0:T(8,128)S(1)}, u32[]{:S(2)}, u32[]{:S(2)}) collective-permute-start(f32[256,256]{1,0:T(8,128)S(1)} %get-tuple-element.157.v0), channel_id=1, source_target_pairs={{0,16},{1,17},{2,18},{3,19},{4,20},{5,21},{6,22},{7,23},{8,24},{9,... | collective-permute-start | bytes 786440 | tf_op jit(solution)/shard_map/ppermute | solution.py:319
  45.3 14.0 %collective-permute-start.17 = (f32[256,256]{1,0:T(8,128)S(1)}, f32[256,256]{1,0:T(8,128)S(1)}, u32[]{:S(2)}, u32[]{:S(2)}) collective-permute-start(f32[256,256]{1,0:T(8,128)S(1)} %get-tuple-element.157.v0), channel_id=1, source_target_pairs={{0,24},{1,25},{2,26},{3,27},{4,28},{5,29},{6,30},{7,31},{8,16},{9,... | collective-permute-start | bytes 786440 | tf_op jit(solution)/shard_map/ppermute | solution.py:319
  47.2 12.1 %collective-permute-start.19 = (f32[256,256]{1,0:T(8,128)S(1)}, f32[256,256]{1,0:T(8,128)S(1)}, u32[]{:S(2)}, u32[]{:S(2)}) collective-permute-start(f32[256,256]{1,0:T(8,128)S(1)} %copy-done.7), channel_id=1, source_target_pairs={{4,6},{5,7},{12,14},{13,15},{20,22},{21,23},{28,30},{29,31}} | collective-permute-start | bytes 786440 | tf_op jit(solution)/shard_map/ppermute | solution.py:319
  64.9 12.0 %collective-permute-start.21 = (f32[256,256]{1,0:T(8,128)S(1)}, f32[256,256]{1,0:T(8,128)S(1)}, u32[]{:S(2)}, u32[]{:S(2)}) collective-permute-start(f32[256,256]{1,0:T(8,128)S(1)} %select_select_fusion), channel_id=1, source_target_pairs={{0,16},{1,17},{2,18},{3,19},{4,20},{5,21},{6,22},{7,23},{8,24},{9,... | collective-permute-start | bytes 786440 | tf_op jit(solution)/shard_map/ppermute | solution.py:319
  65.1 14.1 %collective-permute-start.25 = (f32[256,256]{1,0:T(8,128)S(1)}, f32[256,256]{1,0:T(8,128)S(1)}, u32[]{:S(2)}, u32[]{:S(2)}) collective-permute-start(f32[256,256]{1,0:T(8,128)S(1)} %get-tuple-element.187), channel_id=1, source_target_pairs={{0,2},{1,3},{2,0},{3,1},{4,6},{5,7},{6,4},{7,5},{8,10},{9,11},{10,... | collective-permute-start | bytes 786440 | tf_op jit(solution)/shard_map/ppermute | solution.py:319
  67.3 9.5 %collective-permute-start.22 = (f32[128,256]{1,0:T(8,128)S(1)}, f32[128,256]{1,0:T(8,128)S(1)}, u32[]{:S(2)}, u32[]{:S(2)}) collective-permute-start(f32[128,256]{1,0:T(8,128)S(1)} %get-tuple-element.182), channel_id=1, source_target_pairs={{0,8},{1,9},{2,10},{3,11},{4,12},{5,13},{6,14},{7,15},{8,0},{9,1},... | collective-permute-start | bytes 393224 | tf_op jit(solution)/shard_map/ppermute | solution.py:319
  67.9 11.3 %collective-permute-start.23 = (f32[128,256]{1,0:T(8,128)S(1)}, f32[128,256]{1,0:T(8,128)S(1)}, u32[]{:S(2)}, u32[]{:S(2)}) collective-permute-start(f32[128,256]{1,0:T(8,128)S(1)} %get-tuple-element.183), channel_id=1, source_target_pairs={{0,16},{1,17},{2,18},{3,19},{4,20},{5,21},{6,22},{7,23},{8,24},{9,... | collective-permute-start | bytes 393224 | tf_op jit(solution)/shard_map/ppermute | solution.py:319
  69.0 10.2 %collective-permute-start.24 = (f32[128,256]{1,0:T(8,128)S(1)}, f32[128,256]{1,0:T(8,128)S(1)}, u32[]{:S(2)}, u32[]{:S(2)}) collective-permute-start(f32[128,256]{1,0:T(8,128)S(1)} %get-tuple-element.184), channel_id=1, source_target_pairs={{0,24},{1,25},{2,26},{3,27},{4,28},{5,29},{6,30},{7,31},{8,16},{9,... | collective-permute-start | bytes 393224 | tf_op jit(solution)/shard_map/ppermute | solution.py:319
  80.3 19.8 %collective-permute-start.26 = (f32[256,256]{1,0:T(8,128)S(1)}, f32[256,256]{1,0:T(8,128)S(1)}, u32[]{:S(2)}, u32[]{:S(2)}) collective-permute-start(f32[256,256]{1,0:T(8,128)S(1)} %add.43), channel_id=1, source_target_pairs={{0,4},{1,5},{2,6},{3,7},{4,0},{5,1},{6,2},{7,3},{8,12},{9,13},{10,... | collective-permute-start | bytes 786440 | tf_op jit(solution)/shard_map/ppermute | solution.py:319
  81.0 19.1 %collective-permute-start.29 = (f32[256,256]{1,0:T(8,128)S(1)}, f32[256,256]{1,0:T(8,128)S(1)}, u32[]{:S(2)}, u32[]{:S(2)}) collective-permute-start(f32[256,256]{1,0:T(8,128)S(1)} %get-tuple-element.198), channel_id=1, source_target_pairs={{0,8},{1,9},{2,10},{3,11},{4,12},{5,13},{6,14},{7,15},{8,0},{9,1},... | collective-permute-start | bytes 786440 | tf_op jit(solution)/shard_map/ppermute | solution.py:319
  82.3 17.8 %collective-permute-start.30 = (f32[256,256]{1,0:T(8,128)S(1)}, f32[256,256]{1,0:T(8,128)S(1)}, u32[]{:S(2)}, u32[]{:S(2)}) collective-permute-start(f32[256,256]{1,0:T(8,128)S(1)} %get-tuple-element.199), channel_id=1, source_target_pairs={{0,16},{1,17},{2,18},{3,19},{4,20},{5,21},{6,22},{7,23},{8,24},{9,... | collective-permute-start | bytes 786440 | tf_op jit(solution)/shard_map/ppermute | solution.py:319
  83.2 16.9 %collective-permute-start.31 = (f32[256,256]{1,0:T(8,128)S(1)}, f32[256,256]{1,0:T(8,128)S(1)}, u32[]{:S(2)}, u32[]{:S(2)}) collective-permute-start(f32[256,256]{1,0:T(8,128)S(1)} %get-tuple-element.200), channel_id=1, source_target_pairs={{0,24},{1,25},{2,26},{3,27},{4,28},{5,29},{6,30},{7,31},{8,16},{9,... | collective-permute-start | bytes 786440 | tf_op jit(solution)/shard_map/ppermute | solution.py:319
  86.3 13.8 %collective-permute-start.28 = (f32[128,256]{1,0:T(8,128)S(1)}, f32[128,256]{1,0:T(8,128)S(1)}, u32[]{:S(2)}, u32[]{:S(2)}) collective-permute-start(f32[128,256]{1,0:T(8,128)S(1)} %add.47), channel_id=1, source_target_pairs={{0,4},{1,5},{2,6},{3,7},{4,0},{5,1},{6,2},{7,3},{8,12},{9,13},{10,... | collective-permute-start | bytes 393224 | tf_op jit(solution)/shard_map/ppermute | solution.py:319
  101.5 13.2 %collective-permute-start.32 = (f32[256,256]{1,0:T(8,128)S(1)}, f32[256,256]{1,0:T(8,128)S(1)}, u32[]{:S(2)}, u32[]{:S(2)}) collective-permute-start(f32[256,256]{1,0:T(8,128)S(1)} %add_add_fusion), channel_id=1, source_target_pairs={{0,0},{1,1},{2,20},{3,21},{4,2},{5,3},{6,22},{7,23},{8,8},{9,9},{1... | collective-permute-start | bytes 786440 | tf_op jit(solution)/shard_map/ppermute | solution.py:319
  102.2 12.5 %collective-permute-start.33 = (f32[256,256]{1,0:T(8,128)S(1)}, f32[256,256]{1,0:T(8,128)S(1)}, u32[]{:S(2)}, u32[]{:S(2)}) collective-permute-start(f32[256,256]{1,0:T(8,128)S(1)} %get-tuple-element.207), channel_id=1, source_target_pairs={{0,2},{1,3},{2,0},{3,1},{4,6},{5,7},{6,4},{7,5},{8,10},{9,11},{10,... | collective-permute-start | bytes 786440 | tf_op jit(solution)/shard_map/ppermute | solution.py:319
  103.8 10.9 %collective-permute-start.34 = (f32[256,256]{1,0:T(8,128)S(1)}, f32[256,256]{1,0:T(8,128)S(1)}, u32[]{:S(2)}, u32[]{:S(2)}) collective-permute-start(f32[256,256]{1,0:T(8,128)S(1)} %broadcast_select_fusion.refs_4_.c0), channel_id=1, source_target_pairs={{0,8},{1,9},{2,10},{3,11},{4,12},{5,13},{6,14},{7,15},{8,0},{9,1},... | collective-permute-start | bytes 786440 | tf_op jit(solution)/shard_map/ppermute | solution.py:319
  123.2 12.7 %collective-permute-start.43 = (f32[256,256]{1,0:T(8,128)S(1)}, f32[256,256]{1,0:T(8,128)S(1)}, u32[]{:S(2)}, u32[]{:S(2)}) collective-permute-start(f32[256,256]{1,0:T(8,128)S(1)} %end.1.refs_0_), channel_id=1, source_target_pairs={{0,2},{1,3},{2,0},{3,1},{4,6},{5,7},{6,4},{7,5},{8,10},{9,11},{10,... | collective-permute-start | bytes 786440 | tf_op jit(solution)/shard_map/ppermute | solution.py:319
  123.2 14.9 %collective-permute-start.44 = (f32[256,256]{1,0:T(8,128)S(1)}, f32[256,256]{1,0:T(8,128)S(1)}, u32[]{:S(2)}, u32[]{:S(2)}) collective-permute-start(f32[256,256]{1,0:T(8,128)S(1)} %end.1.refs_0_), channel_id=1, source_target_pairs={{0,4},{1,5},{2,6},{3,7},{4,0},{5,1},{6,2},{7,3},{8,12},{9,13},{10,... | collective-permute-start | bytes 786440 | tf_op jit(solution)/shard_map/ppermute | solution.py:319
  (35 other events, 251.5 us)

commit v5 on v4

--- a/solution.py
+++ b/solution.py
@@ -145,7 +145,8 @@
 
 
 def row_kernel(n_pairs, ids, low_1, low_2, high_1, high_2, v0, v1, v2, v3, adjoint, *refs):
-    shares, product_ref, remaining = refs[:n_pairs], refs[-2], refs[-1]
+    arrived, refs = refs[:n_pairs], refs[n_pairs:]
+    evens, (odds, product_ref, carried, remaining) = refs[:-4], refs[-4:]
     pair, row = ids[PAIR], ids[ROW]
     x_is_0 = row % 2 == 0
     near = row // 2 == pair % 2
@@ -168,8 +169,13 @@
             product += dot3((high_1[upper, :], high_2[upper, :]), panel_high)
         remaining[block] = jnp.where(pair == 0, adjoint[at, :NB], 0.0) - product
         product_ref[at, :] = product
-    for d in range(n_pairs):
-        shares[d][...] = remaining[pair ^ d]
+    for d in range(0, n_pairs, 2):
+        evens[d // 2][...] = remaining[pair ^ d]
+        odds[d // 2 * NB : (d // 2 + 1) * NB, :] = remaining[pair ^ (d + 1)]
+    value = arrived[0][...]
+    for p in range(1, n_pairs):
+        value = jnp.where(pair == p, arrived[p][...], value)
+    carried[...] = value
 
 
 def sum_kernel(n_rows, ids, turned, turned_other, product_ref, low, *refs):
@@ -208,7 +214,7 @@
     total_ref, solved = refs[-2:]
     total = shares[0][...]
     for ref in shares[1:]:
-        total = total + ref[...]
+        total = total + ref[:NB, :]
     total = total - owned[...].T
     inverse, _ = carried_blocks(ids, carried)
     total_ref[...] = total
@@ -268,9 +274,10 @@
         cross = quick(inv1_t, z10)
         k1 = tril(a11 - quick(inv1_t, z11))
         e1 = diagonal_adjoint(tril(l1), k1, inv1_t, inv1)
-        rest = a10 - quick(e1 + e1.T, link) - cross
-        g0 = quick(rest, inv0)
-        k0 = tril(a00 - quick(inv0_t, z00 - quick(link.T, cross) + quick(rest.T, link)))
+        early = quick(a10 - cross, inv0)
+        earlier = a00 - quick(inv0_t, z00 - quick(link.T, cross))
+        g0 = early - quick(e1 + e1.T, quick(link, inv0))
+        k0 = tril(earlier - quick(g0.T, link))
         e0 = diagonal_adjoint(tril(l0), k0, inv0_t, inv0)
         out_ref[...] = jnp.where(
             in_first_row, jnp.where(first, e0, 0.0), jnp.where(first, g0, e1)
@@ -409,18 +416,24 @@
 
     rest = together(*held, turned, low, *block_sums, *carried)
     held, (turned, low), rest = rest[:n_rows], rest[n_rows : n_rows + 2], rest[n_rows + 2 :]
-    block_sums, carried = rest[:n_rows], here(rest[n_rows:])
+    block_sums, carried = rest[:n_rows], rest[n_rows:]
     turned_other, blocks_other, across_other = swap(turned), swap(blocks), swap(across)
 
     height = 2 * NB // n_rows
-    *shares, product = call(
+    *evens, odds, product, carried = call(
         functools.partial(row_kernel, n_pairs),
         "rows",
-        (SQUARE,) * n_pairs + (jax.ShapeDtypeStruct((local_rows, NB), jnp.float32),),
+        (SQUARE,) * middle
+        + (
+            jax.ShapeDtypeStruct((middle * NB, NB), jnp.float32),
+            jax.ShapeDtypeStruct((local_rows, NB), jnp.float32),
+            SQUARE,
+        ),
         ids,
         *masked,
         *held,
         adjoint,
+        *carried,
         scratch=(pltpu.VMEM((n_pairs, NB, NB), jnp.float32),),
     )
     slices = call(
@@ -434,12 +447,12 @@
         low,
         scratch=(pltpu.VMEM((n_rows, height, NB), jnp.float32),),
     )
-    rest = together(blocks_other, across_other, carried, *slices, *shares, *block_sums)
-    (blocks_other, across_other, carried), rest = rest[:3], rest[3:]
-    slices, shares, block_sums = (
+    rest = together(blocks_other, across_other, carried, odds, *slices, *evens, *block_sums)
+    (blocks_other, across_other, carried, odds), rest = rest[:4], rest[4:]
+    slices, evens, block_sums = (
         rest[:n_rows],
-        rest[n_rows : n_rows + n_pairs],
-        rest[n_rows + n_pairs :],
+        rest[n_rows : n_rows + middle],
+        rest[n_rows + middle :],
     )
 
     def folded(values, bit):
@@ -450,19 +463,17 @@
     def added(kept, moved, bit):
         return {d: value + moved[d ^ bit] for d, value in kept.items()}
 
-    nearest_share, shares = shares[1], {d: x for d, x in enumerate(shares) if d != 1}
-    kept, moved = folded(shares, 1)
     slices = [slices[0]] + [swap_rows(slices[d], d) for d in range(1, n_rows)]
-    carried = jnp.where(row_id < 2, carried, swap_rows(carried, 2))
-    rest = together(
-        carried, nearest_share, *block_sums, *slices, *kept.values(), *moved.values()
-    )
-    (carried, nearest_share), rest = rest[:2], rest[2:]
+    beyond = send(carried, lambda r, p, k: (r + 2, p, k) if r < 2 else None)
+    carried = jnp.where(row_id < 2, carried, beyond)
+    rest = together(carried, swap_pairs(odds, 1), *block_sums, *slices, *evens)
+    (carried, odds), rest = rest[:2], rest[2:]
     block_sums, rest = rest[:n_rows], rest[n_rows:]
-    total, rest = sum(rest[1:n_rows], rest[0]), rest[n_rows:]
-    kept, moved = dict(zip(kept, rest)), dict(zip(moved, rest[len(kept) :]))
-    own_share = kept.pop(0)
-    shares = added(kept, moved, 1)
+    total, evens = sum(rest[1:n_rows], rest[0]), rest[n_rows:]
+    own_share = evens[0]
+    shares = {
+        2 * i: evens[i] + odds[i * NB : (i + 1) * NB] for i in range(1, middle)
+    }
     bit = 2
     while bit < n_pairs // 2:
         shares[0] = jnp.zeros_like(own_share)
@@ -470,14 +481,19 @@
         own_share = own_share + shares.pop(0)
         bit *= 2
     moved = swap_pairs(shares[bit], bit)
+    def toward_first(value, bit):
+        return send(
+            value, lambda r, p, k: (r, p - bit, k) if p & bit and not p & (bit - 1) else None
+        )
+
     bit = 1
     while bit < n_pairs // 2:
-        total = total + swap_pairs(total, bit)
+        total = total + toward_first(total, bit)
         bit *= 2
-    total_other = swap_pairs(total, bit)
+    total_other = toward_first(total, bit)
     block_sums = [block_sums[0]] + [swap_rows(block_sums[d], d) for d in range(1, n_rows)]
-    rest = together(own_share, moved, nearest_share, carried, total, total_other, *block_sums)
-    own_share, moved, nearest_share, carried, total, total_other = rest[:6]
+    rest = together(own_share, moved, odds, carried, total, total_other, *block_sums)
+    own_share, moved, odds, carried, total, total_other = rest[:6]
     total, owned = total + total_other, sum(rest[7:], rest[6])
 
     def owner(r, p, k):
@@ -486,11 +502,13 @@
 
     owned = send(owned, owner)
     carried = [carried, swap_rows(carried, 1)]
-    nearest_share = swap_pairs(nearest_share, 1)
-    sums = [total] + [swap_rows(total, d) for d in range(1, n_rows)]
-    owned, nearest_share, *rest = together(owned, nearest_share, *carried, *sums)
+    sums = [total] + [
+        send(total, lambda r, p, k, d=d: (r ^ d, p, k) if p == 0 and r ^ d < 2 else None)
+        for d in range(1, n_rows)
+    ]
+    owned, *rest = together(owned, *carried, *sums)
     carried, sums = rest[:2], jnp.concatenate(rest[2:], 0)
-    shares = own_share, moved, nearest_share
+    shares = own_share, moved, odds
 
     mine, solved = call(
         functools.partial(solve_kernel, 3), "solve", (SQUARE, SQUARE), ids, *shares, owned, *carried

time: 150 us -> 148 us (0.987)
  waiting for transfers between devices: 70 us -> 67.6 us
    ppermute x49 -> x48, waiting for transfers between devices: 70 us -> 67.6 us  [send(): return lax.ppermute(value, ('row', 'col'), edges)]
    ppermute x49 -> x48, starting transfers between devices: 51.4 us -> 51.9 us  [send(): return lax.ppermute(value, ('row', 'col'), edges)]
  transfers between devices with their start and end apart: 49 -> 48, of which waited for: 17 -> 18; matrix products, arithmetic and copies ran while one was open for 3% -> 2% of each run, Pallas kernels for 9% -> 9%
where the time goes in v5:
time: 148 us
  waiting for transfers between devices  67.6 us (46%)
  starting transfers between devices  51.9 us (35%)
  Pallas kernels  20.9 us (14%)
  local copies, waits for them, and re-layouts  3.73 us (3%)
  other arithmetic  2.98 us (2%)
    ppermute x48, waiting for transfers between devices, send(): return lax.ppermute(value, ('row', 'col'), edges)  67.6 us
    ppermute x48, starting transfers between devices, send(): return lax.ppermute(value, ('row', 'col'), edges)  51.9 us
    pallas_call x8, Pallas kernels, call(): pl.pallas_call(kernel, out_shape=out_shape, in_specs=[pl.BlockSpec(memory...  20.9 us
  transfers between devices with their start and end apart: 48, of which 18 were waited for; matrix products, arithmetic and copies ran while one was open for 2% of the time, Pallas kernels for 9%

profile of v5, /device:TPU:0, one launch (start us, length us, event | category | flops | bytes accessed | tf_op | source)
XLA Modules:
  0.0 147.6 jit_solution(12656653306414961490)
XLA Ops:
  0.0 2.1 %fusion = (f32[256,256]{1,0:T(8,128)S(1)}, f32[256,256]{1,0:T(8,128)}, f32[256,256]{1,0:T(8,128)S(1)}, f32[256,256]{1,0:T(8,128)S(1)}) fusion(f32[1024,512]{1,0:T(8,128)} %param.2), kind=kLoop, calls=%fused_computation.18 | loop fusion | bytes 2097152 | tf_op jit(solution)/shard_map/slice | solution.py:338
  2.1 5.6 %collective-permute-start = (f32[256,256]{1,0:T(8,128)S(1)}, f32[256,256]{1,0:T(8,128)}, u32[]{:S(2)}, u32[]{:S(2)}) collective-permute-start(f32[256,256]{1,0:T(8,128)S(1)} %get-tuple-element.139), channel_id=1, source_target_pairs={{0,2},{1,3},{8,10},{9,11},{16,18},{17,19},{24,26},{25,27}} | collective-permute-start | bytes 786440 | tf_op jit(solution)/shard_map/ppermute | solution.py:326
  9.8 2.0 %collective-permute-start.6 = (f32[256,256]{1,0:T(8,128)}, f32[256,256]{1,0:T(8,128)}, u32[]{:S(2)}, u32[]{:S(2)}) collective-permute-start(f32[256,256]{1,0:T(8,128)} %get-tuple-element.131), channel_id=1, source_target_pairs={{0,2},{1,3},{8,10},{9,11},{16,18},{17,19},{24,26},{25,27}} | collective-permute-start | bytes 786440 | tf_op jit(solution)/shard_map/ppermute | solution.py:326
  15.2 4.6 %inverse.1 = f32[256,256]{1,0:T(8,128)S(1)} custom-call(s32[3]{0:T(128)S(1)} %pad_add_fusion.ids, f32[256,256]{1,0:T(8,128)S(1)} %get-tuple-element.117.block_ref), custom_call_target="tpu_custom_call" | custom-call | flops 1 | bytes 1 | tf_op jit(solution)/shard_map/inverse/pallas_call | solution.py:43
  22.5 2.6 %collective-permute-done.6 = f32[256,256]{1,0:T(8,128)} collective-permute-done((f32[256,256]{1,0:T(8,128)}, f32[256,256]{1,0:T(8,128)}, u32[]{:S(2)}, u32[]{:S(2)}) %collective-permute-start.6) | collective-permute-done | bytes 262176 | tf_op jit(solution)/shard_map/ppermute | solution.py:326
  27.9 3.4 %collective-permute-start.5 = (f32[512,256]{1,0:T(8,128)S(1)}, f32[512,256]{1,0:T(8,128)}, u32[]{:S(2)}, u32[]{:S(2)}) collective-permute-start(f32[512,256]{1,0:T(8,128)S(1)} %pad_maximum_fusion.blocks), channel_id=1, source_target_pairs={{0,8},{1,9},{8,0},{9,1}} | collective-permute-start | bytes 1572872 | tf_op jit(solution)/shard_map/ppermute | solution.py:326
  34.6 7.0 %collective-permute-done.5.across = f32[512,256]{1,0:T(8,128)} collective-permute-done((f32[512,256]{1,0:T(8,128)S(1)}, f32[512,256]{1,0:T(8,128)}, u32[]{:S(2)}, u32[]{:S(2)}) %collective-permute-start.5) | collective-permute-done | bytes 524320 | tf_op jit(solution)/shard_map/ppermute | solution.py:326
  49.0 2.5 %masked.1 = (bf16[1024,512]{1,0:T(8,128)(2,1)S(1)}, bf16[1024,512]{1,0:T(8,128)(2,1)S(1)}, bf16[512,512]{1,0:T(8,128)(2,1)S(1)}, bf16[512,512]{1,0:T(8,128)(2,1)S(1)}) custom-call(s32[3]{0:T(128)S(1)} %pad_add_fusion.ids, f32[1024,512]{1,0:T(8,128)S(1)} %copy-done, f32[1024,512]{1,0:T(8,128)} %collective-permute-done.15.other), custom_call_target="tpu_custom_call" | custom-call | flops 1 | bytes 1 | tf_op jit(solution)/shard_map/masked/pallas_call | solution.py:43
  51.5 2.1 %columns.1 = (f32[256,1024]{1,0:T(8,128)S(1)}, f32[256,512]{1,0:T(8,128)S(1)}, f32[256,256]{1,0:T(8,128)S(1)}, f32[256,256]{1,0:T(8,128)S(1)}, f32[256,256]{1,0:T(8,128)S(1)}, /*index=5*/f32[256,256]{1,0:T(8,128)S(1)}) custom-call(s32[3]{0:T(128)S(1)} %pad_add_fusion.ids, bf16[1024,512]{1,0:T(8,128)(2,1)S(1)} %get-tuple-element.122.low_1, ...), custom_call_target="tpu_custom_call" | custom-call | flops 1 | bytes 1 | tf_op jit(solution)/shard_map/columns/pallas_call | solution.py:43
  53.7 6.4 %collective-permute-done.17.v2 = f32[256,256]{1,0:T(8,128)S(1)} collective-permute-done((f32[256,256]{1,0:T(8,128)S(1)}, f32[256,256]{1,0:T(8,128)S(1)}, u32[]{:S(2)}, u32[]{:S(2)}) %collective-permute-start.17) | collective-permute-done | bytes 262176 | tf_op jit(solution)/shard_map/ppermute | solution.py:326
  60.7 2.2 %rows.1 = (f32[256,256]{1,0:T(8,128)S(1)}, f32[256,256]{1,0:T(8,128)S(1)}, f32[512,256]{1,0:T(8,128)S(1)}, f32[1024,256]{1,0:T(8,128)S(1)}, f32[256,256]{1,0:T(8,128)S(1)}) custom-call(s32[3]{0:T(128)S(1)} %pad_add_fusion.ids, bf16[1024,512]{1,0:T(8,128)(2,1)S(1)} %get-tuple-element.122.low_1, bf16[1024,512]{1,0:T(8,128)(2,1)S(1)} %get-tuple-element.123.low_2, ...), custom_call_target="tpu_custom_call" | custom-call | flops 1 | bytes 1 | tf_op jit(solution)/shard_map/rows/pallas_call | solution.py:43
  65.4 3.4 %collective-permute-start.21 = (f32[256,256]{1,0:T(8,128)S(1)}, f32[256,256]{1,0:T(8,128)S(1)}, u32[]{:S(2)}, u32[]{:S(2)}) collective-permute-start(f32[256,256]{1,0:T(8,128)S(1)} %get-tuple-element.172), channel_id=1, source_target_pairs={{0,16},{1,17},{2,18},{3,19},{4,20},{5,21},{6,22},{7,23},{8,24},{9,... | collective-permute-start | bytes 786440 | tf_op jit(solution)/shard_map/ppermute | solution.py:326
  69.4 3.0 %collective-permute-start.25 = (f32[128,256]{1,0:T(8,128)S(1)}, f32[128,256]{1,0:T(8,128)S(1)}, u32[]{:S(2)}, u32[]{:S(2)}) collective-permute-start(f32[128,256]{1,0:T(8,128)S(1)} %get-tuple-element.181), channel_id=1, source_target_pairs={{0,24},{1,25},{2,26},{3,27},{4,28},{5,29},{6,30},{7,31},{8,16},{9,... | collective-permute-start | bytes 393224 | tf_op jit(solution)/shard_map/ppermute | solution.py:326
  72.3 5.9 %collective-permute-done.21 = f32[256,256]{1,0:T(8,128)S(1)} collective-permute-done((f32[256,256]{1,0:T(8,128)S(1)}, f32[256,256]{1,0:T(8,128)S(1)}, u32[]{:S(2)}, u32[]{:S(2)}) %collective-permute-start.21) | collective-permute-done | bytes 262176 | tf_op jit(solution)/shard_map/ppermute | solution.py:326
  83.8 2.5 %collective-permute-start.30 = (f32[256,256]{1,0:T(8,128)S(1)}, f32[256,256]{1,0:T(8,128)S(1)}, u32[]{:S(2)}, u32[]{:S(2)}) collective-permute-start(f32[256,256]{1,0:T(8,128)S(1)} %get-tuple-element.194), channel_id=1, source_target_pairs={{0,16},{1,17},{2,18},{3,19},{4,20},{5,21},{6,22},{7,23},{8,24},{9,... | collective-permute-start | bytes 786440 | tf_op jit(solution)/shard_map/ppermute | solution.py:326
  87.2 3.5 %collective-permute-done.27 = f32[128,256]{1,0:T(8,128)S(1)} collective-permute-done((f32[128,256]{1,0:T(8,128)S(1)}, f32[128,256]{1,0:T(8,128)S(1)}, u32[]{:S(2)}, u32[]{:S(2)}) %collective-permute-start.27) | collective-permute-done | bytes 131104 | tf_op jit(solution)/shard_map/ppermute | solution.py:326
  92.1 6.5 %collective-permute-done.28 = f32[128,256]{1,0:T(8,128)S(1)} collective-permute-done((f32[128,256]{1,0:T(8,128)S(1)}, f32[128,256]{1,0:T(8,128)S(1)}, u32[]{:S(2)}, u32[]{:S(2)}) %collective-permute-start.28) | collective-permute-done | bytes 131104 | tf_op jit(solution)/shard_map/ppermute | solution.py:326
  100.0 3.4 %collective-permute-start.34 = (f32[128,256]{1,0:T(8,128)S(1)}, f32[128,256]{1,0:T(8,128)S(1)}, u32[]{:S(2)}, u32[]{:S(2)}) collective-permute-start(f32[128,256]{1,0:T(8,128)S(1)} %add.51), channel_id=1, source_target_pairs={{0,8},{1,9},{8,0},{9,1}} | collective-permute-start | bytes 393224 | tf_op jit(solution)/shard_map/ppermute | solution.py:326
  106.0 3.2 %collective-permute-done.34 = f32[128,256]{1,0:T(8,128)S(1)} collective-permute-done((f32[128,256]{1,0:T(8,128)S(1)}, f32[128,256]{1,0:T(8,128)S(1)}, u32[]{:S(2)}, u32[]{:S(2)}) %collective-permute-start.34) | collective-permute-done | bytes 131104 | tf_op jit(solution)/shard_map/ppermute | solution.py:326
  109.2 3.6 %collective-permute-done.35 = f32[128,256]{1,0:T(8,128)S(1)} collective-permute-done((f32[128,256]{1,0:T(8,128)S(1)}, f32[128,256]{1,0:T(8,128)S(1)}, u32[]{:S(2)}, u32[]{:S(2)}) %collective-permute-start.35) | collective-permute-done | bytes 131104 | tf_op jit(solution)/shard_map/ppermute | solution.py:326
  116.3 4.9 %end.1.refs_0_ = f32[256,256]{1,0:T(8,128)S(1)} custom-call(s32[3]{0:T(128)S(1)} %pad_add_fusion.ids, f32[256,256]{1,0:T(8,128)S(1)} %get-tuple-element.209.total, f32[256,256]{1,0:T(8,128)S(1)} %get-tuple-element.210.solved, f32[256,256]{1,0:T(8,128)S(1)} %collective-permute-done.37.second, f32[256,256]{1,0:T(8,128)S(1)} %broadcast_select_fusion.refs_4_.c0, ...), custom_call_target="tpu_custom_call" | custom-call | flops 1 | bytes 1 | tf_op jit(solution)/shard_map/end/pallas_call | solution.py:43
  122.8 8.4 %collective-permute-done.42.refs_1_ = f32[256,256]{1,0:T(8,128)S(1)} collective-permute-done((f32[256,256]{1,0:T(8,128)S(1)}, f32[256,256]{1,0:T(8,128)S(1)}, u32[]{:S(2)}, u32[]{:S(2)}) %collective-permute-start.42) | collective-permute-done | bytes 262176 | tf_op jit(solution)/shard_map/ppermute | solution.py:326
  131.2 5.4 %collective-permute-done.43.refs_2_ = f32[256,256]{1,0:T(8,128)S(1)} collective-permute-done((f32[256,256]{1,0:T(8,128)S(1)}, f32[256,256]{1,0:T(8,128)S(1)}, u32[]{:S(2)}, u32[]{:S(2)}) %collective-permute-start.43) | collective-permute-done | bytes 262176 | tf_op jit(solution)/shard_map/ppermute | solution.py:326
  137.1 7.0 %collective-permute-done.44.refs_3_ = f32[256,256]{1,0:T(8,128)S(1)} collective-permute-done((f32[256,256]{1,0:T(8,128)S(1)}, f32[256,256]{1,0:T(8,128)S(1)}, u32[]{:S(2)}, u32[]{:S(2)}) %collective-permute-start.44) | collective-permute-done | bytes 262176 | tf_op jit(solution)/shard_map/ppermute | solution.py:326
  (121 shorter events, 46.0 us)
Async XLA Ops:
  2.1 11.6 %collective-permute-start = (f32[256,256]{1,0:T(8,128)S(1)}, f32[256,256]{1,0:T(8,128)}, u32[]{:S(2)}, u32[]{:S(2)}) collective-permute-start(f32[256,256]{1,0:T(8,128)S(1)} %get-tuple-element.139), channel_id=1, source_target_pairs={{0,2},{1,3},{8,10},{9,11},{16,18},{17,19},{24,26},{25,27}} | collective-permute-start | bytes 786440 | tf_op jit(solution)/shard_map/ppermute | solution.py:326
  7.8 13.4 %collective-permute-start.3 = (f32[256,256]{1,0:T(8,128)S(1)}, f32[256,256]{1,0:T(8,128)}, u32[]{:S(2)}, u32[]{:S(2)}) collective-permute-start(f32[256,256]{1,0:T(8,128)S(1)} %get-tuple-element.135), channel_id=1, source_target_pairs={{0,2},{1,3},{8,10},{9,11},{16,18},{17,19},{24,26},{25,27}} | collective-permute-start | bytes 786440 | tf_op jit(solution)/shard_map/ppermute | solution.py:326
  9.8 15.3 %collective-permute-start.6 = (f32[256,256]{1,0:T(8,128)}, f32[256,256]{1,0:T(8,128)}, u32[]{:S(2)}, u32[]{:S(2)}) collective-permute-start(f32[256,256]{1,0:T(8,128)} %get-tuple-element.131), channel_id=1, source_target_pairs={{0,2},{1,3},{8,10},{9,11},{16,18},{17,19},{24,26},{25,27}} | collective-permute-start | bytes 786440 | tf_op jit(solution)/shard_map/ppermute | solution.py:326
  13.8 12.7 %collective-permute-start.1 = (f32[256,256]{1,0:T(8,128)}, f32[256,256]{1,0:T(8,128)}, u32[]{:S(2)}, u32[]{:S(2)}) collective-permute-start(f32[256,256]{1,0:T(8,128)} %collective-permute-done), channel_id=1, source_target_pairs={{2,4},{3,5},{10,12},{11,13},{18,20},{19,21},{26,28},{27,29}} | collective-permute-start | bytes 786440 | tf_op jit(solution)/shard_map/ppermute | solution.py:326
  19.8 11.5 %collective-permute-start.11 = (f32[256,256]{1,0:T(8,128)S(1)}, f32[256,256]{1,0:T(8,128)S(1)}, u32[]{:S(2)}, u32[]{:S(2)}) collective-permute-start(f32[256,256]{1,0:T(8,128)S(1)} %select_select_fusion.5.refs_0_), channel_id=1, source_target_pairs={{0,2},{1,3},{8,10},{9,11},{16,18},{17,19},{24,26},{25,27}} | collective-permute-start | bytes 786440 | tf_op jit(solution)/shard_map/ppermute | solution.py:326
  21.2 10.9 %collective-permute-start.9 = (f32[256,256]{1,0:T(8,128)}, f32[256,256]{1,0:T(8,128)}, u32[]{:S(2)}, u32[]{:S(2)}) collective-permute-start(f32[256,256]{1,0:T(8,128)} %collective-permute-done.3), channel_id=1, source_target_pairs={{2,4},{3,5},{10,12},{11,13},{18,20},{19,21},{26,28},{27,29}} | collective-permute-start | bytes 786440 | tf_op jit(solution)/shard_map/ppermute | solution.py:326
  27.9 13.6 %collective-permute-start.5 = (f32[512,256]{1,0:T(8,128)S(1)}, f32[512,256]{1,0:T(8,128)}, u32[]{:S(2)}, u32[]{:S(2)}) collective-permute-start(f32[512,256]{1,0:T(8,128)S(1)} %pad_maximum_fusion.blocks), channel_id=1, source_target_pairs={{0,8},{1,9},{8,0},{9,1}} | collective-permute-start | bytes 1572872 | tf_op jit(solution)/shard_map/ppermute | solution.py:326
  32.0 9.5 %collective-permute-start.10 = (f32[256,256]{1,0:T(8,128)}, f32[256,256]{1,0:T(8,128)S(1)}, u32[]{:S(2)}, u32[]{:S(2)}) collective-permute-start(f32[256,256]{1,0:T(8,128)} %collective-permute-done.9), channel_id=1, source_target_pairs={{4,6},{5,7},{12,14},{13,15},{20,22},{21,23},{28,30},{29,31}} | collective-permute-start | bytes 786440 | tf_op jit(solution)/shard_map/ppermute | solution.py:326
  46.0 14.0 %collective-permute-start.17 = (f32[256,256]{1,0:T(8,128)S(1)}, f32[256,256]{1,0:T(8,128)S(1)}, u32[]{:S(2)}, u32[]{:S(2)}) collective-permute-start(f32[256,256]{1,0:T(8,128)S(1)} %get-tuple-element.149.v0), channel_id=1, source_target_pairs={{0,16},{1,17},{2,18},{3,19},{4,20},{5,21},{6,22},{7,23},{8,24},{9,... | collective-permute-start | bytes 786440 | tf_op jit(solution)/shard_map/ppermute | solution.py:326
  46.0 14.0 %collective-permute-start.18 = (f32[256,256]{1,0:T(8,128)S(1)}, f32[256,256]{1,0:T(8,128)S(1)}, u32[]{:S(2)}, u32[]{:S(2)}) collective-permute-start(f32[256,256]{1,0:T(8,128)S(1)} %get-tuple-element.149.v0), channel_id=1, source_target_pairs={{0,24},{1,25},{2,26},{3,27},{4,28},{5,29},{6,30},{7,31},{8,16},{9,... | collective-permute-start | bytes 786440 | tf_op jit(solution)/shard_map/ppermute | solution.py:326
  48.0 12.1 %collective-permute-start.19 = (f32[256,256]{1,0:T(8,128)S(1)}, f32[256,256]{1,0:T(8,128)S(1)}, u32[]{:S(2)}, u32[]{:S(2)}) collective-permute-start(f32[256,256]{1,0:T(8,128)S(1)} %copy-done.2), channel_id=1, source_target_pairs={{4,6},{5,7},{12,14},{13,15},{20,22},{21,23},{28,30},{29,31}} | collective-permute-start | bytes 786440 | tf_op jit(solution)/shard_map/ppermute | solution.py:326
  64.7 15.5 %collective-permute-start.22 = (f32[512,256]{1,0:T(8,128)S(1)}, f32[512,256]{1,0:T(8,128)S(1)}, u32[]{:S(2)}, u32[]{:S(2)}) collective-permute-start(f32[512,256]{1,0:T(8,128)S(1)} %get-tuple-element.173), channel_id=1, source_target_pairs={{0,2},{1,3},{2,0},{3,1},{4,6},{5,7},{6,4},{7,5},{8,10},{9,11},{10,... | collective-permute-start | bytes 1572872 | tf_op jit(solution)/shard_map/ppermute | solution.py:326
  65.4 12.8 %collective-permute-start.21 = (f32[256,256]{1,0:T(8,128)S(1)}, f32[256,256]{1,0:T(8,128)S(1)}, u32[]{:S(2)}, u32[]{:S(2)}) collective-permute-start(f32[256,256]{1,0:T(8,128)S(1)} %get-tuple-element.172), channel_id=1, source_target_pairs={{0,16},{1,17},{2,18},{3,19},{4,20},{5,21},{6,22},{7,23},{8,24},{9,... | collective-permute-start | bytes 786440 | tf_op jit(solution)/shard_map/ppermute | solution.py:326
  69.3 10.9 %collective-permute-start.24 = (f32[128,256]{1,0:T(8,128)S(1)}, f32[128,256]{1,0:T(8,128)S(1)}, u32[]{:S(2)}, u32[]{:S(2)}) collective-permute-start(f32[128,256]{1,0:T(8,128)S(1)} %get-tuple-element.180), channel_id=1, source_target_pairs={{0,16},{1,17},{2,18},{3,19},{4,20},{5,21},{6,22},{7,23},{8,24},{9,... | collective-permute-start | bytes 393224 | tf_op jit(solution)/shard_map/ppermute | solution.py:326
  69.4 10.9 %collective-permute-start.25 = (f32[128,256]{1,0:T(8,128)S(1)}, f32[128,256]{1,0:T(8,128)S(1)}, u32[]{:S(2)}, u32[]{:S(2)}) collective-permute-start(f32[128,256]{1,0:T(8,128)S(1)} %get-tuple-element.181), channel_id=1, source_target_pairs={{0,24},{1,25},{2,26},{3,27},{4,28},{5,29},{6,30},{7,31},{8,16},{9,... | collective-permute-start | bytes 393224 | tf_op jit(solution)/shard_map/ppermute | solution.py:326
  80.3 10.5 %collective-permute-start.27 = (f32[128,256]{1,0:T(8,128)S(1)}, f32[128,256]{1,0:T(8,128)S(1)}, u32[]{:S(2)}, u32[]{:S(2)}) collective-permute-start(f32[128,256]{1,0:T(8,128)S(1)} %add_add_fusion.1), channel_id=1, source_target_pairs={{2,0},{3,1},{6,4},{7,5},{10,8},{11,9},{14,12},{15,13},{18,16},{19,... | collective-permute-start | bytes 393224 | tf_op jit(solution)/shard_map/ppermute | solution.py:326
  81.6 17.0 %collective-permute-start.26 = (f32[256,256]{1,0:T(8,128)S(1)}, f32[256,256]{1,0:T(8,128)S(1)}, u32[]{:S(2)}, u32[]{:S(2)}) collective-permute-start(f32[256,256]{1,0:T(8,128)S(1)} %slice_add_fusion), channel_id=1, source_target_pairs={{0,4},{1,5},{2,6},{3,7},{4,0},{5,1},{6,2},{7,3},{8,12},{9,13},{10,... | collective-permute-start | bytes 786440 | tf_op jit(solution)/shard_map/ppermute | solution.py:326
  83.3 15.3 %collective-permute-start.29 = (f32[256,256]{1,0:T(8,128)S(1)}, f32[256,256]{1,0:T(8,128)S(1)}, u32[]{:S(2)}, u32[]{:S(2)}) collective-permute-start(f32[256,256]{1,0:T(8,128)S(1)} %get-tuple-element.193), channel_id=1, source_target_pairs={{0,8},{1,9},{2,10},{3,11},{4,12},{5,13},{6,14},{7,15},{8,0},{9,1},... | collective-permute-start | bytes 786440 | tf_op jit(solution)/shard_map/ppermute | solution.py:326
  83.8 14.8 %collective-permute-start.30 = (f32[256,256]{1,0:T(8,128)S(1)}, f32[256,256]{1,0:T(8,128)S(1)}, u32[]{:S(2)}, u32[]{:S(2)}) collective-permute-start(f32[256,256]{1,0:T(8,128)S(1)} %get-tuple-element.194), channel_id=1, source_target_pairs={{0,16},{1,17},{2,18},{3,19},{4,20},{5,21},{6,22},{7,23},{8,24},{9,... | collective-permute-start | bytes 786440 | tf_op jit(solution)/shard_map/ppermute | solution.py:326
  86.3 12.3 %collective-permute-start.31 = (f32[256,256]{1,0:T(8,128)S(1)}, f32[256,256]{1,0:T(8,128)S(1)}, u32[]{:S(2)}, u32[]{:S(2)}) collective-permute-start(f32[256,256]{1,0:T(8,128)S(1)} %get-tuple-element.195), channel_id=1, source_target_pairs={{0,24},{1,25},{2,26},{3,27},{4,28},{5,29},{6,30},{7,31},{8,16},{9,... | collective-permute-start | bytes 786440 | tf_op jit(solution)/shard_map/ppermute | solution.py:326
  98.7 14.1 %collective-permute-start.32 = (f32[256,256]{1,0:T(8,128)S(1)}, f32[256,256]{1,0:T(8,128)S(1)}, u32[]{:S(2)}, u32[]{:S(2)}) collective-permute-start(f32[256,256]{1,0:T(8,128)S(1)} %add_add_fusion), channel_id=1, source_target_pairs={{0,0},{1,1},{2,20},{3,21},{4,2},{5,3},{6,22},{7,23},{8,8},{9,9},{1... | collective-permute-start | bytes 786440 | tf_op jit(solution)/shard_map/ppermute | solution.py:326
  99.4 13.4 %collective-permute-start.33 = (f32[256,256]{1,0:T(8,128)S(1)}, f32[256,256]{1,0:T(8,128)S(1)}, u32[]{:S(2)}, u32[]{:S(2)}) collective-permute-start(f32[256,256]{1,0:T(8,128)S(1)} %broadcast_select_fusion.refs_4_.c0), channel_id=1, source_target_pairs={{0,8},{1,9},{2,10},{3,11},{4,12},{5,13},{6,14},{7,15},{8,0},{9,1},... | collective-permute-start | bytes 786440 | tf_op jit(solution)/shard_map/ppermute | solution.py:326
  121.6 9.6 %collective-permute-start.42 = (f32[256,256]{1,0:T(8,128)S(1)}, f32[256,256]{1,0:T(8,128)S(1)}, u32[]{:S(2)}, u32[]{:S(2)}) collective-permute-start(f32[256,256]{1,0:T(8,128)S(1)} %end.1.refs_0_), channel_id=1, source_target_pairs={{0,2},{1,3},{2,0},{3,1},{4,6},{5,7},{6,4},{7,5},{8,10},{9,11},{10,... | collective-permute-start | bytes 786440 | tf_op jit(solution)/shard_map/ppermute | solution.py:326
  121.6 14.9 %collective-permute-start.43 = (f32[256,256]{1,0:T(8,128)S(1)}, f32[256,256]{1,0:T(8,128)S(1)}, u32[]{:S(2)}, u32[]{:S(2)}) collective-permute-start(f32[256,256]{1,0:T(8,128)S(1)} %end.1.refs_0_), channel_id=1, source_target_pairs={{0,4},{1,5},{2,6},{3,7},{4,0},{5,1},{6,2},{7,3},{8,12},{9,13},{10,... | collective-permute-start | bytes 786440 | tf_op jit(solution)/shard_map/ppermute | solution.py:326
  (35 other events, 238.4 us)

commit v6 on v5

--- a/solution.py
+++ b/solution.py
@@ -414,7 +414,8 @@
         scratch=(pltpu.VMEM((4, NB, NB), jnp.float32),),
     )
 
-    rest = together(*held, turned, low, *block_sums, *carried)
+    across = jnp.where(first_pair, across, 0.0)
+    across, *rest = together(across, *held, turned, low, *block_sums, *carried)
     held, (turned, low), rest = rest[:n_rows], rest[n_rows : n_rows + 2], rest[n_rows + 2 :]
     block_sums, carried = rest[:n_rows], rest[n_rows:]
     turned_other, blocks_other, across_other = swap(turned), swap(blocks), swap(across)

time: 148 us -> 148 us (level)
  transfers between devices with their start and end apart: 48 -> 48, of which waited for: 18 -> 18; matrix products, arithmetic and copies ran while one was open for 2% -> 3% of each run, Pallas kernels for 9% -> 10%
where the time goes in v6:
time: 148 us; the launch traced here: 147 us
  waiting for transfers between devices  66.5 us (45%)
  starting transfers between devices  51.9 us (35%)
  Pallas kernels  20.3 us (14%)
  other arithmetic  4.06 us (3%)
  local copies, waits for them, and re-layouts  3.73 us (3%)
    ppermute x48, waiting for transfers between devices, send(): return lax.ppermute(value, ('row', 'col'), edges)  66.5 us
    ppermute x48, starting transfers between devices, send(): return lax.ppermute(value, ('row', 'col'), edges)  51.9 us
    pallas_call x8, Pallas kernels, call(): pl.pallas_call(kernel, out_shape=out_shape, in_specs=[pl.BlockSpec(memory...  20.3 us
  transfers between devices with their start and end apart: 48, of which 18 were waited for; matrix products, arithmetic and copies ran while one was open for 3% of the time, Pallas kernels for 10%

profile of v6, /device:TPU:0, one launch (start us, length us, event | category | flops | bytes accessed | tf_op | source)
XLA Modules:
  0.0 147.1 jit_solution(527037327693863493)
XLA Ops:
  0.0 2.1 %fusion = (f32[256,256]{1,0:T(8,128)S(1)}, f32[256,256]{1,0:T(8,128)}, f32[256,256]{1,0:T(8,128)S(1)}, f32[256,256]{1,0:T(8,128)S(1)}) fusion(f32[1024,512]{1,0:T(8,128)} %param.2), kind=kLoop, calls=%fused_computation.19 | loop fusion | bytes 2097152 | tf_op jit(solution)/shard_map/slice | solution.py:338
  2.1 5.6 %collective-permute-start = (f32[256,256]{1,0:T(8,128)S(1)}, f32[256,256]{1,0:T(8,128)}, u32[]{:S(2)}, u32[]{:S(2)}) collective-permute-start(f32[256,256]{1,0:T(8,128)S(1)} %get-tuple-element.140), channel_id=1, source_target_pairs={{0,2},{1,3},{8,10},{9,11},{16,18},{17,19},{24,26},{25,27}} | collective-permute-start | bytes 786440 | tf_op jit(solution)/shard_map/ppermute | solution.py:326
  9.8 2.0 %collective-permute-start.6 = (f32[256,256]{1,0:T(8,128)}, f32[256,256]{1,0:T(8,128)}, u32[]{:S(2)}, u32[]{:S(2)}) collective-permute-start(f32[256,256]{1,0:T(8,128)} %get-tuple-element.132), channel_id=1, source_target_pairs={{0,2},{1,3},{8,10},{9,11},{16,18},{17,19},{24,26},{25,27}} | collective-permute-start | bytes 786440 | tf_op jit(solution)/shard_map/ppermute | solution.py:326
  15.2 4.6 %inverse.1 = f32[256,256]{1,0:T(8,128)S(1)} custom-call(s32[3]{0:T(128)S(1)} %pad_add_fusion.ids, f32[256,256]{1,0:T(8,128)S(1)} %get-tuple-element.118.block_ref), custom_call_target="tpu_custom_call" | custom-call | flops 1 | bytes 1 | tf_op jit(solution)/shard_map/inverse/pallas_call | solution.py:43
  22.5 2.6 %collective-permute-done.6 = f32[256,256]{1,0:T(8,128)} collective-permute-done((f32[256,256]{1,0:T(8,128)}, f32[256,256]{1,0:T(8,128)}, u32[]{:S(2)}, u32[]{:S(2)}) %collective-permute-start.6) | collective-permute-done | bytes 262176 | tf_op jit(solution)/shard_map/ppermute | solution.py:326
  27.9 3.4 %collective-permute-start.5 = (f32[512,256]{1,0:T(8,128)S(1)}, f32[512,256]{1,0:T(8,128)}, u32[]{:S(2)}, u32[]{:S(2)}) collective-permute-start(f32[512,256]{1,0:T(8,128)S(1)} %pad_maximum_fusion.blocks), channel_id=1, source_target_pairs={{0,8},{1,9},{8,0},{9,1}} | collective-permute-start | bytes 1572872 | tf_op jit(solution)/shard_map/ppermute | solution.py:326
  34.6 7.0 %collective-permute-done.5 = f32[512,256]{1,0:T(8,128)} collective-permute-done((f32[512,256]{1,0:T(8,128)S(1)}, f32[512,256]{1,0:T(8,128)}, u32[]{:S(2)}, u32[]{:S(2)}) %collective-permute-start.5) | collective-permute-done | bytes 524320 | tf_op jit(solution)/shard_map/ppermute | solution.py:326
  50.1 2.5 %masked.1 = (bf16[1024,512]{1,0:T(8,128)(2,1)S(1)}, bf16[1024,512]{1,0:T(8,128)(2,1)S(1)}, bf16[512,512]{1,0:T(8,128)(2,1)S(1)}, bf16[512,512]{1,0:T(8,128)(2,1)S(1)}) custom-call(s32[3]{0:T(128)S(1)} %pad_add_fusion.ids, f32[1024,512]{1,0:T(8,128)S(1)} %copy-done, f32[1024,512]{1,0:T(8,128)} %collective-permute-done.17.other), custom_call_target="tpu_custom_call" | custom-call | flops 1 | bytes 1 | tf_op jit(solution)/shard_map/masked/pallas_call | solution.py:43
  52.6 2.1 %columns.1 = (f32[256,1024]{1,0:T(8,128)S(1)}, f32[256,512]{1,0:T(8,128)S(1)}, f32[256,256]{1,0:T(8,128)S(1)}, f32[256,256]{1,0:T(8,128)S(1)}, f32[256,256]{1,0:T(8,128)S(1)}, /*index=5*/f32[256,256]{1,0:T(8,128)S(1)}) custom-call(s32[3]{0:T(128)S(1)} %pad_add_fusion.ids, bf16[1024,512]{1,0:T(8,128)(2,1)S(1)} %get-tuple-element.127.low_1, ...), custom_call_target="tpu_custom_call" | custom-call | flops 1 | bytes 1 | tf_op jit(solution)/shard_map/columns/pallas_call | solution.py:43
  54.7 5.4 %collective-permute-done.15.v2 = f32[256,256]{1,0:T(8,128)S(1)} collective-permute-done((f32[256,256]{1,0:T(8,128)S(1)}, f32[256,256]{1,0:T(8,128)S(1)}, u32[]{:S(2)}, u32[]{:S(2)}) %collective-permute-start.15) | collective-permute-done | bytes 262176 | tf_op jit(solution)/shard_map/ppermute | solution.py:326
  60.7 2.2 %rows.1 = (f32[256,256]{1,0:T(8,128)S(1)}, f32[256,256]{1,0:T(8,128)S(1)}, f32[512,256]{1,0:T(8,128)S(1)}, f32[1024,256]{1,0:T(8,128)S(1)}, f32[256,256]{1,0:T(8,128)S(1)}) custom-call(s32[3]{0:T(128)S(1)} %pad_add_fusion.ids, bf16[1024,512]{1,0:T(8,128)(2,1)S(1)} %get-tuple-element.127.low_1, bf16[1024,512]{1,0:T(8,128)(2,1)S(1)} %get-tuple-element.128.low_2, ...), custom_call_target="tpu_custom_call" | custom-call | flops 1 | bytes 1 | tf_op jit(solution)/shard_map/rows/pallas_call | solution.py:43
  65.4 3.4 %collective-permute-start.21 = (f32[256,256]{1,0:T(8,128)S(1)}, f32[256,256]{1,0:T(8,128)S(1)}, u32[]{:S(2)}, u32[]{:S(2)}) collective-permute-start(f32[256,256]{1,0:T(8,128)S(1)} %get-tuple-element.174), channel_id=1, source_target_pairs={{0,16},{1,17},{2,18},{3,19},{4,20},{5,21},{6,22},{7,23},{8,24},{9,... | collective-permute-start | bytes 786440 | tf_op jit(solution)/shard_map/ppermute | solution.py:326
  69.4 3.0 %collective-permute-start.25 = (f32[128,256]{1,0:T(8,128)S(1)}, f32[128,256]{1,0:T(8,128)S(1)}, u32[]{:S(2)}, u32[]{:S(2)}) collective-permute-start(f32[128,256]{1,0:T(8,128)S(1)} %get-tuple-element.183), channel_id=1, source_target_pairs={{0,24},{1,25},{2,26},{3,27},{4,28},{5,29},{6,30},{7,31},{8,16},{9,... | collective-permute-start | bytes 393224 | tf_op jit(solution)/shard_map/ppermute | solution.py:326
  72.3 5.9 %collective-permute-done.21 = f32[256,256]{1,0:T(8,128)S(1)} collective-permute-done((f32[256,256]{1,0:T(8,128)S(1)}, f32[256,256]{1,0:T(8,128)S(1)}, u32[]{:S(2)}, u32[]{:S(2)}) %collective-permute-start.21) | collective-permute-done | bytes 262176 | tf_op jit(solution)/shard_map/ppermute | solution.py:326
  83.8 2.5 %collective-permute-start.30 = (f32[256,256]{1,0:T(8,128)S(1)}, f32[256,256]{1,0:T(8,128)S(1)}, u32[]{:S(2)}, u32[]{:S(2)}) collective-permute-start(f32[256,256]{1,0:T(8,128)S(1)} %get-tuple-element.196), channel_id=1, source_target_pairs={{0,16},{1,17},{2,18},{3,19},{4,20},{5,21},{6,22},{7,23},{8,24},{9,... | collective-permute-start | bytes 786440 | tf_op jit(solution)/shard_map/ppermute | solution.py:326
  87.2 3.5 %collective-permute-done.27 = f32[128,256]{1,0:T(8,128)S(1)} collective-permute-done((f32[128,256]{1,0:T(8,128)S(1)}, f32[128,256]{1,0:T(8,128)S(1)}, u32[]{:S(2)}, u32[]{:S(2)}) %collective-permute-start.27) | collective-permute-done | bytes 131104 | tf_op jit(solution)/shard_map/ppermute | solution.py:326
  92.1 6.5 %collective-permute-done.28 = f32[128,256]{1,0:T(8,128)S(1)} collective-permute-done((f32[128,256]{1,0:T(8,128)S(1)}, f32[128,256]{1,0:T(8,128)S(1)}, u32[]{:S(2)}, u32[]{:S(2)}) %collective-permute-start.28) | collective-permute-done | bytes 131104 | tf_op jit(solution)/shard_map/ppermute | solution.py:326
  100.0 3.4 %collective-permute-start.34 = (f32[128,256]{1,0:T(8,128)S(1)}, f32[128,256]{1,0:T(8,128)S(1)}, u32[]{:S(2)}, u32[]{:S(2)}) collective-permute-start(f32[128,256]{1,0:T(8,128)S(1)} %add.51), channel_id=1, source_target_pairs={{0,8},{1,9},{8,0},{9,1}} | collective-permute-start | bytes 393224 | tf_op jit(solution)/shard_map/ppermute | solution.py:326
  106.0 3.2 %collective-permute-done.34 = f32[128,256]{1,0:T(8,128)S(1)} collective-permute-done((f32[128,256]{1,0:T(8,128)S(1)}, f32[128,256]{1,0:T(8,128)S(1)}, u32[]{:S(2)}, u32[]{:S(2)}) %collective-permute-start.34) | collective-permute-done | bytes 131104 | tf_op jit(solution)/shard_map/ppermute | solution.py:326
  109.2 3.6 %collective-permute-done.35 = f32[128,256]{1,0:T(8,128)S(1)} collective-permute-done((f32[128,256]{1,0:T(8,128)S(1)}, f32[128,256]{1,0:T(8,128)S(1)}, u32[]{:S(2)}, u32[]{:S(2)}) %collective-permute-start.35) | collective-permute-done | bytes 131104 | tf_op jit(solution)/shard_map/ppermute | solution.py:326
  116.3 4.3 %end.1.refs_0_ = f32[256,256]{1,0:T(8,128)S(1)} custom-call(s32[3]{0:T(128)S(1)} %pad_add_fusion.ids, f32[256,256]{1,0:T(8,128)S(1)} %get-tuple-element.211.total, f32[256,256]{1,0:T(8,128)S(1)} %get-tuple-element.212.solved, f32[256,256]{1,0:T(8,128)S(1)} %collective-permute-done.37.second, f32[256,256]{1,0:T(8,128)S(1)} %broadcast_select_fusion.1.refs_4_.c0, ...), custom_call_target="tpu_custom_call" | custom-call | flops 1 | bytes 1 | tf_op jit(solution)/shard_map/end/pallas_call | solution.py:43
  122.2 8.4 %collective-permute-done.42.refs_1_ = f32[256,256]{1,0:T(8,128)S(1)} collective-permute-done((f32[256,256]{1,0:T(8,128)S(1)}, f32[256,256]{1,0:T(8,128)S(1)}, u32[]{:S(2)}, u32[]{:S(2)}) %collective-permute-start.42) | collective-permute-done | bytes 262176 | tf_op jit(solution)/shard_map/ppermute | solution.py:326
  130.6 5.4 %collective-permute-done.43.refs_2_ = f32[256,256]{1,0:T(8,128)S(1)} collective-permute-done((f32[256,256]{1,0:T(8,128)S(1)}, f32[256,256]{1,0:T(8,128)S(1)}, u32[]{:S(2)}, u32[]{:S(2)}) %collective-permute-start.43) | collective-permute-done | bytes 262176 | tf_op jit(solution)/shard_map/ppermute | solution.py:326
  136.5 7.0 %collective-permute-done.44.refs_3_ = f32[256,256]{1,0:T(8,128)S(1)} collective-permute-done((f32[256,256]{1,0:T(8,128)S(1)}, f32[256,256]{1,0:T(8,128)S(1)}, u32[]{:S(2)}, u32[]{:S(2)}) %collective-permute-start.44) | collective-permute-done | bytes 262176 | tf_op jit(solution)/shard_map/ppermute | solution.py:326
  (122 shorter events, 47.0 us)
Async XLA Ops:
  2.1 11.6 %collective-permute-start = (f32[256,256]{1,0:T(8,128)S(1)}, f32[256,256]{1,0:T(8,128)}, u32[]{:S(2)}, u32[]{:S(2)}) collective-permute-start(f32[256,256]{1,0:T(8,128)S(1)} %get-tuple-element.140), channel_id=1, source_target_pairs={{0,2},{1,3},{8,10},{9,11},{16,18},{17,19},{24,26},{25,27}} | collective-permute-start | bytes 786440 | tf_op jit(solution)/shard_map/ppermute | solution.py:326
  7.8 13.4 %collective-permute-start.3 = (f32[256,256]{1,0:T(8,128)S(1)}, f32[256,256]{1,0:T(8,128)}, u32[]{:S(2)}, u32[]{:S(2)}) collective-permute-start(f32[256,256]{1,0:T(8,128)S(1)} %get-tuple-element.136), channel_id=1, source_target_pairs={{0,2},{1,3},{8,10},{9,11},{16,18},{17,19},{24,26},{25,27}} | collective-permute-start | bytes 786440 | tf_op jit(solution)/shard_map/ppermute | solution.py:326
  9.8 15.3 %collective-permute-start.6 = (f32[256,256]{1,0:T(8,128)}, f32[256,256]{1,0:T(8,128)}, u32[]{:S(2)}, u32[]{:S(2)}) collective-permute-start(f32[256,256]{1,0:T(8,128)} %get-tuple-element.132), channel_id=1, source_target_pairs={{0,2},{1,3},{8,10},{9,11},{16,18},{17,19},{24,26},{25,27}} | collective-permute-start | bytes 786440 | tf_op jit(solution)/shard_map/ppermute | solution.py:326
  13.8 12.7 %collective-permute-start.1 = (f32[256,256]{1,0:T(8,128)}, f32[256,256]{1,0:T(8,128)}, u32[]{:S(2)}, u32[]{:S(2)}) collective-permute-start(f32[256,256]{1,0:T(8,128)} %collective-permute-done), channel_id=1, source_target_pairs={{2,4},{3,5},{10,12},{11,13},{18,20},{19,21},{26,28},{27,29}} | collective-permute-start | bytes 786440 | tf_op jit(solution)/shard_map/ppermute | solution.py:326
  19.8 11.5 %collective-permute-start.11 = (f32[256,256]{1,0:T(8,128)S(1)}, f32[256,256]{1,0:T(8,128)S(1)}, u32[]{:S(2)}, u32[]{:S(2)}) collective-permute-start(f32[256,256]{1,0:T(8,128)S(1)} %select_select_fusion.5.refs_0_), channel_id=1, source_target_pairs={{0,2},{1,3},{8,10},{9,11},{16,18},{17,19},{24,26},{25,27}} | collective-permute-start | bytes 786440 | tf_op jit(solution)/shard_map/ppermute | solution.py:326
  21.2 10.9 %collective-permute-start.9 = (f32[256,256]{1,0:T(8,128)}, f32[256,256]{1,0:T(8,128)}, u32[]{:S(2)}, u32[]{:S(2)}) collective-permute-start(f32[256,256]{1,0:T(8,128)} %collective-permute-done.3), channel_id=1, source_target_pairs={{2,4},{3,5},{10,12},{11,13},{18,20},{19,21},{26,28},{27,29}} | collective-permute-start | bytes 786440 | tf_op jit(solution)/shard_map/ppermute | solution.py:326
  27.9 13.6 %collective-permute-start.5 = (f32[512,256]{1,0:T(8,128)S(1)}, f32[512,256]{1,0:T(8,128)}, u32[]{:S(2)}, u32[]{:S(2)}) collective-permute-start(f32[512,256]{1,0:T(8,128)S(1)} %pad_maximum_fusion.blocks), channel_id=1, source_target_pairs={{0,8},{1,9},{8,0},{9,1}} | collective-permute-start | bytes 1572872 | tf_op jit(solution)/shard_map/ppermute | solution.py:326
  44.5 10.2 %collective-permute-start.14 = (f32[256,256]{1,0:T(8,128)S(1)}, f32[256,256]{1,0:T(8,128)S(1)}, u32[]{:S(2)}, u32[]{:S(2)}) collective-permute-start(f32[256,256]{1,0:T(8,128)S(1)} %get-tuple-element.151.v0), channel_id=1, source_target_pairs={{0,8},{1,9},{2,10},{3,11},{4,12},{5,13},{6,14},{7,15},{8,0},{9,1},... | collective-permute-start | bytes 786440 | tf_op jit(solution)/shard_map/ppermute | solution.py:326
  46.0 14.0 %collective-permute-start.15 = (f32[256,256]{1,0:T(8,128)S(1)}, f32[256,256]{1,0:T(8,128)S(1)}, u32[]{:S(2)}, u32[]{:S(2)}) collective-permute-start(f32[256,256]{1,0:T(8,128)S(1)} %get-tuple-element.151.v0), channel_id=1, source_target_pairs={{0,16},{1,17},{2,18},{3,19},{4,20},{5,21},{6,22},{7,23},{8,24},{9,... | collective-permute-start | bytes 786440 | tf_op jit(solution)/shard_map/ppermute | solution.py:326
  46.0 14.0 %collective-permute-start.16 = (f32[256,256]{1,0:T(8,128)S(1)}, f32[256,256]{1,0:T(8,128)S(1)}, u32[]{:S(2)}, u32[]{:S(2)}) collective-permute-start(f32[256,256]{1,0:T(8,128)S(1)} %get-tuple-element.151.v0), channel_id=1, source_target_pairs={{0,24},{1,25},{2,26},{3,27},{4,28},{5,29},{6,30},{7,31},{8,16},{9,... | collective-permute-start | bytes 786440 | tf_op jit(solution)/shard_map/ppermute | solution.py:326
  48.0 12.1 %collective-permute-start.18 = (f32[256,256]{1,0:T(8,128)S(1)}, f32[256,256]{1,0:T(8,128)S(1)}, u32[]{:S(2)}, u32[]{:S(2)}) collective-permute-start(f32[256,256]{1,0:T(8,128)S(1)} %copy-done.2), channel_id=1, source_target_pairs={{4,6},{5,7},{12,14},{13,15},{20,22},{21,23},{28,30},{29,31}} | collective-permute-start | bytes 786440 | tf_op jit(solution)/shard_map/ppermute | solution.py:326
  64.7 15.5 %collective-permute-start.22 = (f32[512,256]{1,0:T(8,128)S(1)}, f32[512,256]{1,0:T(8,128)S(1)}, u32[]{:S(2)}, u32[]{:S(2)}) collective-permute-start(f32[512,256]{1,0:T(8,128)S(1)} %get-tuple-element.175), channel_id=1, source_target_pairs={{0,2},{1,3},{2,0},{3,1},{4,6},{5,7},{6,4},{7,5},{8,10},{9,11},{10,... | collective-permute-start | bytes 1572872 | tf_op jit(solution)/shard_map/ppermute | solution.py:326
  65.4 12.8 %collective-permute-start.21 = (f32[256,256]{1,0:T(8,128)S(1)}, f32[256,256]{1,0:T(8,128)S(1)}, u32[]{:S(2)}, u32[]{:S(2)}) collective-permute-start(f32[256,256]{1,0:T(8,128)S(1)} %get-tuple-element.174), channel_id=1, source_target_pairs={{0,16},{1,17},{2,18},{3,19},{4,20},{5,21},{6,22},{7,23},{8,24},{9,... | collective-permute-start | bytes 786440 | tf_op jit(solution)/shard_map/ppermute | solution.py:326
  69.3 10.9 %collective-permute-start.24 = (f32[128,256]{1,0:T(8,128)S(1)}, f32[128,256]{1,0:T(8,128)S(1)}, u32[]{:S(2)}, u32[]{:S(2)}) collective-permute-start(f32[128,256]{1,0:T(8,128)S(1)} %get-tuple-element.182), channel_id=1, source_target_pairs={{0,16},{1,17},{2,18},{3,19},{4,20},{5,21},{6,22},{7,23},{8,24},{9,... | collective-permute-start | bytes 393224 | tf_op jit(solution)/shard_map/ppermute | solution.py:326
  69.4 10.9 %collective-permute-start.25 = (f32[128,256]{1,0:T(8,128)S(1)}, f32[128,256]{1,0:T(8,128)S(1)}, u32[]{:S(2)}, u32[]{:S(2)}) collective-permute-start(f32[128,256]{1,0:T(8,128)S(1)} %get-tuple-element.183), channel_id=1, source_target_pairs={{0,24},{1,25},{2,26},{3,27},{4,28},{5,29},{6,30},{7,31},{8,16},{9,... | collective-permute-start | bytes 393224 | tf_op jit(solution)/shard_map/ppermute | solution.py:326
  80.3 10.5 %collective-permute-start.27 = (f32[128,256]{1,0:T(8,128)S(1)}, f32[128,256]{1,0:T(8,128)S(1)}, u32[]{:S(2)}, u32[]{:S(2)}) collective-permute-start(f32[128,256]{1,0:T(8,128)S(1)} %add_add_fusion.1), channel_id=1, source_target_pairs={{2,0},{3,1},{6,4},{7,5},{10,8},{11,9},{14,12},{15,13},{18,16},{19,... | collective-permute-start | bytes 393224 | tf_op jit(solution)/shard_map/ppermute | solution.py:326
  81.6 17.0 %collective-permute-start.26 = (f32[256,256]{1,0:T(8,128)S(1)}, f32[256,256]{1,0:T(8,128)S(1)}, u32[]{:S(2)}, u32[]{:S(2)}) collective-permute-start(f32[256,256]{1,0:T(8,128)S(1)} %slice_add_fusion), channel_id=1, source_target_pairs={{0,4},{1,5},{2,6},{3,7},{4,0},{5,1},{6,2},{7,3},{8,12},{9,13},{10,... | collective-permute-start | bytes 786440 | tf_op jit(solution)/shard_map/ppermute | solution.py:326
  83.3 15.3 %collective-permute-start.29 = (f32[256,256]{1,0:T(8,128)S(1)}, f32[256,256]{1,0:T(8,128)S(1)}, u32[]{:S(2)}, u32[]{:S(2)}) collective-permute-start(f32[256,256]{1,0:T(8,128)S(1)} %get-tuple-element.195), channel_id=1, source_target_pairs={{0,8},{1,9},{2,10},{3,11},{4,12},{5,13},{6,14},{7,15},{8,0},{9,1},... | collective-permute-start | bytes 786440 | tf_op jit(solution)/shard_map/ppermute | solution.py:326
  83.8 14.8 %collective-permute-start.30 = (f32[256,256]{1,0:T(8,128)S(1)}, f32[256,256]{1,0:T(8,128)S(1)}, u32[]{:S(2)}, u32[]{:S(2)}) collective-permute-start(f32[256,256]{1,0:T(8,128)S(1)} %get-tuple-element.196), channel_id=1, source_target_pairs={{0,16},{1,17},{2,18},{3,19},{4,20},{5,21},{6,22},{7,23},{8,24},{9,... | collective-permute-start | bytes 786440 | tf_op jit(solution)/shard_map/ppermute | solution.py:326
  86.3 12.3 %collective-permute-start.31 = (f32[256,256]{1,0:T(8,128)S(1)}, f32[256,256]{1,0:T(8,128)S(1)}, u32[]{:S(2)}, u32[]{:S(2)}) collective-permute-start(f32[256,256]{1,0:T(8,128)S(1)} %get-tuple-element.197), channel_id=1, source_target_pairs={{0,24},{1,25},{2,26},{3,27},{4,28},{5,29},{6,30},{7,31},{8,16},{9,... | collective-permute-start | bytes 786440 | tf_op jit(solution)/shard_map/ppermute | solution.py:326
  98.7 14.1 %collective-permute-start.32 = (f32[256,256]{1,0:T(8,128)S(1)}, f32[256,256]{1,0:T(8,128)S(1)}, u32[]{:S(2)}, u32[]{:S(2)}) collective-permute-start(f32[256,256]{1,0:T(8,128)S(1)} %add_add_fusion), channel_id=1, source_target_pairs={{0,0},{1,1},{2,20},{3,21},{4,2},{5,3},{6,22},{7,23},{8,8},{9,9},{1... | collective-permute-start | bytes 786440 | tf_op jit(solution)/shard_map/ppermute | solution.py:326
  99.4 13.4 %collective-permute-start.33 = (f32[256,256]{1,0:T(8,128)S(1)}, f32[256,256]{1,0:T(8,128)S(1)}, u32[]{:S(2)}, u32[]{:S(2)}) collective-permute-start(f32[256,256]{1,0:T(8,128)S(1)} %broadcast_select_fusion.1.refs_4_.c0), channel_id=1, source_target_pairs={{0,8},{1,9},{2,10},{3,11},{4,12},{5,13},{6,14},{7,15},{8,0},{9,1},... | collective-permute-start | bytes 786440 | tf_op jit(solution)/shard_map/ppermute | solution.py:326
  121.1 9.6 %collective-permute-start.42 = (f32[256,256]{1,0:T(8,128)S(1)}, f32[256,256]{1,0:T(8,128)S(1)}, u32[]{:S(2)}, u32[]{:S(2)}) collective-permute-start(f32[256,256]{1,0:T(8,128)S(1)} %end.1.refs_0_), channel_id=1, source_target_pairs={{0,2},{1,3},{2,0},{3,1},{4,6},{5,7},{6,4},{7,5},{8,10},{9,11},{10,... | collective-permute-start | bytes 786440 | tf_op jit(solution)/shard_map/ppermute | solution.py:326
  121.1 14.9 %collective-permute-start.43 = (f32[256,256]{1,0:T(8,128)S(1)}, f32[256,256]{1,0:T(8,128)S(1)}, u32[]{:S(2)}, u32[]{:S(2)}) collective-permute-start(f32[256,256]{1,0:T(8,128)S(1)} %end.1.refs_0_), channel_id=1, source_target_pairs={{0,4},{1,5},{2,6},{3,7},{4,0},{5,1},{6,2},{7,3},{8,12},{9,13},{10,... | collective-permute-start | bytes 786440 | tf_op jit(solution)/shard_map/ppermute | solution.py:326
  (35 other events, 239.8 us)

commit v7 on v6

--- a/solution.py
+++ b/solution.py
@@ -540,9 +540,11 @@
         if bit == 2:
             results[1] = swap_pairs(result, 1)
             others[0] = swap(result)
-            names = sorted(results)
+            names = sorted(d for d in results if d != 1)
+            nearest = results[1]
             rest = together(others[0], *[results[d] for d in names])
             others[0], results = rest[0], dict(zip(names, rest[1:]))
+            results[1] = nearest
             for d in names:
                 if d ^ 1 not in results:
                     results[d ^ 1] = swap_pairs(results[d], 1)

time: 148 us -> 145 us (0.980)
  waiting for transfers between devices: 66.5 us -> 64.2 us
    ppermute x48, waiting for transfers between devices: 66.5 us -> 64.2 us  [send(): return lax.ppermute(value, ('row', 'col'), edges)]
where the time goes in v7:
time: 145 us; the launch traced here: 144 us
  waiting for transfers between devices  64.2 us (44%)
  starting transfers between devices  51.4 us (35%)
  Pallas kernels  20.3 us (14%)
  other arithmetic  4.06 us (3%)
  local copies, waits for them, and re-layouts  3.73 us (3%)
    ppermute x48, waiting for transfers between devices, send(): return lax.ppermute(value, ('row', 'col'), edges)  64.2 us
    ppermute x48, starting transfers between devices, send(): return lax.ppermute(value, ('row', 'col'), edges)  51.4 us
    pallas_call x8, Pallas kernels, call(): pl.pallas_call(kernel, out_shape=out_shape, in_specs=[pl.BlockSpec(memory...  20.3 us
  transfers between devices with their start and end apart: 48, of which 18 were waited for; matrix products, arithmetic and copies ran while one was open for 3% of the time, Pallas kernels for 10%

profile of v7, /device:TPU:0, one launch (start us, length us, event | category | flops | bytes accessed | tf_op | source)
XLA Modules:
  0.0 144.2 jit_solution(10834027398669964653)
XLA Ops:
  0.0 2.1 %fusion = (f32[256,256]{1,0:T(8,128)S(1)}, f32[256,256]{1,0:T(8,128)}, f32[256,256]{1,0:T(8,128)S(1)}, f32[256,256]{1,0:T(8,128)S(1)}) fusion(f32[1024,512]{1,0:T(8,128)} %param.2), kind=kLoop, calls=%fused_computation.19 | loop fusion | bytes 2097152 | tf_op jit(solution)/shard_map/slice | solution.py:338
  2.1 5.6 %collective-permute-start = (f32[256,256]{1,0:T(8,128)S(1)}, f32[256,256]{1,0:T(8,128)}, u32[]{:S(2)}, u32[]{:S(2)}) collective-permute-start(f32[256,256]{1,0:T(8,128)S(1)} %get-tuple-element.139), channel_id=1, source_target_pairs={{0,2},{1,3},{8,10},{9,11},{16,18},{17,19},{24,26},{25,27}} | collective-permute-start | bytes 786440 | tf_op jit(solution)/shard_map/ppermute | solution.py:326
  9.8 2.0 %collective-permute-start.6 = (f32[256,256]{1,0:T(8,128)}, f32[256,256]{1,0:T(8,128)}, u32[]{:S(2)}, u32[]{:S(2)}) collective-permute-start(f32[256,256]{1,0:T(8,128)} %get-tuple-element.131), channel_id=1, source_target_pairs={{0,2},{1,3},{8,10},{9,11},{16,18},{17,19},{24,26},{25,27}} | collective-permute-start | bytes 786440 | tf_op jit(solution)/shard_map/ppermute | solution.py:326
  15.2 4.6 %inverse.1 = f32[256,256]{1,0:T(8,128)S(1)} custom-call(s32[3]{0:T(128)S(1)} %pad_add_fusion.ids, f32[256,256]{1,0:T(8,128)S(1)} %get-tuple-element.117.block_ref), custom_call_target="tpu_custom_call" | custom-call | flops 1 | bytes 1 | tf_op jit(solution)/shard_map/inverse/pallas_call | solution.py:43
  22.5 2.6 %collective-permute-done.6 = f32[256,256]{1,0:T(8,128)} collective-permute-done((f32[256,256]{1,0:T(8,128)}, f32[256,256]{1,0:T(8,128)}, u32[]{:S(2)}, u32[]{:S(2)}) %collective-permute-start.6) | collective-permute-done | bytes 262176 | tf_op jit(solution)/shard_map/ppermute | solution.py:326
  27.9 3.4 %collective-permute-start.5 = (f32[512,256]{1,0:T(8,128)S(1)}, f32[512,256]{1,0:T(8,128)}, u32[]{:S(2)}, u32[]{:S(2)}) collective-permute-start(f32[512,256]{1,0:T(8,128)S(1)} %pad_maximum_fusion.blocks), channel_id=1, source_target_pairs={{0,8},{1,9},{8,0},{9,1}} | collective-permute-start | bytes 1572872 | tf_op jit(solution)/shard_map/ppermute | solution.py:326
  34.6 7.0 %collective-permute-done.5 = f32[512,256]{1,0:T(8,128)} collective-permute-done((f32[512,256]{1,0:T(8,128)S(1)}, f32[512,256]{1,0:T(8,128)}, u32[]{:S(2)}, u32[]{:S(2)}) %collective-permute-start.5) | collective-permute-done | bytes 524320 | tf_op jit(solution)/shard_map/ppermute | solution.py:326
  50.1 2.5 %masked.1 = (bf16[1024,512]{1,0:T(8,128)(2,1)S(1)}, bf16[1024,512]{1,0:T(8,128)(2,1)S(1)}, bf16[512,512]{1,0:T(8,128)(2,1)S(1)}, bf16[512,512]{1,0:T(8,128)(2,1)S(1)}) custom-call(s32[3]{0:T(128)S(1)} %pad_add_fusion.ids, f32[1024,512]{1,0:T(8,128)S(1)} %copy-done, f32[1024,512]{1,0:T(8,128)} %collective-permute-done.17.other), custom_call_target="tpu_custom_call" | custom-call | flops 1 | bytes 1 | tf_op jit(solution)/shard_map/masked/pallas_call | solution.py:43
  52.6 2.1 %columns.1 = (f32[256,1024]{1,0:T(8,128)S(1)}, f32[256,512]{1,0:T(8,128)S(1)}, f32[256,256]{1,0:T(8,128)S(1)}, f32[256,256]{1,0:T(8,128)S(1)}, f32[256,256]{1,0:T(8,128)S(1)}, /*index=5*/f32[256,256]{1,0:T(8,128)S(1)}) custom-call(s32[3]{0:T(128)S(1)} %pad_add_fusion.ids, bf16[1024,512]{1,0:T(8,128)(2,1)S(1)} %get-tuple-element.126.low_1, ...), custom_call_target="tpu_custom_call" | custom-call | flops 1 | bytes 1 | tf_op jit(solution)/shard_map/columns/pallas_call | solution.py:43
  54.7 5.4 %collective-permute-done.15.v2 = f32[256,256]{1,0:T(8,128)S(1)} collective-permute-done((f32[256,256]{1,0:T(8,128)S(1)}, f32[256,256]{1,0:T(8,128)S(1)}, u32[]{:S(2)}, u32[]{:S(2)}) %collective-permute-start.15) | collective-permute-done | bytes 262176 | tf_op jit(solution)/shard_map/ppermute | solution.py:326
  60.7 2.2 %rows.1 = (f32[256,256]{1,0:T(8,128)S(1)}, f32[256,256]{1,0:T(8,128)S(1)}, f32[512,256]{1,0:T(8,128)S(1)}, f32[1024,256]{1,0:T(8,128)S(1)}, f32[256,256]{1,0:T(8,128)S(1)}) custom-call(s32[3]{0:T(128)S(1)} %pad_add_fusion.ids, bf16[1024,512]{1,0:T(8,128)(2,1)S(1)} %get-tuple-element.126.low_1, bf16[1024,512]{1,0:T(8,128)(2,1)S(1)} %get-tuple-element.127.low_2, ...), custom_call_target="tpu_custom_call" | custom-call | flops 1 | bytes 1 | tf_op jit(solution)/shard_map/rows/pallas_call | solution.py:43
  65.4 3.4 %collective-permute-start.21 = (f32[256,256]{1,0:T(8,128)S(1)}, f32[256,256]{1,0:T(8,128)S(1)}, u32[]{:S(2)}, u32[]{:S(2)}) collective-permute-start(f32[256,256]{1,0:T(8,128)S(1)} %get-tuple-element.173), channel_id=1, source_target_pairs={{0,16},{1,17},{2,18},{3,19},{4,20},{5,21},{6,22},{7,23},{8,24},{9,... | collective-permute-start | bytes 786440 | tf_op jit(solution)/shard_map/ppermute | solution.py:326
  69.4 3.0 %collective-permute-start.25 = (f32[128,256]{1,0:T(8,128)S(1)}, f32[128,256]{1,0:T(8,128)S(1)}, u32[]{:S(2)}, u32[]{:S(2)}) collective-permute-start(f32[128,256]{1,0:T(8,128)S(1)} %get-tuple-element.182), channel_id=1, source_target_pairs={{0,24},{1,25},{2,26},{3,27},{4,28},{5,29},{6,30},{7,31},{8,16},{9,... | collective-permute-start | bytes 393224 | tf_op jit(solution)/shard_map/ppermute | solution.py:326
  72.3 5.9 %collective-permute-done.21 = f32[256,256]{1,0:T(8,128)S(1)} collective-permute-done((f32[256,256]{1,0:T(8,128)S(1)}, f32[256,256]{1,0:T(8,128)S(1)}, u32[]{:S(2)}, u32[]{:S(2)}) %collective-permute-start.21) | collective-permute-done | bytes 262176 | tf_op jit(solution)/shard_map/ppermute | solution.py:326
  83.8 2.5 %collective-permute-start.30 = (f32[256,256]{1,0:T(8,128)S(1)}, f32[256,256]{1,0:T(8,128)S(1)}, u32[]{:S(2)}, u32[]{:S(2)}) collective-permute-start(f32[256,256]{1,0:T(8,128)S(1)} %get-tuple-element.195), channel_id=1, source_target_pairs={{0,16},{1,17},{2,18},{3,19},{4,20},{5,21},{6,22},{7,23},{8,24},{9,... | collective-permute-start | bytes 786440 | tf_op jit(solution)/shard_map/ppermute | solution.py:326
  87.2 3.5 %collective-permute-done.27 = f32[128,256]{1,0:T(8,128)S(1)} collective-permute-done((f32[128,256]{1,0:T(8,128)S(1)}, f32[128,256]{1,0:T(8,128)S(1)}, u32[]{:S(2)}, u32[]{:S(2)}) %collective-permute-start.27) | collective-permute-done | bytes 131104 | tf_op jit(solution)/shard_map/ppermute | solution.py:326
  92.1 6.5 %collective-permute-done.28 = f32[128,256]{1,0:T(8,128)S(1)} collective-permute-done((f32[128,256]{1,0:T(8,128)S(1)}, f32[128,256]{1,0:T(8,128)S(1)}, u32[]{:S(2)}, u32[]{:S(2)}) %collective-permute-start.28) | collective-permute-done | bytes 131104 | tf_op jit(solution)/shard_map/ppermute | solution.py:326
  100.0 3.4 %collective-permute-start.34 = (f32[128,256]{1,0:T(8,128)S(1)}, f32[128,256]{1,0:T(8,128)S(1)}, u32[]{:S(2)}, u32[]{:S(2)}) collective-permute-start(f32[128,256]{1,0:T(8,128)S(1)} %add.51), channel_id=1, source_target_pairs={{0,8},{1,9},{8,0},{9,1}} | collective-permute-start | bytes 393224 | tf_op jit(solution)/shard_map/ppermute | solution.py:326
  106.0 3.2 %collective-permute-done.34 = f32[128,256]{1,0:T(8,128)S(1)} collective-permute-done((f32[128,256]{1,0:T(8,128)S(1)}, f32[128,256]{1,0:T(8,128)S(1)}, u32[]{:S(2)}, u32[]{:S(2)}) %collective-permute-start.34) | collective-permute-done | bytes 131104 | tf_op jit(solution)/shard_map/ppermute | solution.py:326
  109.2 3.6 %collective-permute-done.35 = f32[128,256]{1,0:T(8,128)S(1)} collective-permute-done((f32[128,256]{1,0:T(8,128)S(1)}, f32[128,256]{1,0:T(8,128)S(1)}, u32[]{:S(2)}, u32[]{:S(2)}) %collective-permute-start.35) | collective-permute-done | bytes 131104 | tf_op jit(solution)/shard_map/ppermute | solution.py:326
  116.3 4.3 %end.1.refs_0_ = f32[256,256]{1,0:T(8,128)S(1)} custom-call(s32[3]{0:T(128)S(1)} %pad_add_fusion.ids, f32[256,256]{1,0:T(8,128)S(1)} %get-tuple-element.210.total, f32[256,256]{1,0:T(8,128)S(1)} %get-tuple-element.211.solved, f32[256,256]{1,0:T(8,128)S(1)} %collective-permute-done.37.second, f32[256,256]{1,0:T(8,128)S(1)} %broadcast_select_fusion.1.refs_4_.c0, ...), custom_call_target="tpu_custom_call" | custom-call | flops 1 | bytes 1 | tf_op jit(solution)/shard_map/end/pallas_call | solution.py:43
  122.2 8.2 %collective-permute-done.42.refs_2_ = f32[256,256]{1,0:T(8,128)S(1)} collective-permute-done((f32[256,256]{1,0:T(8,128)S(1)}, f32[256,256]{1,0:T(8,128)S(1)}, u32[]{:S(2)}, u32[]{:S(2)}) %collective-permute-start.42) | collective-permute-done | bytes 262176 | tf_op jit(solution)/shard_map/ppermute | solution.py:326
  130.4 5.4 %collective-permute-done.43.refs_1_ = f32[256,256]{1,0:T(8,128)S(1)} collective-permute-done((f32[256,256]{1,0:T(8,128)S(1)}, f32[256,256]{1,0:T(8,128)S(1)}, u32[]{:S(2)}, u32[]{:S(2)}) %collective-permute-start.43) | collective-permute-done | bytes 262176 | tf_op jit(solution)/shard_map/ppermute | solution.py:326
  135.8 4.8 %collective-permute-done.44.refs_3_ = f32[256,256]{1,0:T(8,128)S(1)} collective-permute-done((f32[256,256]{1,0:T(8,128)S(1)}, f32[256,256]{1,0:T(8,128)S(1)}, u32[]{:S(2)}, u32[]{:S(2)}) %collective-permute-start.44) | collective-permute-done | bytes 262176 | tf_op jit(solution)/shard_map/ppermute | solution.py:326
  (122 shorter events, 46.5 us)
Async XLA Ops:
  2.1 11.6 %collective-permute-start = (f32[256,256]{1,0:T(8,128)S(1)}, f32[256,256]{1,0:T(8,128)}, u32[]{:S(2)}, u32[]{:S(2)}) collective-permute-start(f32[256,256]{1,0:T(8,128)S(1)} %get-tuple-element.139), channel_id=1, source_target_pairs={{0,2},{1,3},{8,10},{9,11},{16,18},{17,19},{24,26},{25,27}} | collective-permute-start | bytes 786440 | tf_op jit(solution)/shard_map/ppermute | solution.py:326
  7.8 13.4 %collective-permute-start.3 = (f32[256,256]{1,0:T(8,128)S(1)}, f32[256,256]{1,0:T(8,128)}, u32[]{:S(2)}, u32[]{:S(2)}) collective-permute-start(f32[256,256]{1,0:T(8,128)S(1)} %get-tuple-element.135), channel_id=1, source_target_pairs={{0,2},{1,3},{8,10},{9,11},{16,18},{17,19},{24,26},{25,27}} | collective-permute-start | bytes 786440 | tf_op jit(solution)/shard_map/ppermute | solution.py:326
  9.8 15.3 %collective-permute-start.6 = (f32[256,256]{1,0:T(8,128)}, f32[256,256]{1,0:T(8,128)}, u32[]{:S(2)}, u32[]{:S(2)}) collective-permute-start(f32[256,256]{1,0:T(8,128)} %get-tuple-element.131), channel_id=1, source_target_pairs={{0,2},{1,3},{8,10},{9,11},{16,18},{17,19},{24,26},{25,27}} | collective-permute-start | bytes 786440 | tf_op jit(solution)/shard_map/ppermute | solution.py:326
  13.8 12.7 %collective-permute-start.1 = (f32[256,256]{1,0:T(8,128)}, f32[256,256]{1,0:T(8,128)}, u32[]{:S(2)}, u32[]{:S(2)}) collective-permute-start(f32[256,256]{1,0:T(8,128)} %collective-permute-done), channel_id=1, source_target_pairs={{2,4},{3,5},{10,12},{11,13},{18,20},{19,21},{26,28},{27,29}} | collective-permute-start | bytes 786440 | tf_op jit(solution)/shard_map/ppermute | solution.py:326
  19.8 11.5 %collective-permute-start.11 = (f32[256,256]{1,0:T(8,128)S(1)}, f32[256,256]{1,0:T(8,128)S(1)}, u32[]{:S(2)}, u32[]{:S(2)}) collective-permute-start(f32[256,256]{1,0:T(8,128)S(1)} %select_select_fusion.5.refs_0_), channel_id=1, source_target_pairs={{0,2},{1,3},{8,10},{9,11},{16,18},{17,19},{24,26},{25,27}} | collective-permute-start | bytes 786440 | tf_op jit(solution)/shard_map/ppermute | solution.py:326
  21.2 10.9 %collective-permute-start.9 = (f32[256,256]{1,0:T(8,128)}, f32[256,256]{1,0:T(8,128)}, u32[]{:S(2)}, u32[]{:S(2)}) collective-permute-start(f32[256,256]{1,0:T(8,128)} %collective-permute-done.3), channel_id=1, source_target_pairs={{2,4},{3,5},{10,12},{11,13},{18,20},{19,21},{26,28},{27,29}} | collective-permute-start | bytes 786440 | tf_op jit(solution)/shard_map/ppermute | solution.py:326
  27.9 13.6 %collective-permute-start.5 = (f32[512,256]{1,0:T(8,128)S(1)}, f32[512,256]{1,0:T(8,128)}, u32[]{:S(2)}, u32[]{:S(2)}) collective-permute-start(f32[512,256]{1,0:T(8,128)S(1)} %pad_maximum_fusion.blocks), channel_id=1, source_target_pairs={{0,8},{1,9},{8,0},{9,1}} | collective-permute-start | bytes 1572872 | tf_op jit(solution)/shard_map/ppermute | solution.py:326
  46.0 14.0 %collective-permute-start.15 = (f32[256,256]{1,0:T(8,128)S(1)}, f32[256,256]{1,0:T(8,128)S(1)}, u32[]{:S(2)}, u32[]{:S(2)}) collective-permute-start(f32[256,256]{1,0:T(8,128)S(1)} %get-tuple-element.150.v0), channel_id=1, source_target_pairs={{0,16},{1,17},{2,18},{3,19},{4,20},{5,21},{6,22},{7,23},{8,24},{9,... | collective-permute-start | bytes 786440 | tf_op jit(solution)/shard_map/ppermute | solution.py:326
  46.0 14.0 %collective-permute-start.16 = (f32[256,256]{1,0:T(8,128)S(1)}, f32[256,256]{1,0:T(8,128)S(1)}, u32[]{:S(2)}, u32[]{:S(2)}) collective-permute-start(f32[256,256]{1,0:T(8,128)S(1)} %get-tuple-element.150.v0), channel_id=1, source_target_pairs={{0,24},{1,25},{2,26},{3,27},{4,28},{5,29},{6,30},{7,31},{8,16},{9,... | collective-permute-start | bytes 786440 | tf_op jit(solution)/shard_map/ppermute | solution.py:326
  48.0 12.1 %collective-permute-start.18 = (f32[256,256]{1,0:T(8,128)S(1)}, f32[256,256]{1,0:T(8,128)S(1)}, u32[]{:S(2)}, u32[]{:S(2)}) collective-permute-start(f32[256,256]{1,0:T(8,128)S(1)} %copy-done.2), channel_id=1, source_target_pairs={{4,6},{5,7},{12,14},{13,15},{20,22},{21,23},{28,30},{29,31}} | collective-permute-start | bytes 786440 | tf_op jit(solution)/shard_map/ppermute | solution.py:326
  64.7 15.5 %collective-permute-start.22 = (f32[512,256]{1,0:T(8,128)S(1)}, f32[512,256]{1,0:T(8,128)S(1)}, u32[]{:S(2)}, u32[]{:S(2)}) collective-permute-start(f32[512,256]{1,0:T(8,128)S(1)} %get-tuple-element.174), channel_id=1, source_target_pairs={{0,2},{1,3},{2,0},{3,1},{4,6},{5,7},{6,4},{7,5},{8,10},{9,11},{10,... | collective-permute-start | bytes 1572872 | tf_op jit(solution)/shard_map/ppermute | solution.py:326
  65.4 12.8 %collective-permute-start.21 = (f32[256,256]{1,0:T(8,128)S(1)}, f32[256,256]{1,0:T(8,128)S(1)}, u32[]{:S(2)}, u32[]{:S(2)}) collective-permute-start(f32[256,256]{1,0:T(8,128)S(1)} %get-tuple-element.173), channel_id=1, source_target_pairs={{0,16},{1,17},{2,18},{3,19},{4,20},{5,21},{6,22},{7,23},{8,24},{9,... | collective-permute-start | bytes 786440 | tf_op jit(solution)/shard_map/ppermute | solution.py:326
  69.3 10.9 %collective-permute-start.24 = (f32[128,256]{1,0:T(8,128)S(1)}, f32[128,256]{1,0:T(8,128)S(1)}, u32[]{:S(2)}, u32[]{:S(2)}) collective-permute-start(f32[128,256]{1,0:T(8,128)S(1)} %get-tuple-element.181), channel_id=1, source_target_pairs={{0,16},{1,17},{2,18},{3,19},{4,20},{5,21},{6,22},{7,23},{8,24},{9,... | collective-permute-start | bytes 393224 | tf_op jit(solution)/shard_map/ppermute | solution.py:326
  69.4 10.9 %collective-permute-start.25 = (f32[128,256]{1,0:T(8,128)S(1)}, f32[128,256]{1,0:T(8,128)S(1)}, u32[]{:S(2)}, u32[]{:S(2)}) collective-permute-start(f32[128,256]{1,0:T(8,128)S(1)} %get-tuple-element.182), channel_id=1, source_target_pairs={{0,24},{1,25},{2,26},{3,27},{4,28},{5,29},{6,30},{7,31},{8,16},{9,... | collective-permute-start | bytes 393224 | tf_op jit(solution)/shard_map/ppermute | solution.py:326
  80.3 10.5 %collective-permute-start.27 = (f32[128,256]{1,0:T(8,128)S(1)}, f32[128,256]{1,0:T(8,128)S(1)}, u32[]{:S(2)}, u32[]{:S(2)}) collective-permute-start(f32[128,256]{1,0:T(8,128)S(1)} %add_add_fusion.1), channel_id=1, source_target_pairs={{2,0},{3,1},{6,4},{7,5},{10,8},{11,9},{14,12},{15,13},{18,16},{19,... | collective-permute-start | bytes 393224 | tf_op jit(solution)/shard_map/ppermute | solution.py:326
  81.6 17.0 %collective-permute-start.26 = (f32[256,256]{1,0:T(8,128)S(1)}, f32[256,256]{1,0:T(8,128)S(1)}, u32[]{:S(2)}, u32[]{:S(2)}) collective-permute-start(f32[256,256]{1,0:T(8,128)S(1)} %slice_add_fusion), channel_id=1, source_target_pairs={{0,4},{1,5},{2,6},{3,7},{4,0},{5,1},{6,2},{7,3},{8,12},{9,13},{10,... | collective-permute-start | bytes 786440 | tf_op jit(solution)/shard_map/ppermute | solution.py:326
  83.3 15.3 %collective-permute-start.29 = (f32[256,256]{1,0:T(8,128)S(1)}, f32[256,256]{1,0:T(8,128)S(1)}, u32[]{:S(2)}, u32[]{:S(2)}) collective-permute-start(f32[256,256]{1,0:T(8,128)S(1)} %get-tuple-element.194), channel_id=1, source_target_pairs={{0,8},{1,9},{2,10},{3,11},{4,12},{5,13},{6,14},{7,15},{8,0},{9,1},... | collective-permute-start | bytes 786440 | tf_op jit(solution)/shard_map/ppermute | solution.py:326
  83.8 14.8 %collective-permute-start.30 = (f32[256,256]{1,0:T(8,128)S(1)}, f32[256,256]{1,0:T(8,128)S(1)}, u32[]{:S(2)}, u32[]{:S(2)}) collective-permute-start(f32[256,256]{1,0:T(8,128)S(1)} %get-tuple-element.195), channel_id=1, source_target_pairs={{0,16},{1,17},{2,18},{3,19},{4,20},{5,21},{6,22},{7,23},{8,24},{9,... | collective-permute-start | bytes 786440 | tf_op jit(solution)/shard_map/ppermute | solution.py:326
  86.3 12.3 %collective-permute-start.31 = (f32[256,256]{1,0:T(8,128)S(1)}, f32[256,256]{1,0:T(8,128)S(1)}, u32[]{:S(2)}, u32[]{:S(2)}) collective-permute-start(f32[256,256]{1,0:T(8,128)S(1)} %get-tuple-element.196), channel_id=1, source_target_pairs={{0,24},{1,25},{2,26},{3,27},{4,28},{5,29},{6,30},{7,31},{8,16},{9,... | collective-permute-start | bytes 786440 | tf_op jit(solution)/shard_map/ppermute | solution.py:326
  98.7 14.1 %collective-permute-start.32 = (f32[256,256]{1,0:T(8,128)S(1)}, f32[256,256]{1,0:T(8,128)S(1)}, u32[]{:S(2)}, u32[]{:S(2)}) collective-permute-start(f32[256,256]{1,0:T(8,128)S(1)} %add_add_fusion), channel_id=1, source_target_pairs={{0,0},{1,1},{2,20},{3,21},{4,2},{5,3},{6,22},{7,23},{8,8},{9,9},{1... | collective-permute-start | bytes 786440 | tf_op jit(solution)/shard_map/ppermute | solution.py:326
  99.4 13.4 %collective-permute-start.33 = (f32[256,256]{1,0:T(8,128)S(1)}, f32[256,256]{1,0:T(8,128)S(1)}, u32[]{:S(2)}, u32[]{:S(2)}) collective-permute-start(f32[256,256]{1,0:T(8,128)S(1)} %broadcast_select_fusion.1.refs_4_.c0), channel_id=1, source_target_pairs={{0,8},{1,9},{2,10},{3,11},{4,12},{5,13},{6,14},{7,15},{8,0},{9,1},... | collective-permute-start | bytes 786440 | tf_op jit(solution)/shard_map/ppermute | solution.py:326
  121.1 14.8 %collective-permute-start.43 = (f32[256,256]{1,0:T(8,128)S(1)}, f32[256,256]{1,0:T(8,128)S(1)}, u32[]{:S(2)}, u32[]{:S(2)}) collective-permute-start(f32[256,256]{1,0:T(8,128)S(1)} %end.1.refs_0_), channel_id=1, source_target_pairs={{0,2},{1,3},{2,0},{3,1},{4,6},{5,7},{6,4},{7,5},{8,10},{9,11},{10,... | collective-permute-start | bytes 786440 | tf_op jit(solution)/shard_map/ppermute | solution.py:326
  130.4 10.3 %collective-permute-start.44 = (f32[256,256]{1,0:T(8,128)S(1)}, f32[256,256]{1,0:T(8,128)S(1)}, u32[]{:S(2)}, u32[]{:S(2)}) collective-permute-start(f32[256,256]{1,0:T(8,128)S(1)} %collective-permute-done.42.refs_2_), channel_id=1, source_target_pairs={{0,2},{1,3},{2,0},{3,1},{4,6},{5,7},{6,4},{7,5},{8,10},{9,11},{10,... | collective-permute-start | bytes 786440 | tf_op jit(solution)/shard_map/ppermute | solution.py:326
  130.4 10.3 %collective-permute-start.46 = (f32[256,256]{1,0:T(8,128)S(1)}, f32[256,256]{1,0:T(8,128)S(1)}, u32[]{:S(2)}, u32[]{:S(2)}) collective-permute-start(f32[256,256]{1,0:T(8,128)S(1)} %collective-permute-done.42.refs_2_), channel_id=1, source_target_pairs={{0,1},{1,0},{2,3},{3,2},{4,5},{5,4},{6,7},{7,6},{8,9},{9,8},{10,11... | collective-permute-start | bytes 786440 | tf_op jit(solution)/shard_map/ppermute | solution.py:326
  (35 other events, 241.6 us)
